TPU v7x, 32 devices: a whole 2x2x4 slice. The times are simulated.
32 devices in a mesh: dp: 2 (over core), mem: 16 (over z, y, x).
Axes of the slice: x: 2, y: 2, z: 4, core: 2. Of those that a mesh axis runs over, the one named last changes fastest.
Arguments:
- tokens: bfloat16 [4096, 1024], P(('dp', 'mem')), may hold values from -6 to 6
- attn_gain: float32 [1024], replicated, may hold values from 0.5 to 1.5
- qkv_weight: bfloat16 [1024, 3072], replicated, may hold values from -0.1875 to 0.1875
- out_weight: bfloat16 [1024, 1024], replicated, may hold values from -0.75 to 0.75
- bias_table: float32 [8, 32], replicated, may hold values from -4 to 4
- gate_logit: float32 [8], replicated, may hold values from -1.5 to 1.5
- ffn_gain: float32 [1024], replicated, may hold values from 0.5 to 1.5
- up_weight: bfloat16 [1024, 4096], replicated, may hold values from -0.1875 to 0.1875
- down_weight: bfloat16 [1024, 4096], replicated, may hold values from -0.09375 to 0.09375
- memory_keys: bfloat16 [65536, 1024], P('mem'), may hold values from -6 to 6
- memory_values: bfloat16 [65536, 1024], P('mem'), may hold values from -6 to 6
- book_lengths: int32 [2, 3], P('dp'), may hold values from 1 to 2046, as said below
- slot_shard: int32 [4096, 8, 32, 1], P(('dp', 'mem')), may hold values from 0 to 15; in each aligned block of 32768 rows (0 to 32767, 32768 to 65535, ..., all dimensions but the last counted through in order) at most 3072 rows name the same one
- slot_index: int32 [4096, 8, 32], P(('dp', 'mem')), may hold values from 0 to 4095
- slot_live: int32 [4096, 8, 32], P(('dp', 'mem')), may hold values from 0 to 1, as said below
- cotangent: bfloat16 [4096, 1024], P(('dp', 'mem')), may hold values from -6 to 6
Outputs:
- block_out: bfloat16 [4096, 1024], P(('dp', 'mem'))
- tokens_grad: float32 [4096, 1024], P(('dp', 'mem'))
- qkv_grad: float32 [1024, 3072], P('mem')
- out_grad: float32 [1024, 1024], P('mem')
- up_grad: float32 [1024, 4096], P('mem')
- down_grad: float32 [1024, 4096], P('mem')
- attn_gain_grad: float32 [1024], replicated
- ffn_gain_grad: float32 [1024], replicated
- bias_grad: float32 [8, 32], replicated
- gate_grad: float32 [8], replicated
Inputs may be any that keep to these rules, and one draw needn't show every extreme that they name: `book_lengths`: the 3 books of a group fill its 2048 tokens; the middle one begins in the first 128 tokens and ends in the last 128; in some group the first and last books are one token long. `slot_shard`: among the 32768 entries of one device's tokens no device of mem is named more than 3072 times, and some device is named exactly 3072 times. `slot_live`: some token heads have no live entry.
All inputs are finite; a program needn't handle non-finite values.
Results may differ from a plain program's by a relative error of at most 0.014.
Values may be sent and summed in bfloat16 or wider, within the bound.
A program may use at most 256 MiB of HBM per device.

v0:
```python
import math

import jax
import jax.numpy as jnp
from jax import lax
from jax.experimental import pallas as pl
from jax.experimental.pallas import tpu as pltpu
from jax.sharding import PartitionSpec as P

W = 512
VMEM_LIMIT = 56 * 1024 * 1024


eps_norm = 1e-06
bucket_edges = tuple((math.ceil(16 * 8 ** (edge_step / 16)) for edge_step in range(1, 16)))
masked_score = -1e30
dead_score = -10000.0
contract_rows = (((0,), (0,)), ((), ()))
contract_cols = (((1,), (1,)), ((), ()))


def passed_along(value, axis, by):
    size = lax.axis_size(axis)
    pairs = [(i, i + by) for i in range(size) if 0 <= i + by < size]
    return lax.ppermute(value, axis, pairs)


def bucket_of(offset):
    past_edges = sum(((offset >= edge_pos).astype(jnp.int32) for edge_pos in bucket_edges))
    return jnp.where(offset < 16, offset, 16 + past_edges)


def normed(values, gain_vec):
    return (
        values * lax.rsqrt(jnp.mean(values * values, axis=-1, keepdims=True) + eps_norm) * gain_vec
    )


def book_of(positions, lengths):
    book_ends = jnp.cumsum(lengths, dtype=jnp.int32)
    return jnp.sum((positions[..., None] >= book_ends).astype(jnp.int32), axis=-1)


def place_requests(slot_shard, slot_index, slot_live, owners, capacity, slots):
    rows, heads, top_count = slot_index.shape
    entries, empty = rows * heads * top_count, heads * rows * slots
    if (owners + 1) * empty >= 2**31:
        raise ValueError("codes exceed int32")
    row_of = (
        jnp.arange(heads, dtype=jnp.int32)[None, :] * rows
        + jnp.arange(rows, dtype=jnp.int32)[:, None]
    )
    owner = jnp.where(slot_live > 0, slot_shard[..., 0], owners)
    codes = owner * empty + row_of[:, :, None] * slots + slot_index
    codes = lax.sort(codes.reshape(-1), is_stable=False)
    ends = jnp.sum(
        (codes[None, :] < (jnp.arange(owners, dtype=jnp.int32) + 1)[:, None] * empty).astype(jnp.int32),
        axis=1,
    )
    starts = jnp.concatenate([jnp.zeros((1,), jnp.int32), ends[:-1]])
    tall = -(-entries // 128)
    codes = jnp.pad(codes, (0, tall * 128 - entries)).reshape(tall, 128)
    long = capacity // 128

    def kernel(starts_ref, ends_ref, codes_ref, lists_ref, padded):
        padded[:tall, :] = codes_ref[...]
        padded[tall:, :] = jnp.zeros((long + 8, 128), jnp.int32)
        lane = lax.broadcasted_iota(jnp.int32, (long, 128), 1)
        place = lax.broadcasted_iota(jnp.int32, (long, 128), 0) * 128 + lane

        @pl.loop(0, owners)
        def _(i):
            start, end = starts_ref[i], ends_ref[i]
            shift = start % 128
            lines = padded[pl.ds(start // 128, long + 1), :]
            turned = pltpu.roll(lines, (128 - shift) % 128, 1)
            joined = jnp.where(lane < 128 - shift, turned[:long], turned[1:])
            lists_ref[i] = jnp.where(place < end - start, joined - i * empty, empty)

    return pl.pallas_call(
        kernel,
        in_specs=[pl.BlockSpec(memory_space=pltpu.SMEM)] * 2 + [pl.BlockSpec(memory_space=pltpu.VMEM)],
        out_shape=jax.ShapeDtypeStruct((owners, long, 128), jnp.int32),
        scratch_shapes=[pltpu.VMEM((tall + long + 8, 128), jnp.int32)],
        cost_estimate=lasting(3),
        name="make_lists",
    )(starts, ends, codes)


def read_lists(incoming, heads, rows, slots):
    sources, long, _ = incoming.shape

    def kernel(lists_ref, index_ref, ids_ref, bounds_ref):
        lane = lax.broadcasted_iota(jnp.int32, (1, 128), 1)

        def read(source):
            codes = lists_ref[source]
            ids = lax.div(codes, slots)
            index = lax.div(ids, rows) * slots + lax.rem(codes, slots)
            index_ref[source] = jnp.where(ids < heads * rows, index, 0)
            ids_ref[source, :long, :] = ids
            ids_ref[source, long:, :] = jnp.full((1, 128), heads * rows, jnp.int32)
            bounds = jnp.zeros((1, 128), jnp.int32)
            for head in range(1, heads + 1):
                below = jnp.sum(
                    jnp.where(codes < head * rows * slots, 1.0, 0.0), axis=0, keepdims=True
                )
                below = jnp.sum(below, axis=1, keepdims=True).astype(jnp.int32)
                bounds = jnp.where(lane == head, below, bounds)
            bounds_ref[pl.ds(source, 1), :] = bounds

        if sources > 16:
            pl.loop(0, sources)(read)
        else:
            for source in range(sources):
                read(source)

    return pl.pallas_call(
        kernel,
        out_shape=[
            jax.ShapeDtypeStruct((sources, long, 128), jnp.int32),
            jax.ShapeDtypeStruct((sources, long + 1, 128), jnp.int32),
            jax.ShapeDtypeStruct((sources, 128), jnp.int32),
        ],
        cost_estimate=lasting(3),
        name="read_lists",
    )(incoming)


def gather_rows(index, bounds, memory_keys, memory_values, heads, sources, capacity):
    slots, width = memory_keys.shape
    head_dim = width // heads
    step, part = 128, 16

    def kernel(index_ref, bounds_ref, keys, values, out_keys, out_values, key_table, value_table, key_rows, value_rows):
        i = pl.program_id(0)

        @pl.when(i < heads)
        def _():
            place = pl.ds(pl.multiple_of(i * slots, slots), slots)
            key_table[place, :] = keys[...].astype(jnp.float32)
            value_table[place, :] = values[...].astype(jnp.float32)

        @pl.when(i >= heads)
        def _():
            source = i - heads

            used = (bounds_ref[source * 128 + heads] + step - 1) // step

            def store(group):
                for at in range(0, step, part):
                    here = pl.ds(pl.multiple_of(group * step, step) + at, part)
                    out_keys[here, :] = key_rows[at : at + part, :].astype(jnp.bfloat16)
                    out_values[here, :] = value_rows[at : at + part, :].astype(jnp.bfloat16)

            @pl.loop(0, used)
            def _(group):
                store(jnp.maximum(group - 1, 0))
                first = source * capacity + group * step
                for u in range(step):
                    row = index_ref[first + u]
                    key_rows[u : u + 1, :] = key_table[pl.ds(row, 1), :]
                    value_rows[u : u + 1, :] = value_table[pl.ds(row, 1), :]

            pl.when(used > 0)(lambda: store(used - 1))

            @pl.loop(used, capacity // step)
            def _(group):
                here = pl.ds(pl.multiple_of(group * step, step), step)
                out_keys[here, :] = jnp.zeros((step, head_dim), jnp.bfloat16)
                out_values[here, :] = jnp.zeros((step, head_dim), jnp.bfloat16)

    table_spec = pl.BlockSpec((slots, head_dim), lambda i, *_: (0, jnp.minimum(i, heads - 1)))
    out_spec = pl.BlockSpec((capacity, head_dim), lambda i, *_: (jnp.maximum(i - heads, 0), 0))
    out_shape = jax.ShapeDtypeStruct((sources * capacity, head_dim), jnp.bfloat16)
    return pl.pallas_call(
        kernel,
        grid_spec=pltpu.PrefetchScalarGridSpec(
            num_scalar_prefetch=2,
            grid=(heads + sources,),
            in_specs=[table_spec, table_spec],
            out_specs=[out_spec, out_spec],
            scratch_shapes=[
                pltpu.VMEM((heads * slots, head_dim), jnp.float32),
                pltpu.VMEM((heads * slots, head_dim), jnp.float32),
                pltpu.VMEM((step, head_dim), jnp.float32),
                pltpu.VMEM((step, head_dim), jnp.float32),
            ],
        ),
        out_shape=[out_shape, out_shape],
        compiler_params=pltpu.CompilerParams(vmem_limit_bytes=VMEM_LIMIT),
        cost_estimate=lasting(42),
        name="gather_rows",
    )(index, bounds, memory_keys, memory_values)


def lasting(microseconds):
    return pl.CostEstimate(flops=0, bytes_accessed=3_000_000 * microseconds, transcendentals=0)


def triple(stat):
    part = lax.broadcasted_iota(jnp.int32, stat.shape, 1) // 16
    high = stat.astype(jnp.bfloat16).astype(jnp.float32)
    rest = stat - high
    middle = rest.astype(jnp.bfloat16).astype(jnp.float32)
    low = rest - middle
    chosen = jnp.where(part == 0, high, jnp.where(part == 1, middle, jnp.where(part == 2, low, 0.0)))
    return chosen.astype(jnp.bfloat16)


def window_of(bounds, source, head, heads, span, capacity):
    first, last = bounds[source * 128 + head], bounds[source * 128 + head + 1]
    start = jnp.minimum(first // 16 * 16, capacity - span)
    extra = jnp.maximum(last - start - 1, 0) // span
    return start, extra


def columns_of(head, head_dim):
    if isinstance(head, int):
        return slice(head * head_dim, (head + 1) * head_dim)
    return pl.ds(pl.multiple_of(head * head_dim, head_dim), head_dim)


def window_ids(id_ref, start, span):
    lines = id_ref[0, pl.ds(start // 128, span // 128 + 1), :]
    shift = start % 128
    turned = pltpu.roll(lines, (128 - shift) % 128, 1)
    lane = lax.broadcasted_iota(jnp.int32, (span // 128, 128), 1)
    return jnp.where(lane < 128 - shift, turned[:-1], turned[1:])


def owned(lines, first_row, count, start, least):
    row = lax.broadcasted_iota(jnp.int32, (count, 128), 0) + first_row
    masks = []
    for i in range(lines.shape[0]):
        mask = lines[i : i + 1, :] == row
        if least is not None:
            place = lax.broadcasted_iota(jnp.int32, (1, 128), 1) + start + i * 128
            mask = mask & (place >= least)
        masks.append(mask)
    return jnp.concatenate(masks, axis=1)


def memory_forward(bounds, queries, key_rows, value_rows, row_ids, heads, sources, rows, score_scale):
    capacity, head_dim = key_rows.shape[0] // sources, key_rows.shape[1]
    width = heads * head_dim
    span = min(384, capacity)
    chunk = math.gcd(rows, 32)

    def kernel(bounds_ref, q_ref, k_ref, v_ref, id_ref, out_ref, sums, tops, totals, raw, weights):
        source = pl.program_id(0)
        lane = lax.broadcasted_iota(jnp.int32, (chunk, 128), 1) % 16

        def window(heads_here, starts, least):
            here = [pl.ds(pl.multiple_of(start, 16), span) for start in starts]
            columns = [columns_of(head, head_dim) for head in heads_here]
            for slot in range(len(starts)):
                raw[slot] = lax.dot_general(
                    q_ref[:, columns[slot]],
                    k_ref[here[slot], :],
                    contract_cols,
                    preferred_element_type=jnp.float32,
                )
            for slot, (head, start) in enumerate(zip(heads_here, starts)):
                lines = window_ids(id_ref, start, span)
                for at in range(0, rows, chunk):
                    some = slice(at, at + chunk)
                    mine = owned(lines, head * rows + at, chunk, start, least)
                    scores = jnp.where(mine, raw[slot, some, :], masked_score)
                    top = jnp.maximum(jnp.max(scores, axis=1, keepdims=True), 0.1 * masked_score)
                    if least is not None:
                        old_top = jnp.max(
                            jnp.where(lane == head, tops[some, :], masked_score), axis=1, keepdims=True
                        )
                        top = jnp.maximum(top, old_top)
                    exps = jnp.exp((scores - top) * score_scale)
                    weights[slot, some, :] = exps.astype(jnp.bfloat16)
                    total = jnp.sum(exps, axis=1, keepdims=True)
                    if least is not None:
                        faded = jnp.exp((old_top - top) * score_scale)
                        sums[some, columns[slot]] = sums[some, columns[slot]] * faded
                        total = total + totals[some, :] * faded
                    tops[some, :] = jnp.where(lane == head, top, tops[some, :])
                    totals[some, :] = jnp.where(lane == heads + head, total, totals[some, :])
            for slot in range(len(starts)):
                found = jnp.dot(
                    weights[slot], v_ref[here[slot], :], preferred_element_type=jnp.float32
                )
                sums[:, columns[slot]] = found if least is None else sums[:, columns[slot]] + found

        tops[...] = jnp.zeros_like(tops)
        totals[...] = jnp.zeros_like(totals)

        windows = [window_of(bounds_ref, source, head, heads, span, capacity) for head in range(heads)]
        window(list(range(heads)), [start for start, _ in windows], None)

        @pl.when(sum(extra for _, extra in windows) > 0)
        def _():
            @pl.loop(0, heads)
            def _(head):
                start, extra = window_of(bounds_ref, source, head, heads, span, capacity)

                @pl.loop(0, extra)
                def _(turn):
                    least = start + (turn + 1) * span
                    window([head], [jnp.minimum(least, capacity - span)], least)

        out_ref[:, :width] = sums[...].astype(jnp.bfloat16)
        wide = lax.broadcasted_iota(jnp.int32, (rows, 128), 1) % 16
        out_ref[:, width:] = triple(jnp.where(wide < heads, tops[...] * score_scale, totals[...]))

    return pl.pallas_call(
        kernel,
        grid_spec=pltpu.PrefetchScalarGridSpec(
            num_scalar_prefetch=1,
            grid=(sources,),
            in_specs=[
                pl.BlockSpec((rows, width), lambda i, *_: (i, 0)),
                pl.BlockSpec((capacity, head_dim), lambda i, *_: (i, 0)),
                pl.BlockSpec((capacity, head_dim), lambda i, *_: (i, 0)),
                pl.BlockSpec((1, *row_ids.shape[1:]), lambda i, *_: (i, 0, 0)),
            ],
            out_specs=pl.BlockSpec((rows, width + 128), lambda i, *_: (i, 0)),
            scratch_shapes=[
                pltpu.VMEM((rows, width), jnp.float32),
                pltpu.VMEM((rows, 128), jnp.float32),
                pltpu.VMEM((rows, 128), jnp.float32),
                pltpu.VMEM((heads, rows, span), jnp.float32),
                pltpu.VMEM((heads, rows, span), jnp.bfloat16),
            ],
        ),
        out_shape=jax.ShapeDtypeStruct((sources * rows, width + 128), jnp.bfloat16),
        compiler_params=pltpu.CompilerParams(vmem_limit_bytes=VMEM_LIMIT),
        cost_estimate=lasting(25),
        name="memory_forward",
    )(bounds, queries, key_rows, value_rows, row_ids)


def combine_partials(partial, heads, sources, rows):
    width = partial.shape[1] - 128
    head_dim = width // heads

    def kernel(part_ref, out_ref, log_ref, sums, tops, totals):
        i = pl.program_id(0)

        @pl.when(i == 0)
        def _():
            sums[...] = jnp.zeros_like(sums)
            tops[...] = jnp.full_like(tops, masked_score)
            totals[...] = jnp.zeros_like(totals)

        stat = part_ref[:, width:].astype(jnp.float32)
        stat = stat + pltpu.roll(stat, 128 - 16, 1) + pltpu.roll(stat, 128 - 32, 1)
        new_total = pltpu.roll(stat, 128 - heads, 1)
        top = jnp.maximum(tops[...], stat)
        old_fade, new_fade = jnp.exp(tops[...] - top), jnp.exp(stat - top)
        tops[...] = top
        totals[...] = totals[...] * old_fade + new_total * new_fade
        for head in range(heads):
            columns = slice(head * head_dim, (head + 1) * head_dim)
            sums[:, columns] = (
                sums[:, columns] * old_fade[:, head : head + 1]
                + part_ref[:, columns].astype(jnp.float32) * new_fade[:, head : head + 1]
            )

        @pl.when(i == sources - 1)
        def _():
            live = totals[...] > 0
            total = jnp.where(live, totals[...], 1.0)
            log_ref[...] = jnp.where(live, tops[...] + jnp.log(total), 0.0)
            for head in range(heads):
                columns = slice(head * head_dim, (head + 1) * head_dim)
                out_ref[:, columns] = sums[:, columns] / total[:, head : head + 1]

    return pl.pallas_call(
        kernel,
        grid=(sources,),
        in_specs=[pl.BlockSpec((rows, width + 128), lambda i: (i, 0))],
        out_specs=[
            pl.BlockSpec((rows, width), lambda i: (0, 0)),
            pl.BlockSpec((rows, 128), lambda i: (0, 0)),
        ],
        scratch_shapes=[
            pltpu.VMEM((rows, width), jnp.float32),
            pltpu.VMEM((rows, 128), jnp.float32),
            pltpu.VMEM((rows, 128), jnp.float32),
        ],
        out_shape=[
            jax.ShapeDtypeStruct((rows, width), jnp.float32),
            jax.ShapeDtypeStruct((rows, 128), jnp.float32),
        ],
        compiler_params=pltpu.CompilerParams(vmem_limit_bytes=VMEM_LIMIT),
        cost_estimate=lasting(13),
        name="combine_partials",
    )(partial)


def memory_backward(bounds, queries, grads, key_rows, value_rows, row_ids, heads, sources, rows, score_scale):
    capacity, head_dim = key_rows.shape[0] // sources, key_rows.shape[1]
    width = heads * head_dim
    span = min(384, capacity)
    chunk = math.gcd(rows, 32)

    def kernel(bounds_ref, q_ref, g_ref, k_ref, v_ref, id_ref, out_ref, sums, stats, raw, products, slopes):
        source = pl.program_id(0)
        stats[...] = joined_tile(g_ref[:, width : width + 128])

        def window(heads_here, starts, least):
            here = [pl.ds(pl.multiple_of(start, 16), span) for start in starts]
            columns = [columns_of(head, head_dim) for head in heads_here]
            for slot in range(len(starts)):
                raw[slot] = lax.dot_general(
                    q_ref[:, columns[slot]],
                    k_ref[here[slot], :],
                    contract_cols,
                    preferred_element_type=jnp.float32,
                )
                products[slot] = lax.dot_general(
                    g_ref[:, columns[slot]],
                    v_ref[here[slot], :],
                    contract_cols,
                    preferred_element_type=jnp.float32,
                )
            for slot, (head, start) in enumerate(zip(heads_here, starts)):
                lines = window_ids(id_ref, start, span)
                turned = stats[...]
                if least is not None:
                    turned = pltpu.roll(turned, 128 - head, 1)
                elif head:
                    turned = turned[:, head:]
                for at in range(0, rows, chunk):
                    some = slice(at, at + chunk)
                    mine = owned(lines, head * rows + at, chunk, start, least)
                    log, delta = turned[some, :1], turned[some, heads : heads + 1]
                    probs = jnp.exp(jnp.where(mine, raw[slot, some, :] * score_scale - log, dead_score))
                    slopes[slot, some, :] = (probs * (products[slot, some, :] - delta)).astype(
                        jnp.bfloat16
                    )
            for slot in range(len(starts)):
                found = jnp.dot(
                    slopes[slot], k_ref[here[slot], :], preferred_element_type=jnp.float32
                )
                sums[:, columns[slot]] = found if least is None else sums[:, columns[slot]] + found

        windows = [window_of(bounds_ref, source, head, heads, span, capacity) for head in range(heads)]
        window(list(range(heads)), [start for start, _ in windows], None)

        @pl.when(sum(extra for _, extra in windows) > 0)
        def _():
            @pl.loop(0, heads)
            def _(head):
                start, extra = window_of(bounds_ref, source, head, heads, span, capacity)

                @pl.loop(0, extra)
                def _(turn):
                    least = start + (turn + 1) * span
                    window([head], [jnp.minimum(least, capacity - span)], least)

        out_ref[...] = sums[...].astype(jnp.bfloat16)

    return pl.pallas_call(
        kernel,
        grid_spec=pltpu.PrefetchScalarGridSpec(
            num_scalar_prefetch=1,
            grid=(sources,),
            in_specs=[
                pl.BlockSpec((rows, width), lambda i, *_: (i, 0)),
                pl.BlockSpec((rows, width + 128), lambda i, *_: (i, 0)),
                pl.BlockSpec((capacity, head_dim), lambda i, *_: (i, 0)),
                pl.BlockSpec((capacity, head_dim), lambda i, *_: (i, 0)),
                pl.BlockSpec((1, *row_ids.shape[1:]), lambda i, *_: (i, 0, 0)),
            ],
            out_specs=pl.BlockSpec((rows, width), lambda i, *_: (i, 0)),
            scratch_shapes=[
                pltpu.VMEM((rows, width), jnp.float32),
                pltpu.VMEM((rows, 128), jnp.float32),
                pltpu.VMEM((heads, rows, span), jnp.float32),
                pltpu.VMEM((heads, rows, span), jnp.float32),
                pltpu.VMEM((heads, rows, span), jnp.bfloat16),
            ],
        ),
        out_shape=jax.ShapeDtypeStruct((sources * rows, width), jnp.bfloat16),
        compiler_params=pltpu.CompilerParams(vmem_limit_bytes=VMEM_LIMIT),
        cost_estimate=lasting(25),
        name="memory_backward",
    )(bounds, queries, grads, key_rows, value_rows, row_ids)


def remote(source, target, send_sem, recv_sem, device):
    return pltpu.make_async_remote_copy(
        src_ref=source,
        dst_ref=target,
        send_sem=send_sem,
        recv_sem=recv_sem,
        device_id={"mem": device},
        device_id_type=pl.DeviceIdType.MESH,
    )


def grid_place(depth):
    me = lax.axis_index("mem")
    layer, column = me // 4, me % 4
    beside_x = column + 1 - 2 * (column % 2)
    beside_y = column + 2 - 4 * (column // 2)
    across = 3 - column

    def index_of(step, place):
        return (layer + step + depth) % depth * 4 + place

    return me, column, beside_x, beside_y, across, index_of


def greet(devices):
    barrier = pltpu.get_barrier_semaphore()
    for device in devices:
        pl.semaphore_signal(
            barrier, inc=1, device_id={"mem": device}, device_id_type=pl.DeviceIdType.MESH
        )
    pl.semaphore_wait(barrier, len(devices))


def gather_group(block, sources, collective_id, beside):
    rows, width = block.shape
    depth, half = sources // 4, rows // 2
    slots = 2 * depth - 1
    arrays, specs, more_out, more_scratch, begin = beside
    ins, outs = len(arrays), len(more_out)

    def kernel(x_ref, *refs):
        in_refs, (out_ref, *more_refs) = refs[:ins], refs[ins : ins + 1 + outs]
        (own_sem, send, recv), scratch = refs[ins + 1 + outs : ins + 4 + outs], refs[ins + 4 + outs :]
        meanwhile = begin(in_refs, more_refs, scratch)
        me = lax.axis_index("mem")
        layer, column = me // 4, me % 4
        to_x = me + 1 - 2 * (column % 2)
        to_y = me + 2 - 4 * (column // 2)
        across = layer * 4 + 3 - column
        has_above, has_below = layer + 1 < depth, layer > 0
        barrier = pltpu.get_barrier_semaphore()

        def signal(device):
            pl.semaphore_signal(
                barrier, inc=1, device_id={"mem": device}, device_id_type=pl.DeviceIdType.MESH
            )

        signal(to_x)
        signal(to_y)
        pl.when(has_above)(lambda: signal(me + 4))
        pl.when(has_below)(lambda: signal(me - 4))
        pl.semaphore_wait(barrier, 2 + has_above.astype(jnp.int32) + has_below.astype(jnp.int32))

        def part_of(index, part):
            start = pl.multiple_of(index * rows + part * half, half)
            return out_ref.at[pl.ds(start, half), :]

        own = pltpu.make_async_copy(x_ref, out_ref.at[pl.ds(pl.multiple_of(me * rows, rows), rows), :], own_sem)
        own.start()
        sent = []

        def push(condition, source, target, kind, slot, to_slot, part, device):
            copy = remote(source, target, send.at[kind, slot, part], recv.at[kind, to_slot, part], device)
            if condition is None:
                copy.start()
            else:
                pl.when(condition)(copy.start)
            sent.append((condition, copy))

        def arrived(index, kind, slot, part):
            target = part_of(index, part)
            remote(target, target, send.at[kind, slot, part], recv.at[kind, slot, part], to_x).wait_recv()

        def up_slot(distance):
            return distance

        def down_slot(distance):
            return depth - 1 + distance

        for part in (0, 1):
            mine = x_ref.at[pl.ds(part * half, half), :]
            push(has_above, mine, part_of(me, part), 0, 0, down_slot(1), part, me + 4)
            push(has_below, mine, part_of(me, part), 1, 0, up_slot(1), part, me - 4)
            mine_y = x_ref.at[pl.ds((1 - part) * half, half), :]
            push(None, mine, part_of(me, part), 2, 0, 0, part, to_x)
            push(None, mine_y, part_of(me, 1 - part), 3, 0, 0, 1 - part, to_y)

        meanwhile()

        def pass_on(condition, step, slot):
            def go():
                arrived(to_x + step, 2, slot, 0)
                copy_a.start()
                arrived(to_y + step, 3, slot, 1)
                copy_b.start()

            source_a, source_b = part_of(to_x + step, 0), part_of(to_y + step, 1)
            copy_a = remote(source_a, source_a, send.at[4, slot, 0], recv.at[4, slot, 0], to_y)
            copy_b = remote(source_b, source_b, send.at[5, slot, 1], recv.at[5, slot, 1], to_x)
            sent.append((condition, copy_a))
            sent.append((condition, copy_b))
            if condition is None:
                go()
            else:
                pl.when(condition)(go)

        for distance in range(1, depth):
            from_above, from_below = layer + distance < depth, layer - distance >= 0

            def take(kind, back_kind, step, slot, next_slot, onward, onward_device):
                for part in (0, 1):
                    arrived(me + step, kind, slot, part)
                    here = part_of(me + step, part)
                    if next_slot is not None:
                        pl.when(onward)(
                            remote(
                                here, here, send.at[kind, slot, part], recv.at[kind, next_slot, part], onward_device
                            ).start
                        )
                    remote(here, here, send.at[2, slot, part], recv.at[2, slot, part], to_x).start()
                    remote(here, here, send.at[3, slot, part], recv.at[3, slot, part], to_y).start()

            last = distance == depth - 1
            pl.when(from_above)(
                lambda: take(
                    1, 0, 4 * distance, up_slot(distance), None if last else up_slot(distance + 1), has_below, me - 4
                )
            )
            pl.when(from_below)(
                lambda: take(
                    0, 1, -4 * distance, down_slot(distance), None if last else down_slot(distance + 1), has_above, me + 4
                )
            )
            for condition, step, slot, kind, onward in (
                (from_above, 4 * distance, up_slot(distance), 1, has_below),
                (from_below, -4 * distance, down_slot(distance), 0, has_above),
            ):
                for part in (0, 1):
                    here = part_of(me + step, part)
                    if not last:
                        sent.append((condition & onward, remote(here, here, send.at[kind, slot, part], own_sem, me)))
                    sent.append((condition, remote(here, here, send.at[2, slot, part], own_sem, to_x)))
                    sent.append((condition, remote(here, here, send.at[3, slot, part], own_sem, to_y)))
            if distance == 1:
                pass_on(None, 0, 0)
            else:
                pass_on(layer + distance - 1 < depth, 4 * (distance - 1), up_slot(distance - 1))
                pass_on(layer - distance + 1 >= 0, -4 * (distance - 1), down_slot(distance - 1))
        pass_on(layer + depth - 1 < depth, 4 * (depth - 1), up_slot(depth - 1))
        pass_on(layer - depth + 1 >= 0, -4 * (depth - 1), down_slot(depth - 1))

        def close(step, slot):
            arrived(to_x + step, 2, slot, 1)
            arrived(to_y + step, 3, slot, 0)
            arrived(across + step, 4, slot, 0)
            arrived(across + step, 5, slot, 1)

        close(0, 0)
        for distance in range(1, depth):
            pl.when(layer + distance < depth)(lambda: close(4 * distance, up_slot(distance)))
            pl.when(layer - distance >= 0)(lambda: close(-4 * distance, down_slot(distance)))
        for condition, copy in sent:
            if condition is None:
                copy.wait_send()
            else:
                pl.when(condition)(copy.wait_send)
        own.wait()

    return pl.pallas_call(
        kernel,
        in_specs=[pl.BlockSpec(memory_space=pl.ANY), *specs],
        out_specs=[pl.BlockSpec(memory_space=pl.ANY)] + [pl.BlockSpec(memory_space=pltpu.VMEM)] * outs,
        out_shape=[jax.ShapeDtypeStruct((sources * rows, width), block.dtype), *more_out],
        scratch_shapes=[
            pltpu.SemaphoreType.DMA,
            pltpu.SemaphoreType.DMA((6, slots, 2)),
            pltpu.SemaphoreType.DMA((6, slots, 2)),
            *more_scratch,
        ],
        compiler_params=pltpu.CompilerParams(
            collective_id=collective_id, has_side_effects=True, vmem_limit_bytes=VMEM_LIMIT
        ),
        cost_estimate=lasting(50),
        name="gather_group",
    )(block, *arrays)


def reduce_steps(parts_ref, sources, refs, sems, merge, pack, beside=None):
    half_a, half_b, from_x, from_y, from_z, out_x, out_y, out_z = refs
    send, recv_a, recv_b, recv_x, recv_y, recv_z = sems
    rows = parts_ref.shape[0] // sources
    depth, half = sources // 4, rows // 2
    me, column, beside_x, beside_y, across, index_of = grid_place(depth)
    to_x, to_y = index_of(0, beside_x), index_of(0, beside_y)
    order = [*range(1, depth), 0]
    queues = {"x": [], "y": [], "z": []}
    first_limit = 2 if beside is None else depth

    def piece(index, part):
        return parts_ref.at[pl.ds(pl.multiple_of(index * rows + part * half, half), half), :]

    def part_rows(part):
        return pl.ds(part * half, half)

    def push(link, source, target, kind, k, recv_sem, device, limit=2):
        queue = queues[link]
        while link != "z" and len(queue) >= limit:
            queue.pop(0).wait_send()
        copy = remote(source, target, send.at[kind, k], recv_sem, device)
        copy.start()
        queue.append(copy)

    def arrived(target, recv_sem):
        remote(target, target, send.at[0, 0], recv_sem, to_x).wait_recv()

    def plane_rest(k):
        push("x", piece(index_of(k, beside_x), 0), from_x.at[k, part_rows(0)], 2, k, recv_x.at[0, k], to_x)
        push("y", piece(index_of(k, beside_y), 1), from_y.at[k, part_rows(1)], 3, k, recv_y.at[1, k], to_y)

    def plane_merged(k):
        arrived(half_a.at[k], recv_a.at[k])
        pack(out_y.at[k], merge([piece(index_of(k, beside_y), 0), half_a.at[k]]))
        push("y", out_y.at[k], from_y.at[k, part_rows(0)], 4, k, recv_y.at[0, k], to_y)
        arrived(half_b.at[k], recv_b.at[k])
        pack(out_x.at[k], merge([piece(index_of(k, beside_x), 1), half_b.at[k]]))
        push("x", out_x.at[k], from_x.at[k, part_rows(1)], 5, k, recv_x.at[1, k], to_x)

    def column_step(k):
        for part in (0, 1):
            here = part_rows(part)
            arrived(from_x.at[k, here], recv_x.at[part, k])
            arrived(from_y.at[k, here], recv_y.at[part, k])
            if k:
                blocks = [piece(index_of(k, column), part), from_x.at[k, here], from_y.at[k, here]]
                pack(out_z.at[k, here], merge(blocks))
        if k:
            push("z", out_z.at[k], from_z.at[k], 6, k, recv_z.at[k], index_of(k, column))

    for k in order:
        far = index_of(k, across)
        push("x", piece(far, 0), half_a.at[k], 0, k, recv_a.at[k], to_x, first_limit)
        push("y", piece(far, 1), half_b.at[k], 1, k, recv_b.at[k], to_y, first_limit)
    if beside is not None:
        beside()
    for i, k in enumerate(order):
        plane_rest(k)
        plane_merged(k)
        if i:
            column_step(order[i - 1])
    column_step(order[-1])
    for k in range(1, depth):
        arrived(from_z.at[k], recv_z.at[k])
    final = []
    for part in (0, 1):
        here = part_rows(part)
        blocks = [piece(me, part), from_x.at[0, here], from_y.at[0, here]]
        final.append((here, blocks + [from_z.at[k, here] for k in range(1, depth)]))
    return final, [copy for queue in queues.values() for copy in queue]


def reduce_scratch(rows, width, dtype, sources):
    depth, half = sources // 4, rows // 2

    def slots(size):
        return pltpu.VMEM((depth, size, width), dtype)

    refs = [slots(half), slots(half), slots(rows), slots(rows), slots(rows)]
    refs += [slots(half), slots(half), slots(rows)]
    sems = [pltpu.SemaphoreType.DMA((7, depth))]
    sems += [pltpu.SemaphoreType.DMA((depth,))] * 2
    sems += [pltpu.SemaphoreType.DMA((2, depth))] * 2
    sems += [pltpu.SemaphoreType.DMA((depth,))]
    return refs, sems


def run_alone(name, beside):
    arrays, specs, out_shape, scratch, begin = beside
    ins, outs = len(arrays), len(out_shape)

    def kernel(*refs):
        begin(refs[:ins], refs[ins : ins + outs], refs[ins + outs :])()

    return pl.pallas_call(
        kernel,
        in_specs=specs,
        out_specs=[pl.BlockSpec(memory_space=pltpu.VMEM)] * outs,
        out_shape=out_shape,
        scratch_shapes=scratch,
        compiler_params=pltpu.CompilerParams(vmem_limit_bytes=VMEM_LIMIT),
        cost_estimate=lasting(8),
        name=name,
    )(*arrays)


def reduce_group(parts, sources, collective_id, merge, pack, finish, out_shape, beside):
    rows, width = parts.shape[0] // sources, parts.shape[1]
    depth = sources // 4
    arrays, specs, more_out, more_scratch, begin = beside
    ref_shapes, sem_shapes = reduce_scratch(rows, width, parts.dtype, sources)
    sizes = [len(arrays), len(out_shape), len(more_out), len(ref_shapes), len(sem_shapes), len(more_scratch)]

    def kernel(parts_ref, *refs):
        groups, at = [], 0
        for size in sizes:
            groups.append(refs[at : at + size])
            at += size
        ins, out_refs, more_refs, steps_refs, steps_sems, scratch = groups
        meanwhile = begin(ins, more_refs, scratch)
        me, column, beside_x, beside_y, across, index_of = grid_place(depth)
        greet(
            [index_of(0, beside_x), index_of(0, beside_y)]
            + [index_of(-k, column) for k in range(1, depth)]
        )
        final, still_open = reduce_steps(
            parts_ref, sources, steps_refs, steps_sems, merge, pack, meanwhile
        )
        for here, blocks in final:
            finish([out.at[here] for out in out_refs], merge(blocks))
        for copy in still_open:
            copy.wait_send()

    vmem = pl.BlockSpec(memory_space=pltpu.VMEM)
    return pl.pallas_call(
        kernel,
        in_specs=[vmem, *specs],
        out_specs=[vmem] * (len(out_shape) + len(more_out)),
        out_shape=[*out_shape, *more_out],
        scratch_shapes=[*ref_shapes, *sem_shapes, *more_scratch],
        compiler_params=pltpu.CompilerParams(
            collective_id=collective_id, has_side_effects=True, vmem_limit_bytes=VMEM_LIMIT
        ),
        cost_estimate=lasting(50),
        name="reduce_group",
    )(parts, *arrays)


def sum_blocks(parts, sources, collective_id, beside):
    rows, width = parts.shape[0] // sources, parts.shape[1]

    def merge(blocks):
        total = blocks[0][...].astype(jnp.float32)
        for block in blocks[1:]:
            total = total + block[...].astype(jnp.float32)
        return total

    def pack(target, total):
        target[...] = total.astype(parts.dtype)

    def finish(targets, total):
        targets[0][...] = total

    out_shape = [jax.ShapeDtypeStruct((rows, width), jnp.float32)]
    return reduce_group(parts, sources, collective_id, merge, pack, finish, out_shape, beside)


def merge_partials(parts, sources, collective_id, heads, beside):
    rows, width = parts.shape[0] // sources, parts.shape[1] - 128
    head_dim = width // heads

    def merge(blocks):
        stats = []
        for block in blocks:
            stat = block[:, width:].astype(jnp.float32)
            stats.append(stat + pltpu.roll(stat, 128 - 16, 1) + pltpu.roll(stat, 128 - 32, 1))
        top = stats[0]
        for stat in stats[1:]:
            top = jnp.maximum(top, stat)
        fades = [jnp.exp(stat - top) for stat in stats]
        total = sum(fade * pltpu.roll(stat, 128 - heads, 1) for fade, stat in zip(fades, stats))
        sums = []
        for head in range(heads):
            columns = slice(head * head_dim, (head + 1) * head_dim)
            sums.append(
                sum(
                    block[:, columns].astype(jnp.float32) * fade[:, head : head + 1]
                    for block, fade in zip(blocks, fades)
                )
            )
        return sums, top, total

    def pack(target, merged):
        sums, top, total = merged
        for head in range(heads):
            target[:, head * head_dim : (head + 1) * head_dim] = sums[head].astype(parts.dtype)
        lane = lax.broadcasted_iota(jnp.int32, top.shape, 1)
        stat = jnp.where(lane < heads, top, jnp.where(lane < 16, pltpu.roll(total, heads, 1), 0.0))
        target[:, width:] = triple(stat + pltpu.roll(stat, 16, 1) + pltpu.roll(stat, 32, 1))

    def finish(targets, merged):
        sums, top, total = merged
        live = total > 0
        total = jnp.where(live, total, 1.0)
        targets[1][...] = jnp.where(live, top + jnp.log(total), 0.0)
        for head in range(heads):
            targets[0][:, head * head_dim : (head + 1) * head_dim] = sums[head] / total[:, head : head + 1]

    out_shape = [
        jax.ShapeDtypeStruct((rows, width), jnp.float32),
        jax.ShapeDtypeStruct((rows, 128), jnp.float32),
    ]
    return reduce_group(parts, sources, collective_id, merge, pack, finish, out_shape, beside)


def scattered(halves):
    return lax.psum_scatter(halves, "mem", scatter_dimension=0, tiled=True)


def whole_grads(both, widths):
    both = both.astype(jnp.float32)
    grads, at = [], 0
    for size in widths:
        half = size // 2
        grads.append(jnp.concatenate([both[0, :, at : at + half], both[1, :, at : at + half]], 1))
        at += half
    return grads


def lane_tile(columns, rows):
    lane = lax.broadcasted_iota(jnp.int32, (rows, 128), 1)
    tile = jnp.zeros((rows, 128), jnp.float32)
    for i, column in enumerate(columns):
        tile = jnp.where(lane == i, column, tile)
    return tile


def split_tile(tile):
    lane = lax.broadcasted_iota(jnp.int32, tile.shape, 1)
    kept = jnp.where(lane < 32, tile, 0.0)
    kept = kept + pltpu.roll(kept, 32, 1) + pltpu.roll(kept, 64, 1)
    high = kept.astype(jnp.bfloat16).astype(jnp.float32)
    middle = (kept - high).astype(jnp.bfloat16).astype(jnp.float32)
    low = kept - high - middle
    part = lane // 32
    return jnp.where(part == 0, high, jnp.where(part == 1, middle, low)).astype(jnp.bfloat16)


def joined_tile(tile):
    tile = tile.astype(jnp.float32)
    return tile + pltpu.roll(tile, 128 - 32, 1) + pltpu.roll(tile, 128 - 64, 1)


def slanted(base, rows):
    return pltpu.roll(jnp.broadcast_to(base, (rows, base.shape[1])), 0, 1, stride=1, stride_axis=0)


def local_forward(base, book_column, book_row, own, halos, heads, score_scale):
    rows, width = own.shape[0], own.shape[1] // 3
    head_dim = width // heads
    count = len(halos) + 1

    def begin(ins, outs, scratch):
        base_ref, column_ref, row_ref, own_ref, *halo_refs = ins
        out_ref, log_ref = outs

        def run():
            same = column_ref[:, :1] == row_ref[:1, :]
            logs = []
            for head in range(heads):
                columns = slice(head * head_dim, (head + 1) * head_dim)
                above = slice(width + head * head_dim, width + (head + 1) * head_dim)
                twice = slice(2 * width + head * head_dim, 2 * width + (head + 1) * head_dim)
                keys = [ref[:, columns] for ref in halo_refs] + [own_ref[:, above]]
                values = [ref[:, above] for ref in halo_refs] + [own_ref[:, twice]]
                q = own_ref[:, columns]
                raw = [
                    lax.dot_general(q, k, contract_cols, preferred_element_type=jnp.float32) for k in keys
                ]
                bias = slanted(base_ref[head : head + 1, :], rows)[:, : count * rows]
                scores = jnp.concatenate(raw, axis=1) * score_scale + bias
                scores = jnp.where(same, scores, masked_score)
                top = jnp.max(scores, axis=1, keepdims=True)
                weights = jnp.exp(scores - top)
                total = jnp.sum(weights, axis=1, keepdims=True)
                weights = (weights / total).astype(jnp.bfloat16)
                out_ref[:, columns] = sum(
                    jnp.dot(
                        weights[:, i * rows : (i + 1) * rows], v, preferred_element_type=jnp.float32
                    )
                    for i, v in enumerate(values)
                )
                logs.append(top + jnp.log(total))
            log_ref[...] = lane_tile(logs, rows)

        return run

    arrays = [base, book_column, book_row, own, *halos]
    specs = [pl.BlockSpec(memory_space=pltpu.VMEM)] * len(arrays)
    out_shape = [
        jax.ShapeDtypeStruct((rows, width), jnp.float32),
        jax.ShapeDtypeStruct((rows, 128), jnp.float32),
    ]
    return arrays, specs, out_shape, [], begin


def sent_gradients(d_mixed, memory_out, local_out, mem_log, local_log, share, heads):
    rows, width = d_mixed.shape
    head_dim = width // heads

    def kernel(mix_ref, mem_ref, loc_ref, mem_log_ref, log_ref, share_ref, gate_ref, sent_ref):
        mem_deltas, deltas = [], []
        for head in range(heads):
            columns = slice(head * head_dim, (head + 1) * head_dim)
            share_here = share_ref[head]
            d_mix, mem_here, loc_here = mix_ref[:, columns], mem_ref[:, columns], loc_ref[:, columns]
            d_mem = (share_here * d_mix).astype(jnp.bfloat16)
            d_out = ((1.0 - share_here) * d_mix).astype(jnp.bfloat16)
            sent_ref[:, columns] = d_mem
            mem_deltas.append(jnp.sum(d_mem.astype(jnp.float32) * mem_here, axis=1, keepdims=True))
            deltas.append(jnp.sum(d_out.astype(jnp.float32) * loc_here, axis=1, keepdims=True))
            gate_ref[head : head + 1, :] = jnp.sum(
                d_mix * (mem_here - loc_here), axis=0, keepdims=True
            )
        mem_logs = [mem_log_ref[:, head : head + 1] for head in range(heads)]
        logs = [log_ref[:, head : head + 1] for head in range(heads)]
        sent_ref[:, width:] = split_tile(lane_tile(mem_logs + mem_deltas + logs + deltas, rows))

    vmem = pl.BlockSpec(memory_space=pltpu.VMEM)
    return pl.pallas_call(
        kernel,
        in_specs=[vmem] * 5 + [pl.BlockSpec(memory_space=pltpu.SMEM)],
        out_shape=[
            jax.ShapeDtypeStruct((heads, head_dim), jnp.float32),
            jax.ShapeDtypeStruct((rows, width + 128), jnp.bfloat16),
        ],
        compiler_params=pltpu.CompilerParams(vmem_limit_bytes=VMEM_LIMIT),
        cost_estimate=lasting(3),
        name="sent_gradients",
    )(d_mixed, memory_out, local_out, mem_log, local_log, share)


def local_queries(
    base, book_column, book_row, own, halos, d_mixed, local_out, local_log, share, heads, score_scale
):
    rows, width = d_mixed.shape
    head_dim = width // heads
    count = len(halos) + 1
    span = base.shape[1]

    def begin(ins, outs, scratch):
        base_ref, column_ref, row_ref, own_ref, mix_ref, loc_ref, log_ref, share_ref, *halo_refs = ins
        dq_ref, diagonal_ref = outs

        def run():
            same = column_ref[:, :1] == row_ref[:1, :]
            turned = (
                lax.broadcasted_iota(jnp.int32, (rows, rows), 0)
                + lax.broadcasted_iota(jnp.int32, (rows, rows), 1)
                == rows - 1
            ).astype(jnp.bfloat16)
            for head in range(heads):
                columns = slice(head * head_dim, (head + 1) * head_dim)
                above = slice(width + head * head_dim, width + (head + 1) * head_dim)
                twice = slice(2 * width + head * head_dim, 2 * width + (head + 1) * head_dim)
                keys = [ref[:, columns] for ref in halo_refs] + [own_ref[:, above]]
                values = [ref[:, above] for ref in halo_refs] + [own_ref[:, twice]]
                q = own_ref[:, columns]
                d_out = ((1.0 - share_ref[head]) * mix_ref[:, columns]).astype(jnp.bfloat16)
                delta = jnp.sum(
                    d_out.astype(jnp.float32) * loc_ref[:, columns], axis=1, keepdims=True
                )
                raw = [
                    lax.dot_general(q, k, contract_cols, preferred_element_type=jnp.float32)
                    for k in keys
                ]
                bias = slanted(base_ref[head : head + 1, :], rows)[:, : count * rows]
                scores = jnp.concatenate(raw, axis=1) * score_scale + bias
                probs = jnp.exp(jnp.where(same, scores - log_ref[:, head : head + 1], masked_score))
                products = [
                    lax.dot_general(d_out, v, contract_cols, preferred_element_type=jnp.float32)
                    for v in values
                ]
                slopes = (probs * (jnp.concatenate(products, axis=1) - delta)).astype(jnp.bfloat16)
                slope_blocks = [slopes[:, i * rows : (i + 1) * rows] for i in range(count)]
                dq_ref[:, columns] = score_scale * sum(
                    jnp.dot(s, k, preferred_element_type=jnp.float32)
                    for s, k in zip(slope_blocks, keys)
                )
                mirrored = [
                    jnp.dot(s, turned, preferred_element_type=jnp.float32) for s in slope_blocks[::-1]
                ]
                mirrored.append(jnp.zeros((rows, span - count * rows), jnp.float32))
                leaned = pltpu.roll(jnp.concatenate(mirrored, axis=1), 0, 1, stride=1, stride_axis=0)
                diagonal_ref[head : head + 1, :] = jnp.sum(leaned, axis=0, keepdims=True)

        return run

    vmem = pl.BlockSpec(memory_space=pltpu.VMEM)
    arrays = [base, book_column, book_row, own, d_mixed, local_out, local_log, share, *halos]
    specs = [vmem] * 7 + [pl.BlockSpec(memory_space=pltpu.SMEM)] + [vmem] * len(halos)
    out_shape = [
        jax.ShapeDtypeStruct((rows, width), jnp.float32),
        jax.ShapeDtypeStruct((heads, span), jnp.float32),
    ]
    return arrays, specs, out_shape, [], begin


def local_keys(base, book_column, book_row, own, queries, sent, ratio, count, heads, score_scale):
    rows, width = own.shape[0], own.shape[1] // 3
    head_dim = width // heads
    groups = queries.shape[0] // rows

    def begin(ins, outs, scratch):
        base_ref, column_ref, row_ref, own_ref, ratio_ref, queries_ref, sent_ref = ins
        (out_ref,) = outs
        queries_here, sent_here, sems = scratch
        copies = []
        for i in range(count):
            index = jnp.minimum(lax.axis_index("mem") + i, groups - 1)
            there = pl.ds(pl.multiple_of(index * rows, rows), rows)
            copies.append(
                pltpu.make_async_copy(queries_ref.at[there, :], queries_here.at[i], sems.at[0, i])
            )
            copies.append(pltpu.make_async_copy(sent_ref.at[there, :], sent_here.at[i], sems.at[1, i]))
        for copy in copies:
            copy.start()

        def run():
            for copy in copies:
                copy.wait()
            same = column_ref[:, :1] == row_ref[:1, :]
            stats = jnp.concatenate([joined_tile(sent_here[i, :, width:]).T for i in range(count)], axis=1)
            for head in range(heads):
                columns = slice(head * head_dim, (head + 1) * head_dim)
                above = slice(width + head * head_dim, width + (head + 1) * head_dim)
                twice = slice(2 * width + head * head_dim, 2 * width + (head + 1) * head_dim)
                k, v = own_ref[:, above], own_ref[:, twice]
                qs = [queries_here[i, :, columns] for i in range(count)]
                gs = [
                    (sent_here[i, :, columns].astype(jnp.float32) * ratio_ref[head]).astype(jnp.bfloat16)
                    for i in range(count)
                ]
                raw = [
                    lax.dot_general(k, q, contract_cols, preferred_element_type=jnp.float32) for q in qs
                ]
                bias = slanted(base_ref[head : head + 1, :], rows)[:, : count * rows]
                scores = jnp.concatenate(raw, axis=1) * score_scale + bias
                log = stats[2 * heads + head : 2 * heads + head + 1, :]
                delta = stats[3 * heads + head : 3 * heads + head + 1, :]
                probs = jnp.exp(jnp.where(same, scores - log, masked_score))
                products = [
                    lax.dot_general(v, g, contract_cols, preferred_element_type=jnp.float32) for g in gs
                ]
                slopes = (probs * (jnp.concatenate(products, axis=1) - delta)).astype(jnp.bfloat16)
                weights = probs.astype(jnp.bfloat16)
                blocks = [slice(i * rows, (i + 1) * rows) for i in range(count)]
                d_key = sum(
                    jnp.dot(slopes[:, b], q, preferred_element_type=jnp.float32) for b, q in zip(blocks, qs)
                )
                d_value = sum(
                    jnp.dot(weights[:, b], g, preferred_element_type=jnp.float32)
                    for b, g in zip(blocks, gs)
                )
                out_ref[:, columns] = (d_key * score_scale).astype(jnp.bfloat16)
                out_ref[:, above] = d_value.astype(jnp.bfloat16)

        return run

    vmem, anywhere = pl.BlockSpec(memory_space=pltpu.VMEM), pl.BlockSpec(memory_space=pl.ANY)
    arrays = [base, book_column, book_row, own, ratio, queries, sent]
    specs = [vmem] * 4 + [pl.BlockSpec(memory_space=pltpu.SMEM), anywhere, anywhere]
    scratch = [
        pltpu.VMEM((count, rows, width), jnp.bfloat16),
        pltpu.VMEM((count, rows, width + 128), jnp.bfloat16),
        pltpu.SemaphoreType.DMA((2, count)),
    ]
    return arrays, specs, [jax.ShapeDtypeStruct((rows, 2 * width), jnp.bfloat16)], scratch, begin


def feed_forward(normed_mid, cotangent, up_weight, down_weight):
    rows, width = normed_mid.shape
    hidden = up_weight.shape[1]
    block = math.gcd(hidden, 1024)

    def kernel(mid_ref, cot_ref, up_ref, down_ref, act_ref, d_up_ref, branch_ref, d_mid_ref):
        first = pl.program_id(0) == 0
        up = jnp.dot(mid_ref[...], up_ref[...], preferred_element_type=jnp.float32)
        d_act = jnp.dot(cot_ref[...], down_ref[...], preferred_element_type=jnp.float32)
        below = 0.5 * (1.0 + lax.erf(up * math.sqrt(0.5)))
        density = jnp.exp(-0.5 * up * up) * (1.0 / math.sqrt(2.0 * math.pi))
        act = (up * below).astype(jnp.bfloat16)
        d_up = (d_act * (below + up * density)).astype(jnp.bfloat16)
        act_ref[...] = act
        d_up_ref[...] = d_up
        branch = lax.dot_general(act, down_ref[...], contract_cols, preferred_element_type=jnp.float32)
        d_mid = lax.dot_general(d_up, up_ref[...], contract_cols, preferred_element_type=jnp.float32)
        branch_ref[...] = jnp.where(first, branch, branch_ref[...] + branch)
        d_mid_ref[...] = jnp.where(first, d_mid, d_mid_ref[...] + d_mid)

    whole = pl.BlockSpec((rows, width), lambda i: (0, 0))
    weight = pl.BlockSpec((width, block), lambda i: (0, i))
    middle = pl.BlockSpec((rows, block), lambda i: (0, i))
    return pl.pallas_call(
        kernel,
        grid=(hidden // block,),
        in_specs=[whole, whole, weight, weight],
        out_specs=[middle, middle, whole, whole],
        out_shape=[
            jax.ShapeDtypeStruct((rows, hidden), jnp.bfloat16),
            jax.ShapeDtypeStruct((rows, hidden), jnp.bfloat16),
            jax.ShapeDtypeStruct((rows, width), jnp.float32),
            jax.ShapeDtypeStruct((rows, width), jnp.float32),
        ],
        compiler_params=pltpu.CompilerParams(vmem_limit_bytes=VMEM_LIMIT),
        cost_estimate=lasting(15),
        name="feed_forward",
    )(normed_mid, cotangent, up_weight, down_weight)


def exchange_pairs(lefts, rights, other_lefts, other_right, send, recv):
    core = lax.axis_index("dp")
    copies, at = [], 0

    def push(source, target):
        i = len(copies)
        copy = pltpu.make_async_remote_copy(
            src_ref=source,
            dst_ref=target,
            send_sem=send.at[i],
            recv_sem=recv.at[i],
            device_id={"dp": 1 - core},
            device_id_type=pl.DeviceIdType.MESH,
        )
        copy.start()
        copies.append(copy)

    for i, (left, right) in enumerate(zip(lefts, rights)):
        half = right.shape[1] // 2
        push(left, other_lefts.at[i])
        there = pl.ds(pl.multiple_of((1 - core) * half, 128), half)
        push(right.at[:, there], other_right.at[:, pl.ds(at, half)])
        at += half
    return copies


def pair_products(lefts, rights, other_lefts, other_right, turned, store):
    core = lax.axis_index("dp")
    rows = lefts[0].shape[0]
    at = 0
    for i, (left, right) in enumerate(zip(lefts, rights)):
        half = right.shape[1] // 2
        turned[:, :rows] = left[...].T
        turned[:, rows:] = other_lefts[i].T
        block = math.gcd(half, 512)
        for column in range(0, half, block):
            kept = right[:, pl.ds(pl.multiple_of(core * half + column, 128), block)]
            both = jnp.concatenate([kept, other_right[:, at + column : at + column + block]], axis=0)
            store(
                at + column,
                jnp.dot(turned[...], both, preferred_element_type=jnp.float32).astype(jnp.bfloat16),
            )
        at += half


def pair_scratch(lefts, rights):
    rows, width = lefts[0].shape
    count = len(lefts)
    return [
        pltpu.VMEM((count, rows, width), jnp.bfloat16),
        pltpu.VMEM((rows, sum(right.shape[1] for right in rights) // 2), jnp.bfloat16),
        pltpu.VMEM((width, 2 * rows), jnp.bfloat16),
        pltpu.SemaphoreType.DMA((2 * count,)),
        pltpu.SemaphoreType.DMA((2 * count,)),
    ]


def pair_grads(lefts, rights, collective_id):
    count, width = len(lefts), lefts[0].shape[1]
    total = sum(right.shape[1] for right in rights) // 2
    block = math.gcd(*[right.shape[1] // 2 for right in rights], 512)

    def kernel(*refs):
        left_refs, right_refs, out_ref = refs[:count], refs[count : 2 * count], refs[2 * count]
        other_lefts, other_right, turned, send, recv, staged, out_sem = refs[2 * count + 1 :]
        barrier = pltpu.get_barrier_semaphore()
        partner = {"dp": 1 - lax.axis_index("dp")}
        pl.semaphore_signal(barrier, inc=1, device_id=partner, device_id_type=pl.DeviceIdType.MESH)
        pl.semaphore_wait(barrier, 1)
        copies = exchange_pairs(left_refs, right_refs, other_lefts, other_right, send, recv)
        for copy in copies:
            copy.wait_recv()
        written = []

        def store(column, value):
            slot = len(written) % 2
            if len(written) >= 2:
                written[-2].wait()
            staged[slot] = value
            copy = pltpu.make_async_copy(
                staged.at[slot], out_ref.at[:, pl.ds(column, block)], out_sem.at[slot]
            )
            copy.start()
            written.append(copy)

        pair_products(left_refs, right_refs, other_lefts, other_right, turned, store)
        for copy in written[-2:]:
            copy.wait()
        for copy in copies:
            copy.wait_send()

    vmem = pl.BlockSpec(memory_space=pltpu.VMEM)
    return pl.pallas_call(
        kernel,
        in_specs=[vmem] * (2 * count),
        out_specs=pl.BlockSpec(memory_space=pl.ANY),
        out_shape=jax.ShapeDtypeStruct((width, total), jnp.bfloat16),
        scratch_shapes=pair_scratch(lefts, rights)
        + [pltpu.VMEM((2, width, block), jnp.bfloat16), pltpu.SemaphoreType.DMA((2,))],
        compiler_params=pltpu.CompilerParams(
            collective_id=collective_id, has_side_effects=True, vmem_limit_bytes=VMEM_LIMIT
        ),
        cost_estimate=lasting(10),
        name="pair_grads",
    )(*lefts, *rights)


def input_backward(tokens, attn_gain, d_projected, qkv_weight, d_residual):
    rows, width = tokens.shape

    def begin(ins, outs, scratch):
        tokens_ref, gain_ref, d_ref, weight_ref, residual_ref = ins
        grad_ref, part_ref = outs
        weight_here, sem = scratch
        copy = pltpu.make_async_copy(weight_ref, weight_here, sem)
        copy.start()

        def run():
            copy.wait()
            d_in = lax.dot_general(
                d_ref[...], weight_here[...], contract_cols, preferred_element_type=jnp.float32
            )
            x = tokens_ref[...].astype(jnp.float32)
            scale = lax.rsqrt(jnp.mean(x * x, axis=1, keepdims=True) + eps_norm)
            wanted = d_in * gain_ref[...]
            slope = jnp.mean(x * wanted, axis=1, keepdims=True) * scale * scale * scale
            grad_ref[...] = residual_ref[...] + scale * wanted - x * slope
            part_ref[...] = jnp.sum(d_in * x * scale, axis=0, keepdims=True)

        return run

    vmem = pl.BlockSpec(memory_space=pltpu.VMEM)
    arrays = [tokens, attn_gain[None, :], d_projected, qkv_weight, d_residual]
    specs = [vmem, vmem, vmem, pl.BlockSpec(memory_space=pl.ANY), vmem]
    out_shape = [
        jax.ShapeDtypeStruct((rows, width), jnp.float32),
        jax.ShapeDtypeStruct((1, width), jnp.float32),
    ]
    scratch = [pltpu.VMEM(qkv_weight.shape, qkv_weight.dtype), pltpu.SemaphoreType.DMA]
    return arrays, specs, out_shape, scratch, begin


def spread_halves(halves, outs):
    at = 0
    for out in outs:
        half = out.shape[1] // 2
        for c in (0, 1):
            out[:, c * half : (c + 1) * half] = halves[c, :, at : at + half].astype(jnp.float32)
        at += half


def join_halves(sums, widths, collective_id):
    def kernel(sums_ref, *refs):
        outs, (both, send, recv) = refs[: len(widths)], refs[len(widths) :]
        core = lax.axis_index("dp")
        partner = {"dp": 1 - core}
        barrier = pltpu.get_barrier_semaphore()
        pl.semaphore_signal(barrier, inc=1, device_id=partner, device_id_type=pl.DeviceIdType.MESH)
        pl.semaphore_wait(barrier, 1)
        copy = pltpu.make_async_remote_copy(
            src_ref=sums_ref,
            dst_ref=both.at[core],
            send_sem=send,
            recv_sem=recv,
            device_id=partner,
            device_id_type=pl.DeviceIdType.MESH,
        )
        copy.start()
        both[core] = sums_ref[...]
        copy.wait()
        spread_halves(both, outs)

    vmem = pl.BlockSpec(memory_space=pltpu.VMEM)
    return pl.pallas_call(
        kernel,
        in_specs=[vmem],
        out_specs=[vmem] * len(widths),
        out_shape=[jax.ShapeDtypeStruct((sums.shape[0], size), jnp.float32) for size in widths],
        scratch_shapes=[
            pltpu.VMEM((2, *sums.shape), sums.dtype),
            pltpu.SemaphoreType.DMA,
            pltpu.SemaphoreType.DMA,
        ],
        compiler_params=pltpu.CompilerParams(
            collective_id=collective_id, has_side_effects=True, vmem_limit_bytes=VMEM_LIMIT
        ),
        cost_estimate=lasting(5),
        name="join_halves",
    )(sums)


def finish_grads(lefts, rights, small, sources, collective_id, beside):
    width, total = lefts[0].shape[1], sum(right.shape[1] for right in rights) // 2
    rows = width // sources
    count = len(lefts)
    late_widths = [right.shape[1] for right in rights]
    arrays, specs, more_out, more_scratch, begin = beside
    mesh_type = pl.DeviceIdType.MESH
    ref_shapes, sem_shapes = reduce_scratch(rows, total, jnp.bfloat16, sources)
    pair_shapes = pair_scratch(lefts, rights)
    sizes = [count, count, len(arrays), 1, count, 1, len(more_out)]
    sizes += [len(ref_shapes), len(sem_shapes), len(pair_shapes), len(more_scratch), 9]

    def kernel(*refs):
        groups, at = [], 0
        for size in sizes:
            groups.append(refs[at : at + size])
            at += size
        left_refs, right_refs, ins, (small_ref,), late_outs, (small_out,), more_refs = groups[:7]
        steps_refs, steps_sems, (other_lefts, other_right, turned, pair_send, pair_recv), scratch, own = groups[7:]
        parts, late, small_mine, smalls, core_small, small_send, small_recv, core_send, core_recv = own
        meanwhile = begin(ins, more_refs, scratch)
        me, core = lax.axis_index("mem"), lax.axis_index("dp")
        barrier = pltpu.get_barrier_semaphore()
        peers = [lax.rem(me + k, sources) for k in range(1, sources)]
        for peer in peers:
            pl.semaphore_signal(barrier, inc=1, device_id={"mem": peer}, device_id_type=mesh_type)
        pl.semaphore_signal(barrier, inc=1, device_id={"dp": 1 - core}, device_id_type=mesh_type)
        pl.semaphore_wait(barrier, sources)

        def merge(blocks):
            total = blocks[0][...].astype(jnp.float32)
            for block in blocks[1:]:
                total = total + block[...].astype(jnp.float32)
            return total

        def pack(target, total):
            target[...] = total.astype(jnp.bfloat16)

        def across_cores(source, target, i):
            copy = pltpu.make_async_remote_copy(
                src_ref=source,
                dst_ref=target,
                send_sem=core_send.at[i],
                recv_sem=core_recv.at[i],
                device_id={"dp": 1 - core},
                device_id_type=mesh_type,
            )
            copy.start()
            return copy

        pair_copies = exchange_pairs(
            left_refs, right_refs, other_lefts, other_right, pair_send, pair_recv
        )
        for copy in pair_copies:
            copy.wait_recv()

        def store(column, value):
            parts[:, column : column + value.shape[1]] = value

        pair_products(left_refs, right_refs, other_lefts, other_right, turned, store)
        small_copies = [
            remote(small_mine, smalls.at[me], small_send.at[i], small_recv.at[me], peer)
            for i, peer in enumerate(peers)
        ]

        def between():
            meanwhile()
            small_mine[...] = small_ref[...]
            for i in range(width // 128):
                small_mine[i : i + 1, :] = more_refs[-1][:, i * 128 : (i + 1) * 128]
            smalls[me] = small_mine[...]
            for copy in small_copies:
                copy.start()

        final, still_open = reduce_steps(parts, sources, steps_refs, steps_sems, merge, pack, between)
        for here, blocks in final:
            late[core, here] = merge(blocks).astype(jnp.bfloat16)
        late_copy = across_cores(late.at[core], late.at[core], 0)
        for peer in peers:
            remote(
                smalls.at[peer], smalls.at[peer], small_send.at[0], small_recv.at[peer], peer
            ).wait_recv()
        group_small = smalls[0]
        for i in range(1, sources):
            group_small = group_small + smalls[i]
        core_small[0] = group_small
        small_copy = across_cores(core_small.at[0], core_small.at[1], 1)
        for copy in (late_copy, small_copy):
            copy.wait()
        spread_halves(late, late_outs)
        small_out[...] = core_small[0] + core_small[1]
        for copy in still_open + small_copies + pair_copies:
            copy.wait_send()

    vmem = pl.BlockSpec(memory_space=pltpu.VMEM)
    return pl.pallas_call(
        kernel,
        in_specs=[vmem] * (2 * count) + specs + [vmem],
        out_specs=[vmem] * (count + 1 + len(more_out)),
        out_shape=[jax.ShapeDtypeStruct((rows, size), jnp.float32) for size in late_widths]
        + [jax.ShapeDtypeStruct(small.shape, small.dtype)]
        + more_out,
        scratch_shapes=ref_shapes
        + sem_shapes
        + pair_shapes
        + more_scratch
        + [
            pltpu.VMEM((width, total), jnp.bfloat16),
            pltpu.VMEM((2, rows, total), jnp.bfloat16),
            pltpu.VMEM(small.shape, small.dtype),
            pltpu.VMEM((sources, *small.shape), small.dtype),
            pltpu.VMEM((2, *small.shape), small.dtype),
        ]
        + [pltpu.SemaphoreType.DMA((sources,))] * 2
        + [pltpu.SemaphoreType.DMA((2,))] * 2,
        compiler_params=pltpu.CompilerParams(
            collective_id=collective_id, has_side_effects=True, vmem_limit_bytes=VMEM_LIMIT
        ),
        cost_estimate=lasting(45),
        name="finish_grads",
    )(*lefts, *rights, *arrays, small)


def on_device(
    tokens,
    attn_gain,
    qkv_weight,
    out_weight,
    bias_table,
    gate_logit,
    ffn_gain,
    up_weight,
    down_weight,
    memory_keys,
    memory_values,
    book_lengths,
    slot_shard,
    slot_index,
    slot_live,
    cotangent,
):
    rows, width = tokens.shape
    heads, buckets = bias_table.shape
    head_dim = width // heads
    top_count = slot_index.shape[2]
    hidden = up_weight.shape[1]
    groups = lax.axis_size("mem")
    capacity = -(-3 * rows * heads * top_count // (2 * groups) // 128) * 128
    score_scale = 1.0 / math.sqrt(head_dim)
    repeats = W // rows
    span = W + 2 * rows
    me = lax.axis_index("mem")
    first_pos = me * rows
    lengths = book_lengths[0]
    window = jnp.arange(W + rows, dtype=jnp.int32)
    key_pos = first_pos - W + window
    key_book = jnp.where(key_pos >= 0, book_of(key_pos, lengths), -1)
    later_book = book_of(first_pos + window, lengths)
    own_book = jnp.broadcast_to(later_book[:rows, None], (rows, 128))
    key_book = jnp.broadcast_to(key_book[None, :], (8, W + rows))
    later_book = jnp.broadcast_to(later_book[None, :], (8, W + rows))
    bucket = bucket_of(jnp.arange(W, dtype=jnp.int32))
    one_hot = (bucket[:, None] == jnp.arange(buckets, dtype=jnp.int32)).astype(jnp.float32)
    offset_bias = jnp.einsum("rb,hb->hr", one_hot, bias_table, precision=lax.Precision.HIGHEST)
    after_bias = jnp.pad(offset_bias, ((0, 0), (0, span - W)), constant_values=masked_score)
    before_bias = jnp.pad(
        offset_bias[:, ::-1], ((0, 0), (1, span - W - 1)), constant_values=masked_score
    )
    tokens_f = tokens.astype(jnp.float32)
    normed_in = normed(tokens_f, attn_gain).astype(jnp.bfloat16)
    projected = jnp.dot(normed_in, qkv_weight, preferred_element_type=jnp.float32).astype(
        jnp.bfloat16
    )
    slots = memory_keys.shape[0]
    requests = place_requests(slot_shard, slot_index, slot_live, groups, capacity, slots)
    incoming = lax.all_to_all(requests, "mem", split_axis=0, concat_axis=0, tiled=True)
    keys_values, _ = lax.optimization_barrier((projected[:, width:], requests))
    halos = [passed_along(keys_values, "mem", distance) for distance in range(repeats, 0, -1)]
    index, row_ids, bounds = read_lists(incoming, heads, rows, slots)
    bounds = bounds.reshape(-1)
    key_rows, value_rows = gather_rows(
        index.reshape(-1), bounds, memory_keys, memory_values, heads, groups, capacity
    )
    all_queries = lax.all_gather(projected[:, :width], "mem", axis=0, tiled=True)
    local = local_forward(before_bias, own_book, key_book, projected, halos, heads, score_scale)
    partial = memory_forward(
        bounds,
        all_queries,
        key_rows,
        value_rows,
        row_ids,
        heads,
        groups,
        rows,
        score_scale,
    )
    if groups == 16:
        memory_out, mem_log, local_out, local_log = merge_partials(partial, groups, 1, heads, local)
    else:
        local_out, local_log = run_alone("local_forward", local)
        partial = lax.all_to_all(
            partial.reshape(groups, rows, width + 128),
            "mem",
            split_axis=0,
            concat_axis=0,
            tiled=True,
        ).reshape(groups * rows, width + 128)
        memory_out, mem_log = combine_partials(partial, heads, groups, rows)
    gate_share = jax.nn.sigmoid(gate_logit)
    share_wide = jnp.repeat(gate_share, head_dim)[None, :]
    mixed_heads = (share_wide * memory_out + (1.0 - share_wide) * local_out).astype(jnp.bfloat16)
    residual = tokens_f + jnp.dot(mixed_heads, out_weight, preferred_element_type=jnp.float32)
    normed_mid_f, norm_mid_back = jax.vjp(normed, residual, ffn_gain)
    normed_mid = normed_mid_f.astype(jnp.bfloat16)
    activated, d_up, ffn_branch, d_mid = feed_forward(normed_mid, cotangent, up_weight, down_weight)
    block_out = (residual + ffn_branch).astype(jnp.bfloat16)
    d_resid_part, ffn_gain_part = norm_mid_back(d_mid)
    d_residual = cotangent.astype(jnp.float32) + d_resid_part
    d_branch = d_residual.astype(jnp.bfloat16)
    early_halves = pair_grads(
        [mixed_heads, normed_mid, cotangent], [d_branch, d_up, activated], 5
    )
    early_sums = scattered(early_halves)
    d_after, _ = lax.optimization_barrier((d_branch, early_halves))
    d_mixed = lax.dot_general(
        d_after, out_weight, contract_cols, preferred_element_type=jnp.float32
    )
    gate_products, sent_grads = sent_gradients(
        d_mixed, memory_out, local_out, mem_log, local_log, gate_share, heads
    )
    gate_part = jnp.sum(gate_products, axis=1) * gate_share * (1.0 - gate_share)
    local = local_queries(
        before_bias,
        own_book,
        key_book,
        projected,
        halos,
        d_mixed,
        local_out,
        local_log,
        gate_share,
        heads,
        score_scale,
    )
    if groups == 16:
        all_grads, d_queries, diagonals = gather_group(sent_grads, groups, 2, local)
    else:
        all_grads = lax.all_gather(sent_grads, "mem", axis=0, tiled=True)
        d_queries, diagonals = run_alone("local_queries", local)
    bias_part = jnp.dot(diagonals[:, rows - 1 : rows - 1 + W], one_hot, precision=lax.Precision.HIGHEST)
    d_partial = memory_backward(
        bounds,
        all_queries,
        all_grads,
        key_rows,
        value_rows,
        row_ids,
        heads,
        groups,
        rows,
        score_scale,
    )
    local = local_keys(
        after_bias,
        own_book,
        later_book,
        projected,
        all_queries,
        all_grads,
        (1.0 - gate_share) / gate_share,
        repeats + 1,
        heads,
        score_scale,
    )
    if groups == 16:
        d_partial, d_keys_values = sum_blocks(d_partial, groups, 3, local)
    else:
        (d_keys_values,) = run_alone("local_keys", local)
        d_partial, d_keys_values = lax.optimization_barrier((d_partial, d_keys_values))
        d_partial = jnp.sum(
            lax.all_to_all(
                d_partial.reshape(groups, rows, width), "mem", split_axis=0, concat_axis=0, tiled=True
            ).astype(jnp.float32),
            axis=0,
        )
    d_queries = (d_queries + d_partial * score_scale).astype(jnp.bfloat16)
    d_projected = jnp.concatenate([d_queries, d_keys_values], axis=1)
    beside = input_backward(tokens, attn_gain, d_projected, qkv_weight, d_residual)
    small = jnp.concatenate([ffn_gain_part, bias_part.reshape(-1), gate_part], axis=0)
    small = jnp.pad(small, (width, -small.shape[0] % 1024)).reshape(-1, 128)
    early_widths = [width, hidden, hidden]
    if groups == 16:
        qkv_grad, small, tokens_grad, _ = finish_grads(
            [normed_in], [d_projected], small, groups, 4, beside
        )
        early_sums, small = lax.optimization_barrier((early_sums, small))
        out_grad, up_grad, down_grad = join_halves(early_sums, early_widths, 7)
    else:
        tokens_grad, attn_gain_part = run_alone("input_backward", beside)
        late_halves = pair_grads([normed_in], [d_projected], 6)
        late_halves, early_sums = lax.optimization_barrier((late_halves, early_sums))
        late_both = lax.all_gather(scattered(late_halves), "dp", axis=0)
        early_both = lax.all_gather(early_sums, "dp", axis=0)
        small = lax.psum(small.at[: width // 128].set(attn_gain_part.reshape(-1, 128)), ("dp", "mem"))
        out_grad, up_grad, down_grad = whole_grads(early_both, early_widths)
        qkv_grad = whole_grads(late_both, [3 * width])[0]
    small = small.reshape(-1)
    at_bias = 2 * width + heads * buckets
    return (
        block_out,
        tokens_grad,
        qkv_grad,
        out_grad,
        up_grad,
        down_grad,
        small[:width],
        small[width : 2 * width],
        small[2 * width : at_bias].reshape(heads, buckets),
        small[at_bias : at_bias + heads],
    )


def solution(mesh):
    in_specs = (
        P(("dp", "mem"), None),
        P(),
        P(),
        P(),
        P(),
        P(),
        P(),
        P(),
        P(),
        P("mem", None),
        P("mem", None),
        P("dp", None),
        P(("dp", "mem"), None, None, None),
        P(("dp", "mem"), None, None),
        P(("dp", "mem"), None, None),
        P(("dp", "mem"), None),
    )
    out_specs = (
        P(("dp", "mem"), None),
        P(("dp", "mem"), None),
        P("mem", None),
        P("mem", None),
        P("mem", None),
        P("mem", None),
        P(),
        P(),
        P(),
        P(),
    )
    return jax.shard_map(
        on_device, mesh=mesh, in_specs=in_specs, out_specs=out_specs, check_vma=False
    )
```

profile of v0, /device:TPU:9, one launch (start us, length us, event | category | flops | bytes accessed | tf_op | source)
XLA Modules:
  0.0 502.7 jit_solution(17710991709128725430)
XLA Ops:
  7.2 1.2 fusion
  9.6 3.9 convolution_convert_fusion.refs_3_
  14.9 7.3 %sort.7 = s32[32768]{0:T(1024)S(1)} sort(s32[32768]{0:T(1024)S(1)} %reshape.226), dimensions={0}, to_apply=%region_0.0 | sort | flops 491520 | bytes 262144 | tf_op jit(solution)/shard_map/sort | solution.py:55
  23.4 2.9 make_lists.1
  26.2 6.7 %all-to-all-start = ((s32[16,24,128]{2,1,0:T(8,128)}), s32[16,24,128]{2,1,0:T(8,128)}, u32[]{:S(2)}, u32[]{:S(2)}) async-start(s32[16,24,128]{2,1,0:T(8,128)} %make_lists.1), calls=%async_computation | async-start | bytes 393216 | tf_op jit(solution)/shard_map/all_to_all | solution.py:1573
  33.8 3.1 collective-permute-start.3
  36.9 3.1 collective-permute-start.2
  40.0 4.0 collective-permute-start.1
  44.0 3.1 collective-permute-start
  49.6 2.0 read_lists.1
  51.6 37.8 %gather_rows.1 = (bf16[49152,128]{1,0:T(8,128)(2,1)}, bf16[49152,128]{1,0:T(8,128)(2,1)}) custom-call(s32[49152]{0:T(1024)} %bitcast.28, s32[2048]{0:T(1024)} %bitcast.30, bf16[4096,1024]{1,0:T(8,128)(2,1)} %keys.1, bf16[4096,1024]{1,0:T(8,128)(2,1)} %values.1), custom_call_target="tpu_custom_call" | custom-call | bytes 126000000 | tf_op jit(solution)/shard_map/gather_rows/pallas_call | solution.py:176
  89.4 18.5 %all-gather.2.cloned.1.call-done.q_ref.refs_5_ = bf16[2048,1024]{1,0:T(8,128)(2,1)} async-done(((bf16[128,1024]{1,0:T(8,128)(2,1)}), bf16[2048,1024]{1,0:T(8,128)(2,1)}) %all-gather.2.cloned.1.call-update) | async-done | bytes 4194320 | tf_op jit(solution)/shard_map/all_gather | solution.py:1581
  107.8 24.2 %memory_forward.1.parts_ref = bf16[2048,1152]{1,0:T(8,128)(2,1)} custom-call(s32[2048]{0:T(1024)} %bitcast.31, bf16[2048,1024]{1,0:T(8,128)(2,1)} %all-gather.2.cloned.1.call-done.q_ref.refs_5_, bf16[49152,128]{1,0:T(8,128)(2,1)} %get-tuple-element.42.k_ref, bf16[49152,128]{1,0:T(8,128)(2,1)} %get-tuple-element.43.v_ref, s32[16,25,128]{2,1,0:T(8,128)} %get-tuple-element.44.id_ref), custom_call_target="tpu_custom_call" | custom-call | bytes 75000000 | tf_op jit(solution)/shard_map/memory_forward/pallas_call | solution.py:312
  133.4 68.5 %reduce_group.2 = (f32[128,1024]{1,0:T(8,128)}, f32[128,128]{1,0:T(8,128)}, f32[128,1024]{1,0:T(8,128)}, f32[128,128]{1,0:T(8,128)}) custom-call(bf16[2048,1152]{1,0:T(8,128)(2,1)} %memory_forward.1.parts_ref, f32[8,768]{1,0:T(8,128)} %pad.12.refs_0_, s32[128,128]{1,0:T(8,128)} %broadcast_in_dim.21.refs_1_, s32[8,640]{1,0:T(8,128)} %broadcast_in_dim.23.refs_2_, ...), custom_call_target="tpu_custom_call" | custom-call | bytes 150000000 | tf_op jit(solution)/shard_map/reduce_group/pallas_call | solution.py:821
  202.0 1.3 add_convert_fusion.2.refs_0_
  204.7 13.1 %feed_forward.1 = (bf16[128,4096]{1,0:T(8,128)(2,1)}, bf16[128,4096]{1,0:T(8,128)(2,1)}, f32[128,1024]{1,0:T(8,128)}, f32[128,1024]{1,0:T(8,128)}) custom-call(bf16[128,1024]{1,0:T(8,128)(2,1)} %multiply_convert_fusion.mid_ref.refs_1_, bf16[128,1024]{1,0:T(8,128)(2,1)} %refs_2_.2, bf16[1024,4096]{1,0:T(8,128)(2,1)} %up_ref.1, bf16[1024,4096]{1,0:T(8,128)(2,1)} %down_ref.1), custom_call_target="tpu_custom_call" | custom-call | bytes 45000000 | tf_op jit(solution)/shard_map/feed_forward/pallas_call | solution.py:1190
  217.8 1.2 multiply_reduce_fusion
  219.0 2.4 fusion.11
  221.4 14.3 %pair_grads.1 = bf16[1024,4608]{1,0:T(8,128)(2,1)} custom-call(bf16[128,1024]{1,0:T(8,128)(2,1)} %copy-done.5, bf16[128,1024]{1,0:T(8,128)(2,1)} %multiply_convert_fusion.mid_ref.refs_1_, bf16[128,1024]{1,0:T(8,128)(2,1)} %refs_2_.2, bf16[128,1024]{1,0:T(8,128)(2,1)} %get-tuple-element.52.refs_3_, bf16[128,4096]{1,0:T(8,128)(2,1)} %get-tuple-element.50.refs_4_, ...), custom_call_target="tpu_custom_call" | custom-call | bytes 30000000 | tf_op jit(solution)/shard_map/pair_grads/pallas_call | solution.py:1299
  236.6 1.6 fusion.13.mix_ref.refs_4_
  238.3 2.9 sent_gradients.1
  241.2 63.4 %gather_group.1 = (bf16[2048,1152]{1,0:T(8,128)(2,1)}, f32[128,1024]{1,0:T(8,128)}, f32[8,768]{1,0:T(8,128)}) custom-call(bf16[128,1152]{1,0:T(8,128)(2,1)} %get-tuple-element.55.x_ref, f32[8,768]{1,0:T(8,128)} %pad.12.refs_0_, s32[128,128]{1,0:T(8,128)} %broadcast_in_dim.21.refs_1_, s32[8,640]{1,0:T(8,128)} %broadcast_in_dim.23.refs_2_, ...), custom_call_target="tpu_custom_call" | custom-call | bytes 150000000 | tf_op jit(solution)/shard_map/gather_group/pallas_call | solution.py:667
  305.8 25.6 %memory_backward.1.parts_ref = bf16[2048,1024]{1,0:T(8,128)(2,1)} custom-call(s32[2048]{0:T(1024)} %bitcast.32, bf16[2048,1024]{1,0:T(8,128)(2,1)} %all-gather.2.cloned.1.call-done.q_ref.refs_5_, bf16[2048,1152]{1,0:T(8,128)(2,1)} %get-tuple-element.57.g_ref.refs_6_, bf16[49152,128]{1,0:T(8,128)(2,1)} %get-tuple-element.42.k_ref, ...), custom_call_target="tpu_custom_call" | custom-call | bytes 75000000 | tf_op jit(solution)/shard_map/memory_backward/pallas_call | solution.py:461
  332.0 90.3 %reduce_group.3 = (f32[128,1024]{1,0:T(8,128)}, bf16[128,2048]{1,0:T(8,128)(2,1)}) custom-call(bf16[2048,1024]{1,0:T(8,128)(2,1)} %memory_backward.1.parts_ref, f32[8,768]{1,0:T(8,128)} %pad.13.refs_0_, s32[128,128]{1,0:T(8,128)} %broadcast_in_dim.21.refs_1_, s32[8,640]{1,0:T(8,128)} %broadcast_in_dim.26.refs_2_, bf16[128,3072]{1,0:T(8,128)(2,1)} %copy-done.1, ...), custom_call_target="tpu_custom_call" | custom-call | bytes 150000000 | tf_op jit(solution)/shard_map/reduce_group/pallas_call | solution.py:821
  424.0 2.0 pad_maximum_fusion.refs_1_.refs_4_
  426.0 52.0 %finish_grads.1 = (f32[64,3072]{1,0:T(8,128)}, f32[24,128]{1,0:T(8,128)}, f32[128,1024]{1,0:T(8,128)}, f32[1,1024]{1,0:T(1,128)}) custom-call(bf16[128,1024]{1,0:T(8,128)(2,1)} %copy-done.3, bf16[128,3072]{1,0:T(8,128)(2,1)} %pad_maximum_fusion.refs_1_.refs_4_, bf16[128,1024]{1,0:T(8,128)(2,1)} %refs_2_.3, f32[1,1024]{1,0:T(1,128)} %bitcast.33, ...), custom_call_target="tpu_custom_call" | custom-call | bytes 135000000 | tf_op jit(solution)/shard_map/finish_grads/pallas_call | solution.py:1493
  478.7 1.3 slice_bitcast_fusion
  481.8 4.6 join_halves.1
  486.4 2.0 copy.33
  488.4 2.1 copy.34
  490.5 1.7 copy.35
  492.1 2.3 copy.36
  (96 shorter events, 17.7 us)
Async XLA Ops:
  7.2 196.1 %copy-start = (bf16[1024,1024]{1,0:T(8,128)(2,1)S(1)}, bf16[1024,1024]{1,0:T(8,128)(2,1)}, u32[]{:S(2)}) copy-start(bf16[1024,1024]{1,0:T(8,128)(2,1)} %param.19) | copy-start | bytes 6291460
  7.2 100.6 %all-gather.2.cloned.1.call-start = ((), (), s32[]{:S(2)}) async-start(), calls=%async_computation.2 | async-start | bytes 4456448 | tf_op jit(solution)/shard_map/all_gather | solution.py:1581
  9.6 4.0 copy-start.3
  9.6 4.9 copy-start.11
  9.6 4.9 copy-start.12
  9.6 4.8 copy-start.13
  13.6 75.8 %copy-start.1 = (bf16[128,3072]{1,0:T(8,128)(2,1)}, bf16[128,3072]{1,0:T(8,128)(2,1)S(1)}, u32[]{:S(2)}) copy-start(bf16[128,3072]{1,0:T(8,128)(2,1)S(1)} %convolution_convert_fusion.refs_3_) | copy-start | bytes 2359300
  13.6 33.5 %copy-start.20 = (s32[1,3]{1,0:T(1,128)S(1)}, s32[1,3]{1,0:T(1,128)}, u32[]{:S(2)}) copy-start(s32[1,3]{1,0:T(1,128)} %param.27) | copy-start | bytes 40
  13.6 33.7 %copy-start.21 = (f32[8]{0:T(128)S(1)}, f32[8]{0:T(128)}, u32[]{:S(2)}) copy-start(f32[8]{0:T(128)} %param.21) | copy-start | bytes 100
  13.6 34.3 %copy-start.19 = (f32[8,32]{1,0:T(8,128)S(1)}, f32[8,32]{1,0:T(8,128)}, u32[]{:S(2)}) copy-start(f32[8,32]{1,0:T(8,128)} %param.20) | copy-start | bytes 3076
  22.2 1.1 copy-start.8
  22.8 0.6 copy-start.18
  26.2 23.3 %all-to-all-start = ((s32[16,24,128]{2,1,0:T(8,128)}), s32[16,24,128]{2,1,0:T(8,128)}, u32[]{:S(2)}, u32[]{:S(2)}) async-start(s32[16,24,128]{2,1,0:T(8,128)} %make_lists.1), calls=%async_computation | async-start | bytes 393216 | tf_op jit(solution)/shard_map/all_to_all | solution.py:1573
  32.9 445.1 %reduce-scatter.2.cloned.1.call-start = ((), (), s32[]{:S(2)}) async-start(), calls=%async_computation.3 | async-start | bytes 10027008 | tf_op jit(solution)/shard_map/reduce_scatter | solution.py:903
  33.8 98.2 %collective-permute-start.3 = (bf16[128,2048]{1,0:T(8,128)(2,1)}, bf16[128,2048]{1,0:T(8,128)(2,1)S(1)}, u32[]{:S(2)}, u32[]{:S(2)}) collective-permute-start(bf16[128,2048]{1,0:T(8,128)(2,1)} %slice.46), channel_id=1, source_target_pairs={{0,1},{1,2},{2,3},{3,4},{4,5},{5,6},{6,7},{7,8},{8,9},{9,10},{10,1... | collective-permute-start | bytes 1572872 | tf_op jit(solution)/shard_map/ppermute | solution.py:25
  36.9 95.2 %collective-permute-start.2 = (bf16[128,2048]{1,0:T(8,128)(2,1)}, bf16[128,2048]{1,0:T(8,128)(2,1)}, u32[]{:S(2)}, u32[]{:S(2)}) collective-permute-start(bf16[128,2048]{1,0:T(8,128)(2,1)} %slice.46), channel_id=1, source_target_pairs={{0,2},{1,3},{2,4},{3,5},{4,6},{5,7},{6,8},{7,9},{8,10},{9,11},{10,... | collective-permute-start | bytes 1572872 | tf_op jit(solution)/shard_map/ppermute | solution.py:25
  40.0 92.1 %collective-permute-start.1 = (bf16[128,2048]{1,0:T(8,128)(2,1)}, bf16[128,2048]{1,0:T(8,128)(2,1)}, u32[]{:S(2)}, u32[]{:S(2)}) collective-permute-start(bf16[128,2048]{1,0:T(8,128)(2,1)} %slice.46), channel_id=1, source_target_pairs={{0,3},{1,4},{2,5},{3,6},{4,7},{5,8},{6,9},{7,10},{8,11},{9,12},{10... | collective-permute-start | bytes 1572872 | tf_op jit(solution)/shard_map/ppermute | solution.py:25
  44.0 88.1 %collective-permute-start = (bf16[128,2048]{1,0:T(8,128)(2,1)}, bf16[128,2048]{1,0:T(8,128)(2,1)}, u32[]{:S(2)}, u32[]{:S(2)}) collective-permute-start(bf16[128,2048]{1,0:T(8,128)(2,1)} %slice.46), channel_id=1, source_target_pairs={{0,4},{1,5},{2,6},{3,7},{4,8},{5,9},{6,10},{7,11},{8,12},{9,13},{1... | collective-permute-start | bytes 1572872 | tf_op jit(solution)/shard_map/ppermute | solution.py:25
  47.8 41.5 %copy-start.15 = (f32[8]{0:T(128)}, f32[8]{0:T(128)S(1)}, u32[]{:S(2)}) copy-start(f32[8]{0:T(128)S(1)} %get-tuple-element.75.share_ref.refs_7_) | copy-start | bytes 100
  132.0 1.4 copy-start.7
  133.4 69.8 %copy-start.2 = (bf16[128,1024]{1,0:T(8,128)(2,1)S(1)}, bf16[128,1024]{1,0:T(8,128)(2,1)}, u32[]{:S(2)}) copy-start(bf16[128,1024]{1,0:T(8,128)(2,1)} %refs_2_.3) | copy-start | bytes 786436
  133.4 70.4 %copy-start.14 = (f32[1024]{0:T(1024)S(1)}, f32[1024]{0:T(1024)}, u32[]{:S(2)}) copy-start(f32[1024]{0:T(1024)} %param.22) | copy-start | bytes 12292
  203.3 14.5 %copy-start.5 = (bf16[128,1024]{1,0:T(8,128)(2,1)}, bf16[128,1024]{1,0:T(8,128)(2,1)S(1)}, u32[]{:S(2)}) copy-start(bf16[128,1024]{1,0:T(8,128)(2,1)S(1)} %add_convert_fusion.2.refs_0_) | copy-start | bytes 786436
  204.7 14.3 %copy-start.4 = (bf16[128,1024]{1,0:T(8,128)(2,1)S(1)}, bf16[128,1024]{1,0:T(8,128)(2,1)}, u32[]{:S(2)}) copy-start(bf16[128,1024]{1,0:T(8,128)(2,1)} %refs_2_.2) | copy-start | bytes 786436
  235.7 1.0 copy-start.6
  241.2 64.5 %copy-start.17 = (f32[8,128]{1,0:T(8,128)S(1)}, f32[8,128]{1,0:T(8,128)}, u32[]{:S(2)}) copy-start(f32[8,128]{1,0:T(8,128)} %get-tuple-element.61) | copy-start | bytes 12292
  331.9 90.4 %copy-start.16 = (f32[8]{0:T(128)S(1)}, f32[8]{0:T(128)}, u32[]{:S(2)}) copy-start(f32[8]{0:T(128)} %copy-done.15) | copy-start | bytes 100
  332.0 91.0 %copy-start.10 = (f32[128,1024]{1,0:T(8,128)S(1)}, f32[128,1024]{1,0:T(8,128)}, u32[]{:S(2)}) copy-start(f32[128,1024]{1,0:T(8,128)} %get-tuple-element.56) | copy-start | bytes 1572868
  486.4 8.0 %copy-start.9 = (f32[64,4096]{1,0:T(8,128)S(1)}, f32[64,4096]{1,0:T(8,128)}, u32[]{:S(2)}) copy-start(f32[64,4096]{1,0:T(8,128)} %get-tuple-element.100) | copy-start | bytes 3145732
Sparse Core Ops, SparseCore 0:
  14.5 93.3 all-gather.1
  235.8 221.6 reduce-scatter.1
where the time goes:
time: 511 us; the launch traced here: 503 us
  Pallas kernels  402 us (79%)
  other arithmetic  21.2 us (4%)
  starting transfers between devices  20 us (4%)
  local copies, waits for them, and re-layouts  19 us (4%)
  waiting for transfers between devices  18.5 us (4%)
  between operations  14.9 us (3%)
  matrix products  7.41 us (1%)
    pallas_call x2, Pallas kernels, reduce_group(): pl.pallas_call(kernel, in_specs=[vmem, *specs], out_specs=[vmem] * (len(o...  159 us
    pallas_call x1, Pallas kernels, gather_group(): pl.pallas_call(kernel, in_specs=[pl.BlockSpec(memory_space=pl.ANY), *spec...  63.4 us
    pallas_call x1, Pallas kernels, finish_grads(): pl.pallas_call(kernel, in_specs=[vmem] * (2 * count) + specs + [vmem], ou...  52 us
    pallas_call x1, Pallas kernels, gather_rows(): pl.pallas_call(kernel, grid_spec=pltpu.PrefetchScalarGridSpec(num_scalar_...  37.8 us
    pallas_call x1, Pallas kernels, memory_backward(): pl.pallas_call(kernel, grid_spec=pltpu.PrefetchScalarGridSpec(num_scalar_...  25.6 us
    pallas_call x1, Pallas kernels, memory_forward(): pl.pallas_call(kernel, grid_spec=pltpu.PrefetchScalarGridSpec(num_scalar_...  24.2 us
    all_gather x1, waiting for transfers between devices, on_device(): lax.all_gather(projected[:, :width], 'mem', axis=0, tiled=True)  18.5 us
    pallas_call x1, Pallas kernels, pair_grads(): pl.pallas_call(kernel, in_specs=[vmem] * (2 * count), out_specs=pl.BlockS...  14.3 us
  transfers between devices with their start and end apart: 7, of which 1 were waited for; matrix products, arithmetic and copies ran while one was open for 4% of the time, Pallas kernels for 60%

commit v1 on v0

--- a/solution.py
+++ b/solution.py
@@ -34,11 +34,6 @@
     return (
         values * lax.rsqrt(jnp.mean(values * values, axis=-1, keepdims=True) + eps_norm) * gain_vec
     )
-
-
-def book_of(positions, lengths):
-    book_ends = jnp.cumsum(lengths, dtype=jnp.int32)
-    return jnp.sum((positions[..., None] >= book_ends).astype(jnp.int32), axis=-1)
 
 
 def place_requests(slot_shard, slot_index, slot_live, owners, capacity, slots):
@@ -583,8 +578,6 @@
             push(None, mine, part_of(me, part), 2, 0, 0, part, to_x)
             push(None, mine_y, part_of(me, 1 - part), 3, 0, 0, 1 - part, to_y)
 
-        meanwhile()
-
         def pass_on(condition, step, slot):
             def go():
                 arrived(to_x + step, 2, slot, 0)
@@ -639,6 +632,7 @@
                         sent.append((condition & onward, remote(here, here, send.at[kind, slot, part], own_sem, me)))
                     sent.append((condition, remote(here, here, send.at[2, slot, part], own_sem, to_x)))
                     sent.append((condition, remote(here, here, send.at[3, slot, part], own_sem, to_y)))
+            meanwhile(distance - 1, depth - 1)
             if distance == 1:
                 pass_on(None, 0, 0)
             else:
@@ -804,6 +798,9 @@
             at += size
         ins, out_refs, more_refs, steps_refs, steps_sems, scratch = groups
         meanwhile = begin(ins, more_refs, scratch)
+        last = finish
+        if finish is None:
+            meanwhile, last = meanwhile
         me, column, beside_x, beside_y, across, index_of = grid_place(depth)
         greet(
             [index_of(0, beside_x), index_of(0, beside_y)]
@@ -813,7 +810,10 @@
             parts_ref, sources, steps_refs, steps_sems, merge, pack, meanwhile
         )
         for here, blocks in final:
-            finish([out.at[here] for out in out_refs], merge(blocks))
+            if finish is None:
+                last(here, merge(blocks))
+            else:
+                last([out.at[here] for out in out_refs], merge(blocks))
         for copy in still_open:
             copy.wait_send()
 
@@ -832,8 +832,9 @@
     )(parts, *arrays)
 
 
-def sum_blocks(parts, sources, collective_id, beside):
-    rows, width = parts.shape[0] // sources, parts.shape[1]
+def sum_queries(parts, d_queries, sources, collective_id, score_scale, beside):
+    rows, width = d_queries.shape
+    arrays, specs, (whole,), more_scratch, begin = beside
 
     def merge(blocks):
         total = blocks[0][...].astype(jnp.float32)
@@ -844,11 +845,16 @@
     def pack(target, total):
         target[...] = total.astype(parts.dtype)
 
-    def finish(targets, total):
-        targets[0][...] = total
-
-    out_shape = [jax.ShapeDtypeStruct((rows, width), jnp.float32)]
-    return reduce_group(parts, sources, collective_id, merge, pack, finish, out_shape, beside)
+    def begin_both(ins, outs, scratch):
+        run = begin(ins[:-1], outs, scratch)
+
+        def finish(here, total):
+            outs[0][here, :width] = (ins[-1][here, :] + total * score_scale).astype(whole.dtype)
+
+        return run, finish
+
+    more = [*arrays, d_queries], [*specs, pl.BlockSpec(memory_space=pltpu.VMEM)], [whole], more_scratch, begin_both
+    return reduce_group(parts, sources, collective_id, merge, pack, None, [], more)[0]
 
 
 def merge_partials(parts, sources, collective_id, heads, beside):
@@ -903,14 +909,14 @@
     return lax.psum_scatter(halves, "mem", scatter_dimension=0, tiled=True)
 
 
-def whole_grads(both, widths):
-    both = both.astype(jnp.float32)
-    grads, at = [], 0
-    for size in widths:
-        half = size // 2
-        grads.append(jnp.concatenate([both[0, :, at : at + half], both[1, :, at : at + half]], 1))
-        at += half
-    return grads
+def same_book(lengths_ref, first_row, rows, first_lane, lanes):
+    row = lax.broadcasted_iota(jnp.int32, (rows, lanes), 0) + first_row
+    lane = lax.broadcasted_iota(jnp.int32, (rows, lanes), 1) + first_lane
+    end, same = 0, lane >= 0
+    for i in range(lengths_ref.shape[1]):
+        end = end + lengths_ref[0, i]
+        same = same & ((row >= end) == (lane >= end))
+    return same
 
 
 def lane_tile(columns, rows):
@@ -941,17 +947,18 @@
     return pltpu.roll(jnp.broadcast_to(base, (rows, base.shape[1])), 0, 1, stride=1, stride_axis=0)
 
 
-def local_forward(base, book_column, book_row, own, halos, heads, score_scale):
+def local_forward(base, lengths, own, halos, heads, score_scale):
     rows, width = own.shape[0], own.shape[1] // 3
     head_dim = width // heads
     count = len(halos) + 1
 
     def begin(ins, outs, scratch):
-        base_ref, column_ref, row_ref, own_ref, *halo_refs = ins
+        base_ref, lengths_ref, own_ref, *halo_refs = ins
         out_ref, log_ref = outs
 
         def run():
-            same = column_ref[:, :1] == row_ref[:1, :]
+            first = lax.axis_index("mem") * rows
+            same = same_book(lengths_ref, first, rows, first - (count - 1) * rows, count * rows)
             logs = []
             for head in range(heads):
                 columns = slice(head * head_dim, (head + 1) * head_dim)
@@ -981,8 +988,9 @@
 
         return run
 
-    arrays = [base, book_column, book_row, own, *halos]
-    specs = [pl.BlockSpec(memory_space=pltpu.VMEM)] * len(arrays)
+    arrays = [base, lengths, own, *halos]
+    vmem = pl.BlockSpec(memory_space=pltpu.VMEM)
+    specs = [vmem, pl.BlockSpec(memory_space=pltpu.SMEM)] + [vmem] * (1 + len(halos))
     out_shape = [
         jax.ShapeDtypeStruct((rows, width), jnp.float32),
         jax.ShapeDtypeStruct((rows, 128), jnp.float32),
@@ -1027,7 +1035,7 @@
 
 
 def local_queries(
-    base, book_column, book_row, own, halos, d_mixed, local_out, local_log, share, heads, score_scale
+    base, lengths, own, halos, d_mixed, local_out, local_log, share, heads, score_scale
 ):
     rows, width = d_mixed.shape
     head_dim = width // heads
@@ -1035,17 +1043,18 @@
     span = base.shape[1]
 
     def begin(ins, outs, scratch):
-        base_ref, column_ref, row_ref, own_ref, mix_ref, loc_ref, log_ref, share_ref, *halo_refs = ins
+        base_ref, lengths_ref, own_ref, mix_ref, loc_ref, log_ref, share_ref, *halo_refs = ins
         dq_ref, diagonal_ref = outs
 
-        def run():
-            same = column_ref[:, :1] == row_ref[:1, :]
+        def some_heads(some):
+            first = lax.axis_index("mem") * rows
+            same = same_book(lengths_ref, first, rows, first - (count - 1) * rows, count * rows)
             turned = (
                 lax.broadcasted_iota(jnp.int32, (rows, rows), 0)
                 + lax.broadcasted_iota(jnp.int32, (rows, rows), 1)
                 == rows - 1
             ).astype(jnp.bfloat16)
-            for head in range(heads):
+            for head in some:
                 columns = slice(head * head_dim, (head + 1) * head_dim)
                 above = slice(width + head * head_dim, width + (head + 1) * head_dim)
                 twice = slice(2 * width + head * head_dim, 2 * width + (head + 1) * head_dim)
@@ -1080,11 +1089,15 @@
                 leaned = pltpu.roll(jnp.concatenate(mirrored, axis=1), 0, 1, stride=1, stride_axis=0)
                 diagonal_ref[head : head + 1, :] = jnp.sum(leaned, axis=0, keepdims=True)
 
+        def run(part=0, parts=1):
+            some_heads(range(part * heads // parts, (part + 1) * heads // parts))
+
         return run
 
     vmem = pl.BlockSpec(memory_space=pltpu.VMEM)
-    arrays = [base, book_column, book_row, own, d_mixed, local_out, local_log, share, *halos]
-    specs = [vmem] * 7 + [pl.BlockSpec(memory_space=pltpu.SMEM)] + [vmem] * len(halos)
+    smem = pl.BlockSpec(memory_space=pltpu.SMEM)
+    arrays = [base, lengths, own, d_mixed, local_out, local_log, share, *halos]
+    specs = [vmem, smem] + [vmem] * 4 + [smem] + [vmem] * len(halos)
     out_shape = [
         jax.ShapeDtypeStruct((rows, width), jnp.float32),
         jax.ShapeDtypeStruct((heads, span), jnp.float32),
@@ -1092,13 +1105,13 @@
     return arrays, specs, out_shape, [], begin
 
 
-def local_keys(base, book_column, book_row, own, queries, sent, ratio, count, heads, score_scale):
+def local_keys(base, lengths, own, queries, sent, ratio, count, heads, score_scale):
     rows, width = own.shape[0], own.shape[1] // 3
     head_dim = width // heads
     groups = queries.shape[0] // rows
 
     def begin(ins, outs, scratch):
-        base_ref, column_ref, row_ref, own_ref, ratio_ref, queries_ref, sent_ref = ins
+        base_ref, lengths_ref, own_ref, ratio_ref, queries_ref, sent_ref = ins
         (out_ref,) = outs
         queries_here, sent_here, sems = scratch
         copies = []
@@ -1115,7 +1128,8 @@
         def run():
             for copy in copies:
                 copy.wait()
-            same = column_ref[:, :1] == row_ref[:1, :]
+            first = lax.axis_index("mem") * rows
+            same = same_book(lengths_ref, first, rows, first, count * rows)
             stats = jnp.concatenate([joined_tile(sent_here[i, :, width:]).T for i in range(count)], axis=1)
             for head in range(heads):
                 columns = slice(head * head_dim, (head + 1) * head_dim)
@@ -1148,20 +1162,21 @@
                     jnp.dot(weights[:, b], g, preferred_element_type=jnp.float32)
                     for b, g in zip(blocks, gs)
                 )
-                out_ref[:, columns] = (d_key * score_scale).astype(jnp.bfloat16)
-                out_ref[:, above] = d_value.astype(jnp.bfloat16)
+                out_ref[:, above] = (d_key * score_scale).astype(jnp.bfloat16)
+                out_ref[:, twice] = d_value.astype(jnp.bfloat16)
 
         return run
 
     vmem, anywhere = pl.BlockSpec(memory_space=pltpu.VMEM), pl.BlockSpec(memory_space=pl.ANY)
-    arrays = [base, book_column, book_row, own, ratio, queries, sent]
-    specs = [vmem] * 4 + [pl.BlockSpec(memory_space=pltpu.SMEM), anywhere, anywhere]
+    smem = pl.BlockSpec(memory_space=pltpu.SMEM)
+    arrays = [base, lengths, own, ratio, queries, sent]
+    specs = [vmem, smem, vmem, smem, anywhere, anywhere]
     scratch = [
         pltpu.VMEM((count, rows, width), jnp.bfloat16),
         pltpu.VMEM((count, rows, width + 128), jnp.bfloat16),
         pltpu.SemaphoreType.DMA((2, count)),
     ]
-    return arrays, specs, [jax.ShapeDtypeStruct((rows, 2 * width), jnp.bfloat16)], scratch, begin
+    return arrays, specs, [jax.ShapeDtypeStruct((rows, 3 * width), jnp.bfloat16)], scratch, begin
 
 
 def feed_forward(normed_mid, cotangent, up_weight, down_weight):
@@ -1230,12 +1245,14 @@
     return copies
 
 
-def pair_products(lefts, rights, other_lefts, other_right, turned, store):
+def pair_products(lefts, rights, other_lefts, other_right, turned, store, copies):
     core = lax.axis_index("dp")
     rows = lefts[0].shape[0]
     at = 0
     for i, (left, right) in enumerate(zip(lefts, rights)):
         half = right.shape[1] // 2
+        for copy in copies[2 * i : 2 * i + 2]:
+            copy.wait_recv()
         turned[:, :rows] = left[...].T
         turned[:, rows:] = other_lefts[i].T
         block = math.gcd(half, 512)
@@ -1274,8 +1291,6 @@
         pl.semaphore_signal(barrier, inc=1, device_id=partner, device_id_type=pl.DeviceIdType.MESH)
         pl.semaphore_wait(barrier, 1)
         copies = exchange_pairs(left_refs, right_refs, other_lefts, other_right, send, recv)
-        for copy in copies:
-            copy.wait_recv()
         written = []
 
         def store(column, value):
@@ -1289,7 +1304,7 @@
             copy.start()
             written.append(copy)
 
-        pair_products(left_refs, right_refs, other_lefts, other_right, turned, store)
+        pair_products(left_refs, right_refs, other_lefts, other_right, turned, store, copies)
         for copy in written[-2:]:
             copy.wait()
         for copy in copies:
@@ -1355,9 +1370,8 @@
         at += half
 
 
-def join_halves(sums, widths, collective_id):
-    def kernel(sums_ref, *refs):
-        outs, (both, send, recv) = refs[: len(widths)], refs[len(widths) :]
+def join_halves(sums, collective_id):
+    def kernel(sums_ref, both, send, recv):
         core = lax.axis_index("dp")
         partner = {"dp": 1 - core}
         barrier = pltpu.get_barrier_semaphore()
@@ -1374,47 +1388,70 @@
         copy.start()
         both[core] = sums_ref[...]
         copy.wait()
-        spread_halves(both, outs)
 
     vmem = pl.BlockSpec(memory_space=pltpu.VMEM)
     return pl.pallas_call(
         kernel,
         in_specs=[vmem],
-        out_specs=[vmem] * len(widths),
-        out_shape=[jax.ShapeDtypeStruct((sums.shape[0], size), jnp.float32) for size in widths],
-        scratch_shapes=[
-            pltpu.VMEM((2, *sums.shape), sums.dtype),
-            pltpu.SemaphoreType.DMA,
-            pltpu.SemaphoreType.DMA,
-        ],
+        out_specs=vmem,
+        out_shape=jax.ShapeDtypeStruct((2, *sums.shape), sums.dtype),
+        scratch_shapes=[pltpu.SemaphoreType.DMA, pltpu.SemaphoreType.DMA],
         compiler_params=pltpu.CompilerParams(
             collective_id=collective_id, has_side_effects=True, vmem_limit_bytes=VMEM_LIMIT
         ),
-        cost_estimate=lasting(5),
+        cost_estimate=lasting(4),
         name="join_halves",
     )(sums)
+
+
+def write_results(late, late_widths, early, early_widths, small, heads, buckets):
+    rows, width = late.shape[1], late.shape[2] * 2 // 3
+    lines = width // 128
+    count = len(late_widths) + len(early_widths)
+
+    def kernel(late_ref, early_ref, small_ref, *outs):
+        spread_halves(late_ref, outs[: len(late_widths)])
+        spread_halves(early_ref, outs[len(late_widths) : count])
+        attn_ref, ffn_ref, bias_ref, gate_ref = outs[count:]
+        attn_ref[...] = small_ref[:lines, :]
+        ffn_ref[...] = small_ref[lines : 2 * lines, :]
+        for head in range(heads):
+            line, lane = divmod(head * buckets, 128)
+            here = small_ref[2 * lines + line : 2 * lines + line + 1, :]
+            bias_ref[head : head + 1, :] = here[:, lane : lane + buckets]
+        line = 2 * lines + heads * buckets // 128
+        gate_ref[...] = small_ref[line : line + 1, :heads]
+
+    shapes = [(rows, size) for size in [*late_widths, *early_widths]]
+    shapes += [(lines, 128), (lines, 128), (heads, buckets), (1, heads)]
+    return pl.pallas_call(
+        kernel,
+        out_shape=[jax.ShapeDtypeStruct(shape, jnp.float32) for shape in shapes],
+        compiler_params=pltpu.CompilerParams(vmem_limit_bytes=VMEM_LIMIT),
+        cost_estimate=lasting(3),
+        name="write_results",
+    )(late, early, small)
 
 
 def finish_grads(lefts, rights, small, sources, collective_id, beside):
     width, total = lefts[0].shape[1], sum(right.shape[1] for right in rights) // 2
     rows = width // sources
     count = len(lefts)
-    late_widths = [right.shape[1] for right in rights]
     arrays, specs, more_out, more_scratch, begin = beside
     mesh_type = pl.DeviceIdType.MESH
     ref_shapes, sem_shapes = reduce_scratch(rows, total, jnp.bfloat16, sources)
     pair_shapes = pair_scratch(lefts, rights)
-    sizes = [count, count, len(arrays), 1, count, 1, len(more_out)]
-    sizes += [len(ref_shapes), len(sem_shapes), len(pair_shapes), len(more_scratch), 9]
+    sizes = [count, count, len(arrays), 1, 1, 1, len(more_out)]
+    sizes += [len(ref_shapes), len(sem_shapes), len(pair_shapes), len(more_scratch), 8]
 
     def kernel(*refs):
         groups, at = [], 0
         for size in sizes:
             groups.append(refs[at : at + size])
             at += size
-        left_refs, right_refs, ins, (small_ref,), late_outs, (small_out,), more_refs = groups[:7]
+        left_refs, right_refs, ins, (small_ref,), (late,), (small_out,), more_refs = groups[:7]
         steps_refs, steps_sems, (other_lefts, other_right, turned, pair_send, pair_recv), scratch, own = groups[7:]
-        parts, late, small_mine, smalls, core_small, small_send, small_recv, core_send, core_recv = own
+        parts, small_mine, smalls, core_small, small_send, small_recv, core_send, core_recv = own
         meanwhile = begin(ins, more_refs, scratch)
         me, core = lax.axis_index("mem"), lax.axis_index("dp")
         barrier = pltpu.get_barrier_semaphore()
@@ -1448,13 +1485,13 @@
         pair_copies = exchange_pairs(
             left_refs, right_refs, other_lefts, other_right, pair_send, pair_recv
         )
-        for copy in pair_copies:
-            copy.wait_recv()
 
         def store(column, value):
             parts[:, column : column + value.shape[1]] = value
 
-        pair_products(left_refs, right_refs, other_lefts, other_right, turned, store)
+        pair_products(
+            left_refs, right_refs, other_lefts, other_right, turned, store, pair_copies
+        )
         small_copies = [
             remote(small_mine, smalls.at[me], small_send.at[i], small_recv.at[me], peer)
             for i, peer in enumerate(peers)
@@ -1484,7 +1521,6 @@
         small_copy = across_cores(core_small.at[0], core_small.at[1], 1)
         for copy in (late_copy, small_copy):
             copy.wait()
-        spread_halves(late, late_outs)
         small_out[...] = core_small[0] + core_small[1]
         for copy in still_open + small_copies + pair_copies:
             copy.wait_send()
@@ -1493,8 +1529,8 @@
     return pl.pallas_call(
         kernel,
         in_specs=[vmem] * (2 * count) + specs + [vmem],
-        out_specs=[vmem] * (count + 1 + len(more_out)),
-        out_shape=[jax.ShapeDtypeStruct((rows, size), jnp.float32) for size in late_widths]
+        out_specs=[vmem] * (2 + len(more_out)),
+        out_shape=[jax.ShapeDtypeStruct((2, rows, total), jnp.bfloat16)]
         + [jax.ShapeDtypeStruct(small.shape, small.dtype)]
         + more_out,
         scratch_shapes=ref_shapes
@@ -1503,7 +1539,6 @@
         + more_scratch
         + [
             pltpu.VMEM((width, total), jnp.bfloat16),
-            pltpu.VMEM((2, rows, total), jnp.bfloat16),
             pltpu.VMEM(small.shape, small.dtype),
             pltpu.VMEM((sources, *small.shape), small.dtype),
             pltpu.VMEM((2, *small.shape), small.dtype),
@@ -1546,23 +1581,20 @@
     score_scale = 1.0 / math.sqrt(head_dim)
     repeats = W // rows
     span = W + 2 * rows
-    me = lax.axis_index("mem")
-    first_pos = me * rows
-    lengths = book_lengths[0]
-    window = jnp.arange(W + rows, dtype=jnp.int32)
-    key_pos = first_pos - W + window
-    key_book = jnp.where(key_pos >= 0, book_of(key_pos, lengths), -1)
-    later_book = book_of(first_pos + window, lengths)
-    own_book = jnp.broadcast_to(later_book[:rows, None], (rows, 128))
-    key_book = jnp.broadcast_to(key_book[None, :], (8, W + rows))
-    later_book = jnp.broadcast_to(later_book[None, :], (8, W + rows))
+    before = W - jnp.arange(span, dtype=jnp.int32)
+    after = jnp.arange(span, dtype=jnp.int32)
+
+    def bias_rows(offset):
+        reached = (offset >= 0) & (offset < W)
+        hot = (bucket_of(offset)[:, None] == jnp.arange(buckets, dtype=jnp.int32)) & reached[:, None]
+        rows_of_bias = jnp.einsum(
+            "rb,hb->hr", hot.astype(jnp.float32), bias_table, precision=lax.Precision.HIGHEST
+        )
+        return rows_of_bias + jnp.where(reached, 0.0, masked_score)
+
+    before_bias, after_bias = bias_rows(before), bias_rows(after)
     bucket = bucket_of(jnp.arange(W, dtype=jnp.int32))
     one_hot = (bucket[:, None] == jnp.arange(buckets, dtype=jnp.int32)).astype(jnp.float32)
-    offset_bias = jnp.einsum("rb,hb->hr", one_hot, bias_table, precision=lax.Precision.HIGHEST)
-    after_bias = jnp.pad(offset_bias, ((0, 0), (0, span - W)), constant_values=masked_score)
-    before_bias = jnp.pad(
-        offset_bias[:, ::-1], ((0, 0), (1, span - W - 1)), constant_values=masked_score
-    )
     tokens_f = tokens.astype(jnp.float32)
     normed_in = normed(tokens_f, attn_gain).astype(jnp.bfloat16)
     projected = jnp.dot(normed_in, qkv_weight, preferred_element_type=jnp.float32).astype(
@@ -1579,7 +1611,7 @@
         index.reshape(-1), bounds, memory_keys, memory_values, heads, groups, capacity
     )
     all_queries = lax.all_gather(projected[:, :width], "mem", axis=0, tiled=True)
-    local = local_forward(before_bias, own_book, key_book, projected, halos, heads, score_scale)
+    local = local_forward(before_bias, book_lengths, projected, halos, heads, score_scale)
     partial = memory_forward(
         bounds,
         all_queries,
@@ -1628,8 +1660,7 @@
     gate_part = jnp.sum(gate_products, axis=1) * gate_share * (1.0 - gate_share)
     local = local_queries(
         before_bias,
-        own_book,
-        key_book,
+        book_lengths,
         projected,
         halos,
         d_mixed,
@@ -1659,8 +1690,7 @@
     )
     local = local_keys(
         after_bias,
-        own_book,
-        later_book,
+        book_lengths,
         projected,
         all_queries,
         all_grads,
@@ -1670,28 +1700,28 @@
         score_scale,
     )
     if groups == 16:
-        d_partial, d_keys_values = sum_blocks(d_partial, groups, 3, local)
+        d_projected = sum_queries(d_partial, d_queries, groups, 3, score_scale, local)
     else:
-        (d_keys_values,) = run_alone("local_keys", local)
-        d_partial, d_keys_values = lax.optimization_barrier((d_partial, d_keys_values))
+        (d_projected,) = run_alone("local_keys", local)
+        d_partial, d_projected = lax.optimization_barrier((d_partial, d_projected))
         d_partial = jnp.sum(
             lax.all_to_all(
                 d_partial.reshape(groups, rows, width), "mem", split_axis=0, concat_axis=0, tiled=True
             ).astype(jnp.float32),
             axis=0,
         )
-    d_queries = (d_queries + d_partial * score_scale).astype(jnp.bfloat16)
-    d_projected = jnp.concatenate([d_queries, d_keys_values], axis=1)
+        d_queries = (d_queries + d_partial * score_scale).astype(jnp.bfloat16)
+        d_projected = jnp.concatenate([d_queries, d_projected[:, width:]], axis=1)
     beside = input_backward(tokens, attn_gain, d_projected, qkv_weight, d_residual)
     small = jnp.concatenate([ffn_gain_part, bias_part.reshape(-1), gate_part], axis=0)
     small = jnp.pad(small, (width, -small.shape[0] % 1024)).reshape(-1, 128)
     early_widths = [width, hidden, hidden]
     if groups == 16:
-        qkv_grad, small, tokens_grad, _ = finish_grads(
+        late_both, small, tokens_grad, _ = finish_grads(
             [normed_in], [d_projected], small, groups, 4, beside
         )
         early_sums, small = lax.optimization_barrier((early_sums, small))
-        out_grad, up_grad, down_grad = join_halves(early_sums, early_widths, 7)
+        early_both = join_halves(early_sums, 7)
     else:
         tokens_grad, attn_gain_part = run_alone("input_backward", beside)
         late_halves = pair_grads([normed_in], [d_projected], 6)
@@ -1699,10 +1729,9 @@
         late_both = lax.all_gather(scattered(late_halves), "dp", axis=0)
         early_both = lax.all_gather(early_sums, "dp", axis=0)
         small = lax.psum(small.at[: width // 128].set(attn_gain_part.reshape(-1, 128)), ("dp", "mem"))
-        out_grad, up_grad, down_grad = whole_grads(early_both, early_widths)
-        qkv_grad = whole_grads(late_both, [3 * width])[0]
-    small = small.reshape(-1)
-    at_bias = 2 * width + heads * buckets
+    qkv_grad, out_grad, up_grad, down_grad, attn_sum, ffn_sum, bias_sum, gate_sum = write_results(
+        late_both, [3 * width], early_both, early_widths, small, heads, buckets
+    )
     return (
         block_out,
         tokens_grad,
@@ -1710,10 +1739,10 @@
         out_grad,
         up_grad,
         down_grad,
-        small[:width],
-        small[width : 2 * width],
-        small[2 * width : at_bias].reshape(heads, buckets),
-        small[at_bias : at_bias + heads],
+        attn_sum.reshape(-1),
+        ffn_sum.reshape(-1),
+        bias_sum,
+        gate_sum.reshape(-1),
     )
 
 

time: 511 us -> 500 us (0.978)
  local copies, waits for them, and re-layouts: 19 us -> 4.85 us
    unnamed x49 -> x39, local copies, waits for them, and re-layouts: 9.37 us -> 2.75 us
  transfers between devices with their start and end apart: 7 -> 7, of which waited for: 1 -> 1; matrix products, arithmetic and copies ran while one was open for 4% -> 3% of each run, Pallas kernels for 60% -> 62%
where the time goes in v1:
time: 500 us; the launch traced here: 492 us
  Pallas kernels  407 us (81%)
  starting transfers between devices  20 us (4%)
  waiting for transfers between devices  18.4 us (4%)
  other arithmetic  17.9 us (4%)
  between operations  14.9 us (3%)
  matrix products  9.29 us (2%)
    pallas_call x2, Pallas kernels, reduce_group(): pl.pallas_call(kernel, in_specs=[vmem, *specs], out_specs=[vmem] * (len(o...  160 us
    pallas_call x1, Pallas kernels, gather_group(): pl.pallas_call(kernel, in_specs=[pl.BlockSpec(memory_space=pl.ANY), *spec...  63.4 us
    pallas_call x1, Pallas kernels, finish_grads(): pl.pallas_call(kernel, in_specs=[vmem] * (2 * count) + specs + [vmem], ou...  54.3 us
    pallas_call x1, Pallas kernels, gather_rows(): pl.pallas_call(kernel, grid_spec=pltpu.PrefetchScalarGridSpec(num_scalar_...  38.6 us
    pallas_call x1, Pallas kernels, memory_backward(): pl.pallas_call(kernel, grid_spec=pltpu.PrefetchScalarGridSpec(num_scalar_...  25.6 us
    pallas_call x1, Pallas kernels, memory_forward(): pl.pallas_call(kernel, grid_spec=pltpu.PrefetchScalarGridSpec(num_scalar_...  24.2 us
    all_gather x1, waiting for transfers between devices, on_device(): lax.all_gather(projected[:, :width], 'mem', axis=0, tiled=True)  18.3 us
    ppermute x4, starting transfers between devices, passed_along(): return lax.ppermute(value, axis, pairs)  13.3 us
  transfers between devices with their start and end apart: 7, of which 1 were waited for; matrix products, arithmetic and copies ran while one was open for 3% of the time, Pallas kernels for 62%

profile of v1, /device:TPU:9, one launch (start us, length us, event | category | flops | bytes accessed | tf_op | source)
XLA Modules:
  0.0 492.0 jit_solution(16260876276930021135)
XLA Ops:
  7.2 1.2 fusion.2
  8.5 1.1 fusion.4.refs_0_
  9.6 3.9 convolution_convert_fusion.refs_2_
  14.9 7.3 %sort.7 = s32[32768]{0:T(1024)S(1)} sort(s32[32768]{0:T(1024)S(1)} %reshape.322), dimensions={0}, to_apply=%region_0.1 | sort | flops 491520 | bytes 262144 | tf_op jit(solution)/shard_map/sort | solution.py:50
  23.4 2.9 make_lists.1
  26.2 6.7 %all-to-all-start = ((s32[16,24,128]{2,1,0:T(8,128)}), s32[16,24,128]{2,1,0:T(8,128)}, u32[]{:S(2)}, u32[]{:S(2)}) async-start(s32[16,24,128]{2,1,0:T(8,128)} %make_lists.1), calls=%async_computation | async-start | bytes 393216 | tf_op jit(solution)/shard_map/all_to_all | solution.py:1605
  33.8 3.1 collective-permute-start.3
  36.8 3.1 collective-permute-start.2
  40.0 4.0 collective-permute-start.1
  44.0 3.1 collective-permute-start
  47.8 1.1 fusion.1.refs_0_
  48.9 2.0 read_lists.1
  50.9 38.6 %gather_rows.1 = (bf16[49152,128]{1,0:T(8,128)(2,1)}, bf16[49152,128]{1,0:T(8,128)(2,1)}) custom-call(s32[49152]{0:T(1024)} %bitcast.27, s32[2048]{0:T(1024)} %bitcast.29, bf16[4096,1024]{1,0:T(8,128)(2,1)} %keys.1, bf16[4096,1024]{1,0:T(8,128)(2,1)} %values.1), custom_call_target="tpu_custom_call" | custom-call | bytes 126000000 | tf_op jit(solution)/shard_map/gather_rows/pallas_call | solution.py:171
  89.5 18.3 %all-gather.2.cloned.1.call-done.q_ref.refs_4_ = bf16[2048,1024]{1,0:T(8,128)(2,1)} async-done(((bf16[128,1024]{1,0:T(8,128)(2,1)}), bf16[2048,1024]{1,0:T(8,128)(2,1)}) %all-gather.2.cloned.1.call-update) | async-done | bytes 4194320 | tf_op jit(solution)/shard_map/all_gather | solution.py:1613
  107.8 24.2 %memory_forward.1.parts_ref = bf16[2048,1152]{1,0:T(8,128)(2,1)} custom-call(s32[2048]{0:T(1024)} %bitcast.30, bf16[2048,1024]{1,0:T(8,128)(2,1)} %all-gather.2.cloned.1.call-done.q_ref.refs_4_, bf16[49152,128]{1,0:T(8,128)(2,1)} %get-tuple-element.45.k_ref, bf16[49152,128]{1,0:T(8,128)(2,1)} %get-tuple-element.46.v_ref, s32[16,25,128]{2,1,0:T(8,128)} %get-tuple-element.47.id_ref), custom_call_target="tpu_custom_call" | custom-call | bytes 75000000 | tf_op jit(solution)/shard_map/memory_forward/pallas_call | solution.py:307
  132.8 68.5 %reduce_group.2 = (f32[128,1024]{1,0:T(8,128)}, f32[128,128]{1,0:T(8,128)}, f32[128,1024]{1,0:T(8,128)}, f32[128,128]{1,0:T(8,128)}) custom-call(bf16[2048,1152]{1,0:T(8,128)(2,1)} %memory_forward.1.parts_ref, f32[8,768]{1,0:T(8,128)} %fusion.1.refs_0_, s32[1,3]{1,0:T(1,128)} %refs_1_.5, bf16[128,3072]{1,0:T(8,128)(2,1)} %copy-done.1, ...), custom_call_target="tpu_custom_call" | custom-call | bytes 150000000 | tf_op jit(solution)/shard_map/reduce_group/pallas_call | solution.py:821
  201.3 1.3 add_convert_fusion.1.refs_0_
  204.0 13.1 %feed_forward.1 = (bf16[128,4096]{1,0:T(8,128)(2,1)}, bf16[128,4096]{1,0:T(8,128)(2,1)}, f32[128,1024]{1,0:T(8,128)}, f32[128,1024]{1,0:T(8,128)}) custom-call(bf16[128,1024]{1,0:T(8,128)(2,1)} %multiply_convert_fusion.mid_ref.refs_1_, bf16[128,1024]{1,0:T(8,128)(2,1)} %refs_2_.2, bf16[1024,4096]{1,0:T(8,128)(2,1)} %up_ref.1, bf16[1024,4096]{1,0:T(8,128)(2,1)} %down_ref.1), custom_call_target="tpu_custom_call" | custom-call | bytes 45000000 | tf_op jit(solution)/shard_map/feed_forward/pallas_call | solution.py:1205
  217.1 1.2 multiply_reduce_fusion
  218.3 2.4 fusion.38
  220.7 12.4 %pair_grads.1 = bf16[1024,4608]{1,0:T(8,128)(2,1)} custom-call(bf16[128,1024]{1,0:T(8,128)(2,1)} %copy-done.5, bf16[128,1024]{1,0:T(8,128)(2,1)} %multiply_convert_fusion.mid_ref.refs_1_, bf16[128,1024]{1,0:T(8,128)(2,1)} %refs_2_.2, bf16[128,1024]{1,0:T(8,128)(2,1)} %get-tuple-element.55.refs_3_, bf16[128,4096]{1,0:T(8,128)(2,1)} %get-tuple-element.53.refs_4_, ...), custom_call_target="tpu_custom_call" | custom-call | bytes 30000000 | tf_op jit(solution)/shard_map/pair_grads/pallas_call | solution.py:1314
  233.2 1.1 fusion.refs_0_
  234.3 1.6 fusion.40.mix_ref.refs_3_
  235.9 2.9 sent_gradients.1
  238.8 63.4 %gather_group.1 = (bf16[2048,1152]{1,0:T(8,128)(2,1)}, f32[128,1024]{1,0:T(8,128)}, f32[8,768]{1,0:T(8,128)}) custom-call(bf16[128,1152]{1,0:T(8,128)(2,1)} %get-tuple-element.58.x_ref, f32[8,768]{1,0:T(8,128)} %fusion.1.refs_0_, s32[1,3]{1,0:T(1,128)} %refs_1_.5, bf16[128,3072]{1,0:T(8,128)(2,1)} %copy-done.1, f32[128,1024]{1,0:T(8,128)} %fusion.40.mix_ref.refs_3_, ...), custom_call_target="tpu_custom_call" | custom-call | bytes 150000000 | tf_op jit(solution)/shard_map/gather_group/pallas_call | solution.py:661
  302.2 1.0 fusion.10
  303.4 25.6 %memory_backward.1.parts_ref = bf16[2048,1024]{1,0:T(8,128)(2,1)} custom-call(s32[2048]{0:T(1024)} %bitcast.31, bf16[2048,1024]{1,0:T(8,128)(2,1)} %all-gather.2.cloned.1.call-done.q_ref.refs_4_, bf16[2048,1152]{1,0:T(8,128)(2,1)} %get-tuple-element.59.g_ref.refs_5_, bf16[49152,128]{1,0:T(8,128)(2,1)} %get-tuple-element.45.k_ref, ...), custom_call_target="tpu_custom_call" | custom-call | bytes 75000000 | tf_op jit(solution)/shard_map/memory_backward/pallas_call | solution.py:456
  329.0 91.7 %reduce_group.3.refs_1_.refs_4_ = bf16[128,3072]{1,0:T(8,128)(2,1)} custom-call(bf16[2048,1024]{1,0:T(8,128)(2,1)} %memory_backward.1.parts_ref, f32[8,768]{1,0:T(8,128)} %fusion.refs_0_, s32[1,3]{1,0:T(1,128)} %refs_1_.5, bf16[128,3072]{1,0:T(8,128)(2,1)} %copy-done.1, f32[8]{0:T(128)} %get-tuple-element.78.refs_3_, ...), custom_call_target="tpu_custom_call" | custom-call | bytes 150000000 | tf_op jit(solution)/shard_map/reduce_group/pallas_call | solution.py:821
  421.3 54.3 %finish_grads.1 = (bf16[2,64,1536]{2,1,0:T(8,128)(2,1)}, f32[24,128]{1,0:T(8,128)}, f32[128,1024]{1,0:T(8,128)}, f32[1,1024]{1,0:T(1,128)}) custom-call(bf16[128,1024]{1,0:T(8,128)(2,1)} %copy-done.3, bf16[128,3072]{1,0:T(8,128)(2,1)} %reduce_group.3.refs_1_.refs_4_, bf16[128,1024]{1,0:T(8,128)(2,1)} %refs_2_.3, f32[1,1024]{1,0:T(1,128)} %bitcast.32, ...), custom_call_target="tpu_custom_call" | custom-call | bytes 135000000 | tf_op jit(solution)/shard_map/finish_grads/pallas_call | solution.py:1529
  475.6 4.2 join_halves.1.early_ref
  479.8 3.0 write_results.1
  482.9 1.9 copy.29
  (77 shorter events, 7.1 us)
Async XLA Ops:
  7.2 195.4 %copy-start = (bf16[1024,1024]{1,0:T(8,128)(2,1)S(1)}, bf16[1024,1024]{1,0:T(8,128)(2,1)}, u32[]{:S(2)}) copy-start(bf16[1024,1024]{1,0:T(8,128)(2,1)} %param.19) | copy-start | bytes 6291460
  7.2 100.6 %all-gather.2.cloned.1.call-start = ((), (), s32[]{:S(2)}) async-start(), calls=%async_computation.2 | async-start | bytes 4456448 | tf_op jit(solution)/shard_map/all_gather | solution.py:1613
  9.6 4.0 copy-start.3
  9.6 4.9 copy-start.9
  9.6 4.8 copy-start.10
  9.6 4.8 copy-start.11
  13.6 75.9 %copy-start.1 = (bf16[128,3072]{1,0:T(8,128)(2,1)}, bf16[128,3072]{1,0:T(8,128)(2,1)S(1)}, u32[]{:S(2)}) copy-start(bf16[128,3072]{1,0:T(8,128)(2,1)S(1)} %convolution_convert_fusion.refs_2_) | copy-start | bytes 2359300
  13.6 33.5 %copy-start.18 = (f32[8]{0:T(128)S(1)}, f32[8]{0:T(128)}, u32[]{:S(2)}) copy-start(f32[8]{0:T(128)} %param.21) | copy-start | bytes 100
  13.6 34.2 %copy-start.17 = (f32[8,32]{1,0:T(8,128)S(1)}, f32[8,32]{1,0:T(8,128)}, u32[]{:S(2)}) copy-start(f32[8,32]{1,0:T(8,128)} %param.20) | copy-start | bytes 3076
  22.2 1.1 copy-start.8
  22.8 0.6 copy-start.16
  26.2 22.7 %all-to-all-start = ((s32[16,24,128]{2,1,0:T(8,128)}), s32[16,24,128]{2,1,0:T(8,128)}, u32[]{:S(2)}, u32[]{:S(2)}) async-start(s32[16,24,128]{2,1,0:T(8,128)} %make_lists.1), calls=%async_computation | async-start | bytes 393216 | tf_op jit(solution)/shard_map/all_to_all | solution.py:1605
  32.9 442.8 %reduce-scatter.2.cloned.1.call-start = ((), (), s32[]{:S(2)}) async-start(), calls=%async_computation.3 | async-start | bytes 10027008 | tf_op jit(solution)/shard_map/reduce_scatter | solution.py:909
  33.8 98.2 %collective-permute-start.3 = (bf16[128,2048]{1,0:T(8,128)(2,1)}, bf16[128,2048]{1,0:T(8,128)(2,1)S(1)}, u32[]{:S(2)}, u32[]{:S(2)}) collective-permute-start(bf16[128,2048]{1,0:T(8,128)(2,1)} %slice.17), channel_id=1, source_target_pairs={{0,1},{1,2},{2,3},{3,4},{4,5},{5,6},{6,7},{7,8},{8,9},{9,10},{10,1... | collective-permute-start | bytes 1572872 | tf_op jit(solution)/shard_map/ppermute | solution.py:25
  36.8 95.2 %collective-permute-start.2 = (bf16[128,2048]{1,0:T(8,128)(2,1)}, bf16[128,2048]{1,0:T(8,128)(2,1)}, u32[]{:S(2)}, u32[]{:S(2)}) collective-permute-start(bf16[128,2048]{1,0:T(8,128)(2,1)} %slice.17), channel_id=1, source_target_pairs={{0,2},{1,3},{2,4},{3,5},{4,6},{5,7},{6,8},{7,9},{8,10},{9,11},{10,... | collective-permute-start | bytes 1572872 | tf_op jit(solution)/shard_map/ppermute | solution.py:25
  40.0 92.1 %collective-permute-start.1 = (bf16[128,2048]{1,0:T(8,128)(2,1)}, bf16[128,2048]{1,0:T(8,128)(2,1)}, u32[]{:S(2)}, u32[]{:S(2)}) collective-permute-start(bf16[128,2048]{1,0:T(8,128)(2,1)} %slice.17), channel_id=1, source_target_pairs={{0,3},{1,4},{2,5},{3,6},{4,7},{5,8},{6,9},{7,10},{8,11},{9,12},{10... | collective-permute-start | bytes 1572872 | tf_op jit(solution)/shard_map/ppermute | solution.py:25
  44.0 88.1 %collective-permute-start = (bf16[128,2048]{1,0:T(8,128)(2,1)}, bf16[128,2048]{1,0:T(8,128)(2,1)}, u32[]{:S(2)}, u32[]{:S(2)}) collective-permute-start(bf16[128,2048]{1,0:T(8,128)(2,1)} %slice.17), channel_id=1, source_target_pairs={{0,4},{1,5},{2,6},{3,7},{4,8},{5,9},{6,10},{7,11},{8,12},{9,13},{1... | collective-permute-start | bytes 1572872 | tf_op jit(solution)/shard_map/ppermute | solution.py:25
  47.6 41.9 %copy-start.13 = (f32[8]{0:T(128)}, f32[8]{0:T(128)S(1)}, u32[]{:S(2)}) copy-start(f32[8]{0:T(128)S(1)} %get-tuple-element.79.share_ref.refs_6_) | copy-start | bytes 100
  132.0 70.6 %copy-start.2 = (bf16[128,1024]{1,0:T(8,128)(2,1)S(1)}, bf16[128,1024]{1,0:T(8,128)(2,1)}, u32[]{:S(2)}) copy-start(bf16[128,1024]{1,0:T(8,128)(2,1)} %refs_2_.3) | copy-start | bytes 786436
  132.0 71.2 %copy-start.12 = (f32[1024]{0:T(1024)S(1)}, f32[1024]{0:T(1024)}, u32[]{:S(2)}) copy-start(f32[1024]{0:T(1024)} %param.22) | copy-start | bytes 12292
  132.0 0.8 copy-start.7
  202.6 14.5 %copy-start.5 = (bf16[128,1024]{1,0:T(8,128)(2,1)}, bf16[128,1024]{1,0:T(8,128)(2,1)S(1)}, u32[]{:S(2)}) copy-start(bf16[128,1024]{1,0:T(8,128)(2,1)S(1)} %add_convert_fusion.1.refs_0_) | copy-start | bytes 786436
  204.0 14.3 %copy-start.4 = (bf16[128,1024]{1,0:T(8,128)(2,1)S(1)}, bf16[128,1024]{1,0:T(8,128)(2,1)}, u32[]{:S(2)}) copy-start(bf16[128,1024]{1,0:T(8,128)(2,1)} %refs_2_.2) | copy-start | bytes 786436
  233.1 1.2 copy-start.6
  238.8 64.5 %copy-start.15 = (f32[8,128]{1,0:T(8,128)S(1)}, f32[8,128]{1,0:T(8,128)}, u32[]{:S(2)}) copy-start(f32[8,128]{1,0:T(8,128)} %get-tuple-element.62) | copy-start | bytes 12292
  329.0 91.7 %copy-start.14 = (f32[8]{0:T(128)S(1)}, f32[8]{0:T(128)}, u32[]{:S(2)}) copy-start(f32[8]{0:T(128)} %copy-done.13) | copy-start | bytes 100
Sparse Core Ops, SparseCore 0:
  14.5 93.3 all-gather.1
  233.3 225.2 reduce-scatter.1

commit v2 on v1

--- a/solution.py
+++ b/solution.py
@@ -1405,8 +1405,7 @@
 
 
 def write_results(late, late_widths, early, early_widths, small, heads, buckets):
-    rows, width = late.shape[1], late.shape[2] * 2 // 3
-    lines = width // 128
+    rows, lines = late.shape[1], late.shape[1] * lax.axis_size("mem") // 128
     count = len(late_widths) + len(early_widths)
 
     def kernel(late_ref, early_ref, small_ref, *outs):
@@ -1643,16 +1642,14 @@
     normed_mid = normed_mid_f.astype(jnp.bfloat16)
     activated, d_up, ffn_branch, d_mid = feed_forward(normed_mid, cotangent, up_weight, down_weight)
     block_out = (residual + ffn_branch).astype(jnp.bfloat16)
+    early_halves = pair_grads([cotangent], [activated], 5)
+    early_sums = scattered(early_halves)
+    d_mid, _ = lax.optimization_barrier((d_mid, early_halves))
     d_resid_part, ffn_gain_part = norm_mid_back(d_mid)
     d_residual = cotangent.astype(jnp.float32) + d_resid_part
     d_branch = d_residual.astype(jnp.bfloat16)
-    early_halves = pair_grads(
-        [mixed_heads, normed_mid, cotangent], [d_branch, d_up, activated], 5
-    )
-    early_sums = scattered(early_halves)
-    d_after, _ = lax.optimization_barrier((d_branch, early_halves))
     d_mixed = lax.dot_general(
-        d_after, out_weight, contract_cols, preferred_element_type=jnp.float32
+        d_branch, out_weight, contract_cols, preferred_element_type=jnp.float32
     )
     gate_products, sent_grads = sent_gradients(
         d_mixed, memory_out, local_out, mem_log, local_log, gate_share, heads
@@ -1715,22 +1712,22 @@
     beside = input_backward(tokens, attn_gain, d_projected, qkv_weight, d_residual)
     small = jnp.concatenate([ffn_gain_part, bias_part.reshape(-1), gate_part], axis=0)
     small = jnp.pad(small, (width, -small.shape[0] % 1024)).reshape(-1, 128)
-    early_widths = [width, hidden, hidden]
+    lefts, rights = [normed_in, mixed_heads, normed_mid], [d_projected, d_branch, d_up]
     if groups == 16:
         late_both, small, tokens_grad, _ = finish_grads(
-            [normed_in], [d_projected], small, groups, 4, beside
+            lefts, rights, small, groups, 4, beside
         )
         early_sums, small = lax.optimization_barrier((early_sums, small))
         early_both = join_halves(early_sums, 7)
     else:
         tokens_grad, attn_gain_part = run_alone("input_backward", beside)
-        late_halves = pair_grads([normed_in], [d_projected], 6)
+        late_halves = pair_grads(lefts, rights, 6)
         late_halves, early_sums = lax.optimization_barrier((late_halves, early_sums))
         late_both = lax.all_gather(scattered(late_halves), "dp", axis=0)
         early_both = lax.all_gather(early_sums, "dp", axis=0)
         small = lax.psum(small.at[: width // 128].set(attn_gain_part.reshape(-1, 128)), ("dp", "mem"))
     qkv_grad, out_grad, up_grad, down_grad, attn_sum, ffn_sum, bias_sum, gate_sum = write_results(
-        late_both, [3 * width], early_both, early_widths, small, heads, buckets
+        late_both, [right.shape[1] for right in rights], early_both, [hidden], small, heads, buckets
     )
     return (
         block_out,

time: 500 us -> 533 us (1.066)
  Pallas kernels: 407 us -> 457 us
  waiting for transfers between devices: 18.4 us -> 2.54 us
    pallas_call x1, Pallas kernels: 54.3 us -> 99 us  [finish_grads(): pl.pallas_call(kernel, in_specs=[vmem] * (2 * count) + specs + [vmem], ou...]
    pallas_call x2, Pallas kernels: 160 us -> 127 us  [reduce_group(): pl.pallas_call(kernel, in_specs=[vmem, *specs], out_specs=[vmem] * (len(o...]
    pallas_call x1, Pallas kernels: 63.4 us -> 91.9 us  [gather_group(): pl.pallas_call(kernel, in_specs=[pl.BlockSpec(memory_space=pl.ANY), *spec...]
    all_gather x1, waiting for transfers between devices: 18.3 us -> 2.47 us  [on_device(): lax.all_gather(projected[:, :width], 'mem', axis=0, tiled=True)]
    pallas_call x1, Pallas kernels: 38.6 us -> 54.4 us  [gather_rows(): pl.pallas_call(kernel, grid_spec=pltpu.PrefetchScalarGridSpec(num_scalar_...]
  transfers between devices with their start and end apart: 7 -> 7, of which waited for: 1 -> 1; matrix products, arithmetic and copies ran while one was open for 3% -> 4% of each run, Pallas kernels for 62% -> 69%
where the time goes in v2:
time: 533 us; the launch traced here: 526 us
  Pallas kernels  457 us (86%)
  starting transfers between devices  20 us (4%)
  other arithmetic  16.7 us (3%)
  between operations  14.9 us (3%)
  matrix products  9.31 us (2%)
    pallas_call x2, Pallas kernels, reduce_group(): pl.pallas_call(kernel, in_specs=[vmem, *specs], out_specs=[vmem] * (len(o...  127 us
    pallas_call x1, Pallas kernels, finish_grads(): pl.pallas_call(kernel, in_specs=[vmem] * (2 * count) + specs + [vmem], ou...  99 us
    pallas_call x1, Pallas kernels, gather_group(): pl.pallas_call(kernel, in_specs=[pl.BlockSpec(memory_space=pl.ANY), *spec...  91.9 us
    pallas_call x1, Pallas kernels, gather_rows(): pl.pallas_call(kernel, grid_spec=pltpu.PrefetchScalarGridSpec(num_scalar_...  54.4 us
    pallas_call x1, Pallas kernels, memory_backward(): pl.pallas_call(kernel, grid_spec=pltpu.PrefetchScalarGridSpec(num_scalar_...  25.4 us
    pallas_call x1, Pallas kernels, memory_forward(): pl.pallas_call(kernel, grid_spec=pltpu.PrefetchScalarGridSpec(num_scalar_...  24.1 us
    ppermute x4, starting transfers between devices, passed_along(): return lax.ppermute(value, axis, pairs)  13.3 us
    pallas_call x1, Pallas kernels, feed_forward(): pl.pallas_call(kernel, grid=(hidden // block,), in_specs=[whole, whole, w...  12.2 us
  transfers between devices with their start and end apart: 7, of which 1 were waited for; matrix products, arithmetic and copies ran while one was open for 4% of the time, Pallas kernels for 69%

profile of v2, /device:TPU:9, one launch (start us, length us, event | category | flops | bytes accessed | tf_op | source)
XLA Modules:
  0.0 525.5 jit_solution(17242251951057332174)
XLA Ops:
  7.2 1.2 fusion.2
  8.5 1.1 fusion.4.refs_0_
  9.6 3.9 convolution_convert_fusion.refs_2_
  14.9 7.3 %sort.7 = s32[32768]{0:T(1024)S(1)} sort(s32[32768]{0:T(1024)S(1)} %reshape.322), dimensions={0}, to_apply=%region_0.1 | sort | flops 491520 | bytes 262144 | tf_op jit(solution)/shard_map/sort | solution.py:50
  23.4 2.9 make_lists.1
  26.2 6.7 %all-to-all-start = ((s32[16,24,128]{2,1,0:T(8,128)}), s32[16,24,128]{2,1,0:T(8,128)}, u32[]{:S(2)}, u32[]{:S(2)}) async-start(s32[16,24,128]{2,1,0:T(8,128)} %make_lists.1), calls=%async_computation | async-start | bytes 393216 | tf_op jit(solution)/shard_map/all_to_all | solution.py:1604
  32.9 0.8 slice.17
  33.8 3.1 collective-permute-start.3
  36.8 3.1 collective-permute-start.2
  40.0 4.0 collective-permute-start.1
  44.0 3.1 collective-permute-start
  47.8 1.1 fusion.1.refs_0_
  48.9 2.0 read_lists.1
  50.9 54.4 %gather_rows.1 = (bf16[49152,128]{1,0:T(8,128)(2,1)}, bf16[49152,128]{1,0:T(8,128)(2,1)}) custom-call(s32[49152]{0:T(1024)} %bitcast.27, s32[2048]{0:T(1024)} %bitcast.29, bf16[4096,1024]{1,0:T(8,128)(2,1)} %keys.1, bf16[4096,1024]{1,0:T(8,128)(2,1)} %values.1), custom_call_target="tpu_custom_call" | custom-call | bytes 126000000 | tf_op jit(solution)/shard_map/gather_rows/pallas_call | solution.py:171
  105.4 2.5 all-gather.2.cloned.1.call-done.q_ref.refs_4_
  107.8 24.1 %memory_forward.1.parts_ref = bf16[2048,1152]{1,0:T(8,128)(2,1)} custom-call(s32[2048]{0:T(1024)} %bitcast.30, bf16[2048,1024]{1,0:T(8,128)(2,1)} %all-gather.2.cloned.1.call-done.q_ref.refs_4_, bf16[49152,128]{1,0:T(8,128)(2,1)} %get-tuple-element.45.k_ref, bf16[49152,128]{1,0:T(8,128)(2,1)} %get-tuple-element.46.v_ref, s32[16,25,128]{2,1,0:T(8,128)} %get-tuple-element.47.id_ref), custom_call_target="tpu_custom_call" | custom-call | bytes 75000000 | tf_op jit(solution)/shard_map/memory_forward/pallas_call | solution.py:307
  132.8 68.4 %reduce_group.2 = (f32[128,1024]{1,0:T(8,128)}, f32[128,128]{1,0:T(8,128)}, f32[128,1024]{1,0:T(8,128)}, f32[128,128]{1,0:T(8,128)}) custom-call(bf16[2048,1152]{1,0:T(8,128)(2,1)} %memory_forward.1.parts_ref, f32[8,768]{1,0:T(8,128)} %fusion.1.refs_0_, s32[1,3]{1,0:T(1,128)} %refs_1_.5, bf16[128,3072]{1,0:T(8,128)(2,1)} %copy-done.1, ...), custom_call_target="tpu_custom_call" | custom-call | bytes 150000000 | tf_op jit(solution)/shard_map/reduce_group/pallas_call | solution.py:821
  201.2 1.3 add_convert_fusion.1.refs_1_
  203.9 12.2 %feed_forward.1 = (bf16[128,4096]{1,0:T(8,128)(2,1)}, bf16[128,4096]{1,0:T(8,128)(2,1)}, f32[128,1024]{1,0:T(8,128)}, f32[128,1024]{1,0:T(8,128)}) custom-call(bf16[128,1024]{1,0:T(8,128)(2,1)} %multiply_convert_fusion.mid_ref.refs_2_, bf16[128,1024]{1,0:T(8,128)(2,1)} %refs_0_.1, bf16[1024,4096]{1,0:T(8,128)(2,1)} %up_ref.1, bf16[1024,4096]{1,0:T(8,128)(2,1)} %down_ref.1), custom_call_target="tpu_custom_call" | custom-call | bytes 45000000 | tf_op jit(solution)/shard_map/feed_forward/pallas_call | solution.py:1205
  216.2 8.3 %pair_grads.1 = bf16[1024,2048]{1,0:T(8,128)(2,1)} custom-call(bf16[128,1024]{1,0:T(8,128)(2,1)} %refs_0_.1, bf16[128,4096]{1,0:T(8,128)(2,1)} %get-tuple-element.53.refs_1_), custom_call_target="tpu_custom_call" | custom-call | bytes 30000000 | tf_op jit(solution)/shard_map/pair_grads/pallas_call | solution.py:1314
  224.6 1.1 fusion.refs_0_
  225.9 2.1 fusion.38
  228.0 1.6 fusion.40.mix_ref.refs_3_
  229.6 2.9 sent_gradients.1
  232.5 91.9 %gather_group.1 = (bf16[2048,1152]{1,0:T(8,128)(2,1)}, f32[128,1024]{1,0:T(8,128)}, f32[8,768]{1,0:T(8,128)}) custom-call(bf16[128,1152]{1,0:T(8,128)(2,1)} %get-tuple-element.57.x_ref, f32[8,768]{1,0:T(8,128)} %fusion.1.refs_0_, s32[1,3]{1,0:T(1,128)} %refs_1_.5, bf16[128,3072]{1,0:T(8,128)(2,1)} %copy-done.1, f32[128,1024]{1,0:T(8,128)} %fusion.40.mix_ref.refs_3_, ...), custom_call_target="tpu_custom_call" | custom-call | bytes 150000000 | tf_op jit(solution)/shard_map/gather_group/pallas_call | solution.py:661
  324.5 1.0 fusion.10
  325.7 25.4 %memory_backward.1.parts_ref = bf16[2048,1024]{1,0:T(8,128)(2,1)} custom-call(s32[2048]{0:T(1024)} %bitcast.31, bf16[2048,1024]{1,0:T(8,128)(2,1)} %all-gather.2.cloned.1.call-done.q_ref.refs_4_, bf16[2048,1152]{1,0:T(8,128)(2,1)} %get-tuple-element.58.g_ref.refs_5_, bf16[49152,128]{1,0:T(8,128)(2,1)} %get-tuple-element.45.k_ref, ...), custom_call_target="tpu_custom_call" | custom-call | bytes 75000000 | tf_op jit(solution)/shard_map/memory_backward/pallas_call | solution.py:456
  351.2 59.1 %reduce_group.3.refs_3_.refs_8_ = bf16[128,3072]{1,0:T(8,128)(2,1)} custom-call(bf16[2048,1024]{1,0:T(8,128)(2,1)} %memory_backward.1.parts_ref, f32[8,768]{1,0:T(8,128)} %fusion.refs_0_, s32[1,3]{1,0:T(1,128)} %refs_1_.5, bf16[128,3072]{1,0:T(8,128)(2,1)} %copy-done.1, f32[8]{0:T(128)} %get-tuple-element.78.refs_3_, ...), custom_call_target="tpu_custom_call" | custom-call | bytes 150000000 | tf_op jit(solution)/shard_map/reduce_group/pallas_call | solution.py:821
  410.9 99.0 %finish_grads.1 = (bf16[2,64,4096]{2,1,0:T(8,128)(2,1)}, f32[24,128]{1,0:T(8,128)}, f32[128,1024]{1,0:T(8,128)}, f32[1,1024]{1,0:T(1,128)}) custom-call(bf16[128,1024]{1,0:T(8,128)(2,1)} %copy-done.3, bf16[128,1024]{1,0:T(8,128)(2,1)} %copy-done.5, bf16[128,1024]{1,0:T(8,128)(2,1)} %multiply_convert_fusion.mid_ref.refs_2_, ...), custom_call_target="tpu_custom_call" | custom-call | bytes 135000000 | tf_op jit(solution)/shard_map/finish_grads/pallas_call | solution.py:1528
  509.9 3.3 join_halves.1.early_ref
  513.3 3.1 write_results.1
  516.4 1.9 copy.29
  (79 shorter events, 6.5 us)
Async XLA Ops:
  7.2 195.4 %copy-start = (bf16[1024,1024]{1,0:T(8,128)(2,1)S(1)}, bf16[1024,1024]{1,0:T(8,128)(2,1)}, u32[]{:S(2)}) copy-start(bf16[1024,1024]{1,0:T(8,128)(2,1)} %param.19) | copy-start | bytes 6291460
  7.2 100.6 %all-gather.2.cloned.1.call-start = ((), (), s32[]{:S(2)}) async-start(), calls=%async_computation.2 | async-start | bytes 4456448 | tf_op jit(solution)/shard_map/all_gather | solution.py:1612
  9.6 4.0 copy-start.3
  9.6 4.9 copy-start.10
  9.6 4.8 copy-start.11
  9.6 4.8 copy-start.12
  13.6 91.8 %copy-start.1 = (bf16[128,3072]{1,0:T(8,128)(2,1)}, bf16[128,3072]{1,0:T(8,128)(2,1)S(1)}, u32[]{:S(2)}) copy-start(bf16[128,3072]{1,0:T(8,128)(2,1)S(1)} %convolution_convert_fusion.refs_2_) | copy-start | bytes 2359300
  13.6 33.5 %copy-start.19 = (f32[8]{0:T(128)S(1)}, f32[8]{0:T(128)}, u32[]{:S(2)}) copy-start(f32[8]{0:T(128)} %param.21) | copy-start | bytes 100
  13.6 34.2 %copy-start.18 = (f32[8,32]{1,0:T(8,128)S(1)}, f32[8,32]{1,0:T(8,128)}, u32[]{:S(2)}) copy-start(f32[8,32]{1,0:T(8,128)} %param.20) | copy-start | bytes 3076
  22.2 1.1 copy-start.9
  22.8 0.6 copy-start.17
  26.2 22.7 %all-to-all-start = ((s32[16,24,128]{2,1,0:T(8,128)}), s32[16,24,128]{2,1,0:T(8,128)}, u32[]{:S(2)}, u32[]{:S(2)}) async-start(s32[16,24,128]{2,1,0:T(8,128)} %make_lists.1), calls=%async_computation | async-start | bytes 393216 | tf_op jit(solution)/shard_map/all_to_all | solution.py:1604
  32.9 477.0 %reduce-scatter.2.cloned.1.call-start = ((), (), s32[]{:S(2)}) async-start(), calls=%async_computation.3 | async-start | bytes 4456448 | tf_op jit(solution)/shard_map/reduce_scatter | solution.py:909
  33.8 98.2 %collective-permute-start.3 = (bf16[128,2048]{1,0:T(8,128)(2,1)}, bf16[128,2048]{1,0:T(8,128)(2,1)S(1)}, u32[]{:S(2)}, u32[]{:S(2)}) collective-permute-start(bf16[128,2048]{1,0:T(8,128)(2,1)} %slice.17), channel_id=1, source_target_pairs={{0,1},{1,2},{2,3},{3,4},{4,5},{5,6},{6,7},{7,8},{8,9},{9,10},{10,1... | collective-permute-start | bytes 1572872 | tf_op jit(solution)/shard_map/ppermute | solution.py:25
  36.8 95.1 %collective-permute-start.2 = (bf16[128,2048]{1,0:T(8,128)(2,1)}, bf16[128,2048]{1,0:T(8,128)(2,1)}, u32[]{:S(2)}, u32[]{:S(2)}) collective-permute-start(bf16[128,2048]{1,0:T(8,128)(2,1)} %slice.17), channel_id=1, source_target_pairs={{0,2},{1,3},{2,4},{3,5},{4,6},{5,7},{6,8},{7,9},{8,10},{9,11},{10,... | collective-permute-start | bytes 1572872 | tf_op jit(solution)/shard_map/ppermute | solution.py:25
  40.0 92.1 %collective-permute-start.1 = (bf16[128,2048]{1,0:T(8,128)(2,1)}, bf16[128,2048]{1,0:T(8,128)(2,1)}, u32[]{:S(2)}, u32[]{:S(2)}) collective-permute-start(bf16[128,2048]{1,0:T(8,128)(2,1)} %slice.17), channel_id=1, source_target_pairs={{0,3},{1,4},{2,5},{3,6},{4,7},{5,8},{6,9},{7,10},{8,11},{9,12},{10... | collective-permute-start | bytes 1572872 | tf_op jit(solution)/shard_map/ppermute | solution.py:25
  44.0 88.1 %collective-permute-start = (bf16[128,2048]{1,0:T(8,128)(2,1)}, bf16[128,2048]{1,0:T(8,128)(2,1)}, u32[]{:S(2)}, u32[]{:S(2)}) collective-permute-start(bf16[128,2048]{1,0:T(8,128)(2,1)} %slice.17), channel_id=1, source_target_pairs={{0,4},{1,5},{2,6},{3,7},{4,8},{5,9},{6,10},{7,11},{8,12},{9,13},{1... | collective-permute-start | bytes 1572872 | tf_op jit(solution)/shard_map/ppermute | solution.py:25
  47.6 57.8 %copy-start.14 = (f32[8]{0:T(128)}, f32[8]{0:T(128)S(1)}, u32[]{:S(2)}) copy-start(f32[8]{0:T(128)S(1)} %get-tuple-element.79.share_ref.refs_6_) | copy-start | bytes 100
  132.0 70.6 %copy-start.2 = (bf16[128,1024]{1,0:T(8,128)(2,1)S(1)}, bf16[128,1024]{1,0:T(8,128)(2,1)}, u32[]{:S(2)}) copy-start(bf16[128,1024]{1,0:T(8,128)(2,1)} %refs_6_.1) | copy-start | bytes 786436
  132.0 71.1 %copy-start.13 = (f32[1024]{0:T(1024)S(1)}, f32[1024]{0:T(1024)}, u32[]{:S(2)}) copy-start(f32[1024]{0:T(1024)} %param.22) | copy-start | bytes 12292
  132.0 0.8 copy-start.7
  202.6 13.6 %copy-start.5 = (bf16[128,1024]{1,0:T(8,128)(2,1)}, bf16[128,1024]{1,0:T(8,128)(2,1)S(1)}, u32[]{:S(2)}) copy-start(bf16[128,1024]{1,0:T(8,128)(2,1)S(1)} %add_convert_fusion.1.refs_1_) | copy-start | bytes 786436
  216.2 9.5 %copy-start.8 = (f32[128,1024]{1,0:T(8,128)S(1)}, f32[128,1024]{1,0:T(8,128)}, u32[]{:S(2)}) copy-start(f32[128,1024]{1,0:T(8,128)} %get-tuple-element.54) | copy-start | bytes 1572868
  216.2 9.7 %copy-start.4 = (bf16[128,1024]{1,0:T(8,128)(2,1)S(1)}, bf16[128,1024]{1,0:T(8,128)(2,1)}, u32[]{:S(2)}) copy-start(bf16[128,1024]{1,0:T(8,128)(2,1)} %refs_0_.1) | copy-start | bytes 786436
  228.0 96.5 %copy-start.6 = (bf16[128,1024]{1,0:T(8,128)(2,1)}, bf16[128,1024]{1,0:T(8,128)(2,1)S(1)}, u32[]{:S(2)}) copy-start(bf16[128,1024]{1,0:T(8,128)(2,1)S(1)} %get-tuple-element.80.refs_4_) | copy-start | bytes 786436
  232.5 93.0 %copy-start.16 = (f32[8,128]{1,0:T(8,128)S(1)}, f32[8,128]{1,0:T(8,128)}, u32[]{:S(2)}) copy-start(f32[8,128]{1,0:T(8,128)} %get-tuple-element.62) | copy-start | bytes 12292
  351.2 59.1 %copy-start.15 = (f32[8]{0:T(128)S(1)}, f32[8]{0:T(128)}, u32[]{:S(2)}) copy-start(f32[8]{0:T(128)} %copy-done.14) | copy-start | bytes 100
Sparse Core Ops, SparseCore 0:
  14.5 93.3 all-gather.1
  224.6 132.5 reduce-scatter.1

commit v3 on v1

--- a/solution.py
+++ b/solution.py
@@ -996,42 +996,6 @@
         jax.ShapeDtypeStruct((rows, 128), jnp.float32),
     ]
     return arrays, specs, out_shape, [], begin
-
-
-def sent_gradients(d_mixed, memory_out, local_out, mem_log, local_log, share, heads):
-    rows, width = d_mixed.shape
-    head_dim = width // heads
-
-    def kernel(mix_ref, mem_ref, loc_ref, mem_log_ref, log_ref, share_ref, gate_ref, sent_ref):
-        mem_deltas, deltas = [], []
-        for head in range(heads):
-            columns = slice(head * head_dim, (head + 1) * head_dim)
-            share_here = share_ref[head]
-            d_mix, mem_here, loc_here = mix_ref[:, columns], mem_ref[:, columns], loc_ref[:, columns]
-            d_mem = (share_here * d_mix).astype(jnp.bfloat16)
-            d_out = ((1.0 - share_here) * d_mix).astype(jnp.bfloat16)
-            sent_ref[:, columns] = d_mem
-            mem_deltas.append(jnp.sum(d_mem.astype(jnp.float32) * mem_here, axis=1, keepdims=True))
-            deltas.append(jnp.sum(d_out.astype(jnp.float32) * loc_here, axis=1, keepdims=True))
-            gate_ref[head : head + 1, :] = jnp.sum(
-                d_mix * (mem_here - loc_here), axis=0, keepdims=True
-            )
-        mem_logs = [mem_log_ref[:, head : head + 1] for head in range(heads)]
-        logs = [log_ref[:, head : head + 1] for head in range(heads)]
-        sent_ref[:, width:] = split_tile(lane_tile(mem_logs + mem_deltas + logs + deltas, rows))
-
-    vmem = pl.BlockSpec(memory_space=pltpu.VMEM)
-    return pl.pallas_call(
-        kernel,
-        in_specs=[vmem] * 5 + [pl.BlockSpec(memory_space=pltpu.SMEM)],
-        out_shape=[
-            jax.ShapeDtypeStruct((heads, head_dim), jnp.float32),
-            jax.ShapeDtypeStruct((rows, width + 128), jnp.bfloat16),
-        ],
-        compiler_params=pltpu.CompilerParams(vmem_limit_bytes=VMEM_LIMIT),
-        cost_estimate=lasting(3),
-        name="sent_gradients",
-    )(d_mixed, memory_out, local_out, mem_log, local_log, share)
 
 
 def local_queries(
@@ -1179,13 +1143,52 @@
     return arrays, specs, [jax.ShapeDtypeStruct((rows, 3 * width), jnp.bfloat16)], scratch, begin
 
 
-def feed_forward(normed_mid, cotangent, up_weight, down_weight):
-    rows, width = normed_mid.shape
+def middle(
+    tokens,
+    memory_out,
+    local_out,
+    mem_log,
+    local_log,
+    share,
+    out_weight,
+    ffn_gain,
+    up_weight,
+    down_weight,
+    cotangent,
+    heads,
+):
+    rows, width = tokens.shape
+    head_dim = width // heads
     hidden = up_weight.shape[1]
     block = math.gcd(hidden, 1024)
-
-    def kernel(mid_ref, cot_ref, up_ref, down_ref, act_ref, d_up_ref, branch_ref, d_mid_ref):
-        first = pl.program_id(0) == 0
+    steps = hidden // block
+
+    def kernel(
+        tokens_ref, mem_ref, loc_ref, mem_log_ref, log_ref, share_ref, out_w_ref, gain_ref, up_ref, down_ref, cot_ref, *refs
+    ):
+        mixed_ref, mid_ref, act_ref, d_up_ref, block_ref, d_res_ref, gain_part_ref, d_branch_ref, d_mix_ref = refs[:9]
+        gate_ref, sent_ref, residual, branch_sum, d_mid_sum = refs[9:]
+        i = pl.program_id(0)
+
+        def scale_of(values):
+            return lax.rsqrt(jnp.mean(values * values, axis=1, keepdims=True) + eps_norm)
+
+        @pl.when(i == 0)
+        def _():
+            for head in range(heads):
+                columns = slice(head * head_dim, (head + 1) * head_dim)
+                part = share_ref[head]
+                mixed_ref[:, columns] = (
+                    part * mem_ref[:, columns] + (1.0 - part) * loc_ref[:, columns]
+                ).astype(jnp.bfloat16)
+            values = tokens_ref[...].astype(jnp.float32) + jnp.dot(
+                mixed_ref[...], out_w_ref[...], preferred_element_type=jnp.float32
+            )
+            residual[...] = values
+            mid_ref[...] = (values * scale_of(values) * gain_ref[...]).astype(jnp.bfloat16)
+            branch_sum[...] = jnp.zeros_like(branch_sum)
+            d_mid_sum[...] = jnp.zeros_like(d_mid_sum)
+
         up = jnp.dot(mid_ref[...], up_ref[...], preferred_element_type=jnp.float32)
         d_act = jnp.dot(cot_ref[...], down_ref[...], preferred_element_type=jnp.float32)
         below = 0.5 * (1.0 + lax.erf(up * math.sqrt(0.5)))
@@ -1194,29 +1197,91 @@
         d_up = (d_act * (below + up * density)).astype(jnp.bfloat16)
         act_ref[...] = act
         d_up_ref[...] = d_up
-        branch = lax.dot_general(act, down_ref[...], contract_cols, preferred_element_type=jnp.float32)
-        d_mid = lax.dot_general(d_up, up_ref[...], contract_cols, preferred_element_type=jnp.float32)
-        branch_ref[...] = jnp.where(first, branch, branch_ref[...] + branch)
-        d_mid_ref[...] = jnp.where(first, d_mid, d_mid_ref[...] + d_mid)
-
-    whole = pl.BlockSpec((rows, width), lambda i: (0, 0))
+        branch_sum[...] += lax.dot_general(
+            act, down_ref[...], contract_cols, preferred_element_type=jnp.float32
+        )
+        d_mid_sum[...] += lax.dot_general(
+            d_up, up_ref[...], contract_cols, preferred_element_type=jnp.float32
+        )
+
+        @pl.when(i == steps - 1)
+        def _():
+            values, d_mid = residual[...], d_mid_sum[...]
+            block_ref[...] = (values + branch_sum[...]).astype(jnp.bfloat16)
+            scale = scale_of(values)
+            wanted = d_mid * gain_ref[...]
+            slope = jnp.mean(values * wanted, axis=1, keepdims=True) * scale * scale * scale
+            d_res = cot_ref[...].astype(jnp.float32) + scale * wanted - values * slope
+            d_res_ref[...] = d_res
+            gain_part_ref[...] = jnp.sum(d_mid * values * scale, axis=0, keepdims=True)
+            d_branch_ref[...] = d_res.astype(jnp.bfloat16)
+            d_mix_ref[...] = lax.dot_general(
+                d_branch_ref[...], out_w_ref[...], contract_cols, preferred_element_type=jnp.float32
+            )
+            mem_deltas, deltas = [], []
+            for head in range(heads):
+                columns = slice(head * head_dim, (head + 1) * head_dim)
+                part = share_ref[head]
+                d_mix, mem_here, loc_here = d_mix_ref[:, columns], mem_ref[:, columns], loc_ref[:, columns]
+                d_mem = (part * d_mix).astype(jnp.bfloat16)
+                d_out = ((1.0 - part) * d_mix).astype(jnp.bfloat16)
+                sent_ref[:, columns] = d_mem
+                mem_deltas.append(
+                    jnp.sum(d_mem.astype(jnp.float32) * mem_here, axis=1, keepdims=True)
+                )
+                deltas.append(jnp.sum(d_out.astype(jnp.float32) * loc_here, axis=1, keepdims=True))
+                gate_ref[head : head + 1, :] = jnp.sum(
+                    d_mix * (mem_here - loc_here), axis=0, keepdims=True
+                )
+            mem_logs = [mem_log_ref[:, head : head + 1] for head in range(heads)]
+            logs = [log_ref[:, head : head + 1] for head in range(heads)]
+            sent_ref[:, width:] = split_tile(lane_tile(mem_logs + mem_deltas + logs + deltas, rows))
+
+    def whole(*shape):
+        return pl.BlockSpec(shape, lambda i: (0, 0))
+
     weight = pl.BlockSpec((width, block), lambda i: (0, i))
-    middle = pl.BlockSpec((rows, block), lambda i: (0, i))
+    column = pl.BlockSpec((rows, block), lambda i: (0, i))
+    full = whole(rows, width)
+    low, high = jnp.bfloat16, jnp.float32
+    outs = [
+        (full, (rows, width), low),
+        (full, (rows, width), low),
+        (column, (rows, hidden), low),
+        (column, (rows, hidden), low),
+        (full, (rows, width), low),
+        (full, (rows, width), high),
+        (whole(1, width), (1, width), high),
+        (full, (rows, width), low),
+        (full, (rows, width), high),
+        (whole(heads, head_dim), (heads, head_dim), high),
+        (whole(rows, width + 128), (rows, width + 128), low),
+    ]
     return pl.pallas_call(
         kernel,
-        grid=(hidden // block,),
-        in_specs=[whole, whole, weight, weight],
-        out_specs=[middle, middle, whole, whole],
-        out_shape=[
-            jax.ShapeDtypeStruct((rows, hidden), jnp.bfloat16),
-            jax.ShapeDtypeStruct((rows, hidden), jnp.bfloat16),
-            jax.ShapeDtypeStruct((rows, width), jnp.float32),
-            jax.ShapeDtypeStruct((rows, width), jnp.float32),
-        ],
+        grid=(steps,),
+        in_specs=[full, full, full, whole(rows, 128), whole(rows, 128)]
+        + [pl.BlockSpec(memory_space=pltpu.SMEM)]
+        + [whole(width, width), whole(1, width), weight, weight, full],
+        out_specs=[spec for spec, _, _ in outs],
+        out_shape=[jax.ShapeDtypeStruct(shape, dtype) for _, shape, dtype in outs],
+        scratch_shapes=[pltpu.VMEM((rows, width), jnp.float32)] * 3,
         compiler_params=pltpu.CompilerParams(vmem_limit_bytes=VMEM_LIMIT),
-        cost_estimate=lasting(15),
-        name="feed_forward",
-    )(normed_mid, cotangent, up_weight, down_weight)
+        cost_estimate=lasting(18),
+        name="middle",
+    )(
+        tokens,
+        memory_out,
+        local_out,
+        mem_log,
+        local_log,
+        share,
+        out_weight,
+        ffn_gain[None, :],
+        up_weight,
+        down_weight,
+        cotangent,
+    )
 
 
 def exchange_pairs(lefts, rights, other_lefts, other_right, send, recv):
@@ -1636,27 +1701,38 @@
         ).reshape(groups * rows, width + 128)
         memory_out, mem_log = combine_partials(partial, heads, groups, rows)
     gate_share = jax.nn.sigmoid(gate_logit)
-    share_wide = jnp.repeat(gate_share, head_dim)[None, :]
-    mixed_heads = (share_wide * memory_out + (1.0 - share_wide) * local_out).astype(jnp.bfloat16)
-    residual = tokens_f + jnp.dot(mixed_heads, out_weight, preferred_element_type=jnp.float32)
-    normed_mid_f, norm_mid_back = jax.vjp(normed, residual, ffn_gain)
-    normed_mid = normed_mid_f.astype(jnp.bfloat16)
-    activated, d_up, ffn_branch, d_mid = feed_forward(normed_mid, cotangent, up_weight, down_weight)
-    block_out = (residual + ffn_branch).astype(jnp.bfloat16)
-    d_resid_part, ffn_gain_part = norm_mid_back(d_mid)
-    d_residual = cotangent.astype(jnp.float32) + d_resid_part
-    d_branch = d_residual.astype(jnp.bfloat16)
+    (
+        mixed_heads,
+        normed_mid,
+        activated,
+        d_up,
+        block_out,
+        d_residual,
+        ffn_gain_part,
+        d_branch,
+        d_mixed,
+        gate_products,
+        sent_grads,
+    ) = middle(
+        tokens,
+        memory_out,
+        local_out,
+        mem_log,
+        local_log,
+        gate_share,
+        out_weight,
+        ffn_gain,
+        up_weight,
+        down_weight,
+        cotangent,
+        heads,
+    )
+    ffn_gain_part = ffn_gain_part.reshape(-1)
     early_halves = pair_grads(
         [mixed_heads, normed_mid, cotangent], [d_branch, d_up, activated], 5
     )
     early_sums = scattered(early_halves)
-    d_after, _ = lax.optimization_barrier((d_branch, early_halves))
-    d_mixed = lax.dot_general(
-        d_after, out_weight, contract_cols, preferred_element_type=jnp.float32
-    )
-    gate_products, sent_grads = sent_gradients(
-        d_mixed, memory_out, local_out, mem_log, local_log, gate_share, heads
-    )
+    sent_grads, _ = lax.optimization_barrier((sent_grads, early_halves))
     gate_part = jnp.sum(gate_products, axis=1) * gate_share * (1.0 - gate_share)
     local = local_queries(
         before_bias,

time: 500 us -> 486 us (0.972)
  waiting for transfers between devices: 18.4 us -> 2.16 us
  Pallas kernels: 407 us -> 416 us
  other arithmetic: 17.9 us -> 12.1 us
    pallas_call x2, Pallas kernels: 160 us -> 141 us  [reduce_group(): pl.pallas_call(kernel, in_specs=[vmem, *specs], out_specs=[vmem] * (len(o...]
    pallas_call x1, Pallas kernels: 54.3 us -> 70.9 us  [finish_grads(): pl.pallas_call(kernel, in_specs=[vmem] * (2 * count) + specs + [vmem], ou...]
    all_gather x1, waiting for transfers between devices: 18.3 us -> 2.09 us  [on_device(): lax.all_gather(projected[:, :width], 'mem', axis=0, tiled=True)]
    pallas_call x1, Pallas kernels: 38.6 us -> 54.1 us  [gather_rows(): pl.pallas_call(kernel, grid_spec=pltpu.PrefetchScalarGridSpec(num_scalar_...]
    pallas_call x2 -> x1, Pallas kernels: 16 us -> 16.1 us  [middle(): pl.pallas_call(kernel, grid=(steps,), in_specs=[full, full, full, whole(r...]
  transfers between devices with their start and end apart: 7 -> 7, of which waited for: 1 -> 1; matrix products, arithmetic and copies ran while one was open for 3% -> 3% of each run, Pallas kernels for 62% -> 65%
where the time goes in v3:
time: 486 us; the launch traced here: 479 us
  Pallas kernels  416 us (86%)
  starting transfers between devices  20.2 us (4%)
  between operations  14.8 us (3%)
  other arithmetic  12.1 us (2%)
  matrix products  7.16 us (1%)
  local copies, waits for them, and re-layouts  6.6 us (1%)
    pallas_call x2, Pallas kernels, reduce_group(): pl.pallas_call(kernel, in_specs=[vmem, *specs], out_specs=[vmem] * (len(o...  141 us
    pallas_call x1, Pallas kernels, finish_grads(): pl.pallas_call(kernel, in_specs=[vmem] * (2 * count) + specs + [vmem], ou...  70.9 us
    pallas_call x1, Pallas kernels, gather_group(): pl.pallas_call(kernel, in_specs=[pl.BlockSpec(memory_space=pl.ANY), *spec...  59.4 us
    pallas_call x1, Pallas kernels, gather_rows(): pl.pallas_call(kernel, grid_spec=pltpu.PrefetchScalarGridSpec(num_scalar_...  54.1 us
    pallas_call x1, Pallas kernels, memory_backward(): pl.pallas_call(kernel, grid_spec=pltpu.PrefetchScalarGridSpec(num_scalar_...  25.6 us
    pallas_call x1, Pallas kernels, memory_forward(): pl.pallas_call(kernel, grid_spec=pltpu.PrefetchScalarGridSpec(num_scalar_...  24.2 us
    pallas_call x1, Pallas kernels, middle(): pl.pallas_call(kernel, grid=(steps,), in_specs=[full, full, full, whole(r...  16.1 us
    ppermute x4, starting transfers between devices, passed_along(): return lax.ppermute(value, axis, pairs)  13.4 us
  transfers between devices with their start and end apart: 7, of which 1 were waited for; matrix products, arithmetic and copies ran while one was open for 3% of the time, Pallas kernels for 65%

profile of v3, /device:TPU:9, one launch (start us, length us, event | category | flops | bytes accessed | tf_op | source)
XLA Modules:
  0.0 479.0 jit_solution(3665822219932574826)
XLA Ops:
  7.2 1.1 fusion.2
  8.3 1.1 fusion.4.refs_0_
  9.5 4.0 convolution_convert_fusion.refs_2_
  13.5 0.8 slice.16
  14.8 7.3 %sort.7 = s32[32768]{0:T(1024)S(1)} sort(s32[32768]{0:T(1024)S(1)} %reshape.297), dimensions={0}, to_apply=%region_0.1 | sort | flops 491520 | bytes 262144 | tf_op jit(solution)/shard_map/sort | solution.py:50
  23.3 2.9 make_lists.1
  26.1 6.7 %all-to-all-start = ((s32[16,24,128]{2,1,0:T(8,128)}), s32[16,24,128]{2,1,0:T(8,128)S(1)}, u32[]{:S(2)}, u32[]{:S(2)}) async-start(s32[16,24,128]{2,1,0:T(8,128)} %make_lists.1), calls=%async_computation | async-start | bytes 393216 | tf_op jit(solution)/shard_map/all_to_all | solution.py:1670
  32.9 0.8 slice.17
  33.7 3.1 collective-permute-start.3
  36.8 3.1 collective-permute-start.2
  39.9 4.0 collective-permute-start.1
  43.9 3.3 collective-permute-start
  47.7 1.1 fusion.1.refs_0_
  48.8 0.7 copy-done.8
  49.5 2.0 read_lists.1
  51.5 54.1 %gather_rows.1 = (bf16[49152,128]{1,0:T(8,128)(2,1)}, bf16[49152,128]{1,0:T(8,128)(2,1)}) custom-call(s32[49152]{0:T(1024)} %bitcast.22, s32[2048]{0:T(1024)} %bitcast.24, bf16[4096,1024]{1,0:T(8,128)(2,1)} %keys.1, bf16[4096,1024]{1,0:T(8,128)(2,1)} %values.1), custom_call_target="tpu_custom_call" | custom-call | bytes 126000000 | tf_op jit(solution)/shard_map/gather_rows/pallas_call | solution.py:171
  105.6 2.1 all-gather.2.cloned.1.call-done.q_ref.refs_4_
  107.7 24.2 %memory_forward.1.parts_ref = bf16[2048,1152]{1,0:T(8,128)(2,1)} custom-call(s32[2048]{0:T(1024)} %bitcast.25, bf16[2048,1024]{1,0:T(8,128)(2,1)} %all-gather.2.cloned.1.call-done.q_ref.refs_4_, bf16[49152,128]{1,0:T(8,128)(2,1)} %get-tuple-element.50.k_ref, bf16[49152,128]{1,0:T(8,128)(2,1)} %get-tuple-element.51.v_ref, s32[16,25,128]{2,1,0:T(8,128)} %get-tuple-element.52.id_ref), custom_call_target="tpu_custom_call" | custom-call | bytes 75000000 | tf_op jit(solution)/shard_map/memory_forward/pallas_call | solution.py:307
  132.0 0.7 copy-done.3
  133.1 0.8 copy-done.6
  133.9 68.5 %reduce_group.2 = (f32[128,1024]{1,0:T(8,128)}, f32[128,128]{1,0:T(8,128)}, f32[128,1024]{1,0:T(8,128)}, f32[128,128]{1,0:T(8,128)}) custom-call(bf16[2048,1152]{1,0:T(8,128)(2,1)} %memory_forward.1.parts_ref, f32[8,768]{1,0:T(8,128)} %fusion.1.refs_0_, s32[1,3]{1,0:T(1,128)} %refs_1_.5, bf16[128,3072]{1,0:T(8,128)(2,1)} %copy-done.1, ...), custom_call_target="tpu_custom_call" | custom-call | bytes 150000000 | tf_op jit(solution)/shard_map/reduce_group/pallas_call | solution.py:821
  202.4 16.1 %middle.1 = (bf16[128,1024]{1,0:T(8,128)(2,1)}, bf16[128,1024]{1,0:T(8,128)(2,1)}, bf16[128,4096]{1,0:T(8,128)(2,1)}, bf16[128,4096]{1,0:T(8,128)(2,1)}, bf16[12...) custom-call(bf16[128,1024]{1,0:T(8,128)(2,1)} %refs_2_.3, ...), custom_call_target="tpu_custom_call" | custom-call | bytes 54000000 | tf_op jit(solution)/shard_map/middle/pallas_call | solution.py:1260
  218.4 12.5 %pair_grads.1 = bf16[1024,4608]{1,0:T(8,128)(2,1)} custom-call(bf16[128,1024]{1,0:T(8,128)(2,1)} %get-tuple-element.60.refs_0_, bf16[128,1024]{1,0:T(8,128)(2,1)} %get-tuple-element.61.refs_1_, bf16[128,1024]{1,0:T(8,128)(2,1)} %refs_2_.2, bf16[128,1024]{1,0:T(8,128)(2,1)} %get-tuple-element.62.refs_3_, bf16[128,4096]{1,0:T(8,128)(2,1)} %get-tuple-element.63.refs_4_, ...), custom_call_target="tpu_custom_call" | custom-call | bytes 30000000 | tf_op jit(solution)/shard_map/pair_grads/pallas_call | solution.py:1379
  231.1 1.1 fusion.refs_0_
  232.2 59.4 %gather_group.1 = (bf16[2048,1152]{1,0:T(8,128)(2,1)}, f32[128,1024]{1,0:T(8,128)}, f32[8,768]{1,0:T(8,128)}) custom-call(bf16[128,1152]{1,0:T(8,128)(2,1)} %get-tuple-element.65.x_ref, f32[8,768]{1,0:T(8,128)} %fusion.1.refs_0_, s32[1,3]{1,0:T(1,128)} %refs_1_.5, bf16[128,3072]{1,0:T(8,128)(2,1)} %copy-done.1, f32[128,1024]{1,0:T(8,128)} %get-tuple-element.66.refs_3_, ...), custom_call_target="tpu_custom_call" | custom-call | bytes 150000000 | tf_op jit(solution)/shard_map/gather_group/pallas_call | solution.py:661
  291.6 1.0 fusion.9
  292.8 25.6 %memory_backward.1.parts_ref = bf16[2048,1024]{1,0:T(8,128)(2,1)} custom-call(s32[2048]{0:T(1024)} %bitcast.26, bf16[2048,1024]{1,0:T(8,128)(2,1)} %all-gather.2.cloned.1.call-done.q_ref.refs_4_, bf16[2048,1152]{1,0:T(8,128)(2,1)} %get-tuple-element.67.g_ref.refs_5_, bf16[49152,128]{1,0:T(8,128)(2,1)} %get-tuple-element.50.k_ref, ...), custom_call_target="tpu_custom_call" | custom-call | bytes 75000000 | tf_op jit(solution)/shard_map/memory_backward/pallas_call | solution.py:456
  318.4 72.6 %reduce_group.3.refs_1_.refs_4_ = bf16[128,3072]{1,0:T(8,128)(2,1)} custom-call(bf16[2048,1024]{1,0:T(8,128)(2,1)} %memory_backward.1.parts_ref, f32[8,768]{1,0:T(8,128)} %fusion.refs_0_, s32[1,3]{1,0:T(1,128)} %refs_1_.5, bf16[128,3072]{1,0:T(8,128)(2,1)} %copy-done.1, f32[8]{0:T(128)} %get-tuple-element.86.refs_3_, ...), custom_call_target="tpu_custom_call" | custom-call | bytes 150000000 | tf_op jit(solution)/shard_map/reduce_group/pallas_call | solution.py:821
  391.7 70.9 %finish_grads.1 = (bf16[2,64,1536]{2,1,0:T(8,128)(2,1)}, f32[24,128]{1,0:T(8,128)}, f32[128,1024]{1,0:T(8,128)}, f32[1,1024]{1,0:T(1,128)}) custom-call(bf16[128,1024]{1,0:T(8,128)(2,1)} %copy-done.2, bf16[128,3072]{1,0:T(8,128)(2,1)} %reduce_group.3.refs_1_.refs_4_, bf16[128,1024]{1,0:T(8,128)(2,1)} %refs_2_.3, f32[1,1024]{1,0:T(1,128)} %bitcast.27, ...), custom_call_target="tpu_custom_call" | custom-call | bytes 135000000 | tf_op jit(solution)/shard_map/finish_grads/pallas_call | solution.py:1594
  462.7 4.1 join_halves.1.early_ref
  466.8 3.0 write_results.1
  469.9 1.9 copy.29
  (62 shorter events, 3.6 us)
Async XLA Ops:
  7.2 40.5 %copy-start = (f32[8,32]{1,0:T(8,128)S(1)}, f32[8,32]{1,0:T(8,128)}, u32[]{:S(2)}) copy-start(f32[8,32]{1,0:T(8,128)} %param.20) | copy-start | bytes 3076
  7.2 100.5 %all-gather.2.cloned.1.call-start = ((), (), s32[]{:S(2)}) async-start(), calls=%async_computation.2 | async-start | bytes 4456448 | tf_op jit(solution)/shard_map/all_gather | solution.py:1678
  9.4 4.8 %copy-start.2 = (bf16[128,1024]{1,0:T(8,128)(2,1)}, bf16[128,1024]{1,0:T(8,128)(2,1)S(1)}, u32[]{:S(2)}) copy-start(bf16[128,1024]{1,0:T(8,128)(2,1)S(1)} %fusion.4.refs_0_) | copy-start | bytes 786436
  9.4 4.9 %copy-start.9 = (s32[128,8,32]{0,2,1:T(8,128)S(1)}, s32[128,8,32]{0,2,1:T(8,128)}, u32[]{:S(2)}) copy-start(s32[128,8,32]{0,2,1:T(8,128)} %param.29) | copy-start | bytes 393220
  9.4 4.9 %copy-start.10 = (s32[128,8,32,1]{0,3,2,1:T(1,128)S(1)}, s32[128,8,32,1]{0,3,2,1:T(1,128)}, u32[]{:S(2)}) copy-start(s32[128,8,32,1]{0,3,2,1:T(1,128)} %param.28) | copy-start | bytes 393220
  9.5 4.9 %copy-start.11 = (s32[128,8,32]{0,2,1:T(8,128)S(1)}, s32[128,8,32]{0,2,1:T(8,128)}, u32[]{:S(2)}) copy-start(s32[128,8,32]{0,2,1:T(8,128)} %param.30) | copy-start | bytes 393220
  9.5 37.7 %copy-start.16 = (f32[8]{0:T(128)S(1)}, f32[8]{0:T(128)}, u32[]{:S(2)}) copy-start(f32[8]{0:T(128)} %param.21) | copy-start | bytes 100
  13.4 92.2 %copy-start.1 = (bf16[128,3072]{1,0:T(8,128)(2,1)}, bf16[128,3072]{1,0:T(8,128)(2,1)S(1)}, u32[]{:S(2)}) copy-start(bf16[128,3072]{1,0:T(8,128)(2,1)S(1)} %convolution_convert_fusion.refs_2_) | copy-start | bytes 2359300
  22.1 1.1 copy-start.7
  22.7 0.6 copy-start.15
  26.1 22.7 %all-to-all-start = ((s32[16,24,128]{2,1,0:T(8,128)}), s32[16,24,128]{2,1,0:T(8,128)S(1)}, u32[]{:S(2)}, u32[]{:S(2)}) async-start(s32[16,24,128]{2,1,0:T(8,128)} %make_lists.1), calls=%async_computation | async-start | bytes 393216 | tf_op jit(solution)/shard_map/all_to_all | solution.py:1670
  32.8 429.8 %reduce-scatter.2.cloned.1.call-start = ((), (), s32[]{:S(2)}) async-start(), calls=%async_computation.3 | async-start | bytes 10027008 | tf_op jit(solution)/shard_map/reduce_scatter | solution.py:909
  33.7 98.2 %collective-permute-start.3 = (bf16[128,2048]{1,0:T(8,128)(2,1)}, bf16[128,2048]{1,0:T(8,128)(2,1)S(1)}, u32[]{:S(2)}, u32[]{:S(2)}) collective-permute-start(bf16[128,2048]{1,0:T(8,128)(2,1)} %slice.17), channel_id=1, source_target_pairs={{0,1},{1,2},{2,3},{3,4},{4,5},{5,6},{6,7},{7,8},{8,9},{9,10},{10,1... | collective-permute-start | bytes 1572872 | tf_op jit(solution)/shard_map/ppermute | solution.py:25
  36.8 95.2 %collective-permute-start.2 = (bf16[128,2048]{1,0:T(8,128)(2,1)}, bf16[128,2048]{1,0:T(8,128)(2,1)S(1)}, u32[]{:S(2)}, u32[]{:S(2)}) collective-permute-start(bf16[128,2048]{1,0:T(8,128)(2,1)} %slice.17), channel_id=1, source_target_pairs={{0,2},{1,3},{2,4},{3,5},{4,6},{5,7},{6,8},{7,9},{8,10},{9,11},{10,... | collective-permute-start | bytes 1572872 | tf_op jit(solution)/shard_map/ppermute | solution.py:25
  39.9 92.1 %collective-permute-start.1 = (bf16[128,2048]{1,0:T(8,128)(2,1)}, bf16[128,2048]{1,0:T(8,128)(2,1)S(1)}, u32[]{:S(2)}, u32[]{:S(2)}) collective-permute-start(bf16[128,2048]{1,0:T(8,128)(2,1)} %slice.17), channel_id=1, source_target_pairs={{0,3},{1,4},{2,5},{3,6},{4,7},{5,8},{6,9},{7,10},{8,11},{9,12},{10... | collective-permute-start | bytes 1572872 | tf_op jit(solution)/shard_map/ppermute | solution.py:25
  43.9 88.1 %collective-permute-start = (bf16[128,2048]{1,0:T(8,128)(2,1)}, bf16[128,2048]{1,0:T(8,128)(2,1)S(1)}, u32[]{:S(2)}, u32[]{:S(2)}) collective-permute-start(bf16[128,2048]{1,0:T(8,128)(2,1)} %slice.17), channel_id=1, source_target_pairs={{0,4},{1,5},{2,6},{3,7},{4,8},{5,9},{6,10},{7,11},{8,12},{9,13},{1... | collective-permute-start | bytes 1572872 | tf_op jit(solution)/shard_map/ppermute | solution.py:25
  48.8 0.7 copy-start.8
  131.9 0.8 copy-start.3
  131.9 0.9 copy-start.4
  132.0 1.1 copy-start.5
  133.1 0.8 copy-start.6
  231.0 61.7 %copy-start.12 = (f32[8,128]{1,0:T(8,128)S(1)}, f32[8,128]{1,0:T(8,128)}, u32[]{:S(2)}) copy-start(f32[8,128]{1,0:T(8,128)} %get-tuple-element.72) | copy-start | bytes 12292
  318.4 72.6 %copy-start.14 = (f32[8]{0:T(128)S(1)}, f32[8]{0:T(128)}, u32[]{:S(2)}) copy-start(f32[8]{0:T(128)} %get-tuple-element.87.share_ref.refs_6_) | copy-start | bytes 100
  318.4 72.6 %copy-start.13 = (f32[1,1024]{1,0:T(1,128)S(1)}, f32[1,1024]{1,0:T(1,128)}, u32[]{:S(2)}) copy-start(f32[1,1024]{1,0:T(1,128)} %get-tuple-element.70) | copy-start | bytes 12292
Sparse Core Ops, SparseCore 0:
  14.4 93.3 all-gather.1
  231.1 217.1 reduce-scatter.1

commit v4 on v3

--- a/solution.py
+++ b/solution.py
@@ -1668,13 +1668,13 @@
     slots = memory_keys.shape[0]
     requests = place_requests(slot_shard, slot_index, slot_live, groups, capacity, slots)
     incoming = lax.all_to_all(requests, "mem", split_axis=0, concat_axis=0, tiled=True)
-    keys_values, _ = lax.optimization_barrier((projected[:, width:], requests))
-    halos = [passed_along(keys_values, "mem", distance) for distance in range(repeats, 0, -1)]
     index, row_ids, bounds = read_lists(incoming, heads, rows, slots)
     bounds = bounds.reshape(-1)
     key_rows, value_rows = gather_rows(
         index.reshape(-1), bounds, memory_keys, memory_values, heads, groups, capacity
     )
+    keys_values, key_rows = lax.optimization_barrier((projected[:, width:], key_rows))
+    halos = [passed_along(keys_values, "mem", distance) for distance in range(repeats, 0, -1)]
     all_queries = lax.all_gather(projected[:, :width], "mem", axis=0, tiled=True)
     local = local_forward(before_bias, book_lengths, projected, halos, heads, score_scale)
     partial = memory_forward(

time: 486 us -> 491 us (1.010)
  starting transfers between devices: 20.2 us -> 37.3 us
  Pallas kernels: 416 us -> 403 us
  waiting for transfers between devices: 2.16 us -> 7.69 us
    pallas_call x1, Pallas kernels: 54.1 us -> 36.8 us  [gather_rows(): pl.pallas_call(kernel, grid_spec=pltpu.PrefetchScalarGridSpec(num_scalar_...]
    ppermute x4, starting transfers between devices: 13.4 us -> 30.6 us  [passed_along(): return lax.ppermute(value, axis, pairs)]
    all_to_all x1, waiting for transfers between devices: 0.01 us -> 7.62 us  [on_device(): lax.all_to_all(requests, 'mem', split_axis=0, concat_axis=0, tiled=True)]
  transfers between devices with their start and end apart: 7 -> 7, of which waited for: 1 -> 1; matrix products, arithmetic and copies ran while one was open for 3% -> 3% of each run, Pallas kernels for 65% -> 61%
where the time goes in v4:
time: 491 us; the launch traced here: 488 us
  Pallas kernels  403 us (82%)
  starting transfers between devices  37.3 us (8%)
  between operations  14.8 us (3%)
  other arithmetic  12.1 us (2%)
  waiting for transfers between devices  7.69 us (2%)
  matrix products  7.14 us (1%)
  local copies, waits for them, and re-layouts  5.81 us (1%)
    pallas_call x2, Pallas kernels, reduce_group(): pl.pallas_call(kernel, in_specs=[vmem, *specs], out_specs=[vmem] * (len(o...  143 us
    pallas_call x1, Pallas kernels, finish_grads(): pl.pallas_call(kernel, in_specs=[vmem] * (2 * count) + specs + [vmem], ou...  72.5 us
    pallas_call x1, Pallas kernels, gather_group(): pl.pallas_call(kernel, in_specs=[pl.BlockSpec(memory_space=pl.ANY), *spec...  60.6 us
    pallas_call x1, Pallas kernels, gather_rows(): pl.pallas_call(kernel, grid_spec=pltpu.PrefetchScalarGridSpec(num_scalar_...  36.8 us
    ppermute x4, starting transfers between devices, passed_along(): return lax.ppermute(value, axis, pairs)  30.6 us
    pallas_call x1, Pallas kernels, memory_backward(): pl.pallas_call(kernel, grid_spec=pltpu.PrefetchScalarGridSpec(num_scalar_...  25.6 us
    pallas_call x1, Pallas kernels, memory_forward(): pl.pallas_call(kernel, grid_spec=pltpu.PrefetchScalarGridSpec(num_scalar_...  24.1 us
    pallas_call x1, Pallas kernels, middle(): pl.pallas_call(kernel, grid=(steps,), in_specs=[full, full, full, whole(r...  16 us
  transfers between devices with their start and end apart: 7, of which 1 were waited for; matrix products, arithmetic and copies ran while one was open for 3% of the time, Pallas kernels for 61%

profile of v4, /device:TPU:9, one launch (start us, length us, event | category | flops | bytes accessed | tf_op | source)
XLA Modules:
  0.0 488.3 jit_solution(780873687202106984)
XLA Ops:
  7.2 1.1 fusion.2
  8.3 1.1 fusion.4.refs_0_
  9.5 3.9 convolution_convert_fusion.refs_2_
  13.4 0.8 slice.16
  14.8 7.3 %sort.7 = s32[32768]{0:T(1024)S(1)} sort(s32[32768]{0:T(1024)S(1)} %reshape.297), dimensions={0}, to_apply=%region_0.1 | sort | flops 491520 | bytes 262144 | tf_op jit(solution)/shard_map/sort | solution.py:50
  23.2 2.9 make_lists.1
  26.1 6.7 %all-to-all-start = ((s32[16,24,128]{2,1,0:T(8,128)}), s32[16,24,128]{2,1,0:T(8,128)S(1)}, u32[]{:S(2)}, u32[]{:S(2)}) async-start(s32[16,24,128]{2,1,0:T(8,128)} %make_lists.1), calls=%async_computation | async-start | bytes 393216 | tf_op jit(solution)/shard_map/all_to_all | solution.py:1670
  32.9 7.6 %all-to-all-done.lists_ref = s32[16,24,128]{2,1,0:T(8,128)S(1)} async-done(((s32[16,24,128]{2,1,0:T(8,128)}), s32[16,24,128]{2,1,0:T(8,128)S(1)}, u32[]{:S(2)}, u32[]{:S(2)}) %all-to-all-start) | async-done | bytes 196640 | tf_op jit(solution)/shard_map/all_to_all | solution.py:1670
  40.5 0.7 copy-done.8
  41.2 2.0 read_lists.1
  43.2 36.8 %gather_rows.1 = (bf16[49152,128]{1,0:T(8,128)(2,1)}, bf16[49152,128]{1,0:T(8,128)(2,1)}) custom-call(s32[49152]{0:T(1024)} %bitcast.22, s32[2048]{0:T(1024)} %bitcast.24, bf16[4096,1024]{1,0:T(8,128)(2,1)} %keys.1, bf16[4096,1024]{1,0:T(8,128)(2,1)} %values.1), custom_call_target="tpu_custom_call" | custom-call | bytes 126000000 | tf_op jit(solution)/shard_map/gather_rows/pallas_call | solution.py:171
  80.0 19.0 %collective-permute-start.3 = (bf16[128,2048]{1,0:T(8,128)(2,1)S(1)}, bf16[128,2048]{1,0:T(8,128)(2,1)S(1)}, u32[]{:S(2)}, u32[]{:S(2)}) collective-permute-start(bf16[128,2048]{1,0:T(8,128)(2,1)S(1)} %slice.17), channel_id=1, source_target_pairs={{0,1},{1,2},{2,3},{3,4},{4,5},{5,6},{6,7},{7,8},{8,9},{9,10},{10,1... | collective-permute-start | bytes 1572872 | tf_op jit(solution)/shard_map/ppermute | solution.py:25
  99.0 1.9 collective-permute-start.2
  101.0 7.6 %collective-permute-start.1 = (bf16[128,2048]{1,0:T(8,128)(2,1)S(1)}, bf16[128,2048]{1,0:T(8,128)(2,1)S(1)}, u32[]{:S(2)}, u32[]{:S(2)}) collective-permute-start(bf16[128,2048]{1,0:T(8,128)(2,1)S(1)} %slice.17), channel_id=1, source_target_pairs={{0,3},{1,4},{2,5},{3,6},{4,7},{5,8},{6,9},{7,10},{8,11},{9,12},{10... | collective-permute-start | bytes 1572872 | tf_op jit(solution)/shard_map/ppermute | solution.py:25
  108.5 2.1 collective-permute-start
  111.2 1.1 fusion.1.refs_0_
  112.3 24.1 %memory_forward.1.parts_ref = bf16[2048,1152]{1,0:T(8,128)(2,1)} custom-call(s32[2048]{0:T(1024)} %bitcast.25, bf16[2048,1024]{1,0:T(8,128)(2,1)} %all-gather.2.cloned.1.call-done.q_ref.refs_4_, bf16[49152,128]{1,0:T(8,128)(2,1)} %get-tuple-element.52.k_ref, bf16[49152,128]{1,0:T(8,128)(2,1)} %get-tuple-element.53.v_ref, s32[16,25,128]{2,1,0:T(8,128)} %get-tuple-element.54.id_ref), custom_call_target="tpu_custom_call" | custom-call | bytes 75000000 | tf_op jit(solution)/shard_map/memory_forward/pallas_call | solution.py:307
  136.5 0.7 copy-done.3
  137.6 0.8 copy-done.6
  138.4 71.6 %reduce_group.2 = (f32[128,1024]{1,0:T(8,128)}, f32[128,128]{1,0:T(8,128)}, f32[128,1024]{1,0:T(8,128)}, f32[128,128]{1,0:T(8,128)}) custom-call(bf16[2048,1152]{1,0:T(8,128)(2,1)} %memory_forward.1.parts_ref, f32[8,768]{1,0:T(8,128)} %fusion.1.refs_0_, s32[1,3]{1,0:T(1,128)} %refs_1_.5, bf16[128,3072]{1,0:T(8,128)(2,1)} %copy-done.1, ...), custom_call_target="tpu_custom_call" | custom-call | bytes 150000000 | tf_op jit(solution)/shard_map/reduce_group/pallas_call | solution.py:821
  210.0 16.0 %middle.1 = (bf16[128,1024]{1,0:T(8,128)(2,1)}, bf16[128,1024]{1,0:T(8,128)(2,1)}, bf16[128,4096]{1,0:T(8,128)(2,1)}, bf16[128,4096]{1,0:T(8,128)(2,1)}, bf16[12...) custom-call(bf16[128,1024]{1,0:T(8,128)(2,1)} %refs_2_.3, ...), custom_call_target="tpu_custom_call" | custom-call | bytes 54000000 | tf_op jit(solution)/shard_map/middle/pallas_call | solution.py:1260
  226.1 12.9 %pair_grads.1 = bf16[1024,4608]{1,0:T(8,128)(2,1)} custom-call(bf16[128,1024]{1,0:T(8,128)(2,1)} %get-tuple-element.62.refs_0_, bf16[128,1024]{1,0:T(8,128)(2,1)} %get-tuple-element.63.refs_1_, bf16[128,1024]{1,0:T(8,128)(2,1)} %refs_2_.2, bf16[128,1024]{1,0:T(8,128)(2,1)} %get-tuple-element.64.refs_3_, bf16[128,4096]{1,0:T(8,128)(2,1)} %get-tuple-element.65.refs_4_, ...), custom_call_target="tpu_custom_call" | custom-call | bytes 30000000 | tf_op jit(solution)/shard_map/pair_grads/pallas_call | solution.py:1379
  239.1 1.1 fusion.refs_0_
  240.2 60.6 %gather_group.1 = (bf16[2048,1152]{1,0:T(8,128)(2,1)}, f32[128,1024]{1,0:T(8,128)}, f32[8,768]{1,0:T(8,128)}) custom-call(bf16[128,1152]{1,0:T(8,128)(2,1)} %get-tuple-element.67.x_ref, f32[8,768]{1,0:T(8,128)} %fusion.1.refs_0_, s32[1,3]{1,0:T(1,128)} %refs_1_.5, bf16[128,3072]{1,0:T(8,128)(2,1)} %copy-done.1, f32[128,1024]{1,0:T(8,128)} %get-tuple-element.68.refs_3_, ...), custom_call_target="tpu_custom_call" | custom-call | bytes 150000000 | tf_op jit(solution)/shard_map/gather_group/pallas_call | solution.py:661
  300.8 1.0 fusion.9
  302.0 25.6 %memory_backward.1.parts_ref = bf16[2048,1024]{1,0:T(8,128)(2,1)} custom-call(s32[2048]{0:T(1024)} %bitcast.26, bf16[2048,1024]{1,0:T(8,128)(2,1)} %all-gather.2.cloned.1.call-done.q_ref.refs_4_, bf16[2048,1152]{1,0:T(8,128)(2,1)} %get-tuple-element.69.g_ref.refs_5_, bf16[49152,128]{1,0:T(8,128)(2,1)} %get-tuple-element.52.k_ref, ...), custom_call_target="tpu_custom_call" | custom-call | bytes 75000000 | tf_op jit(solution)/shard_map/memory_backward/pallas_call | solution.py:456
  327.6 71.1 %reduce_group.3.refs_1_.refs_4_ = bf16[128,3072]{1,0:T(8,128)(2,1)} custom-call(bf16[2048,1024]{1,0:T(8,128)(2,1)} %memory_backward.1.parts_ref, f32[8,768]{1,0:T(8,128)} %fusion.refs_0_, s32[1,3]{1,0:T(1,128)} %refs_1_.5, bf16[128,3072]{1,0:T(8,128)(2,1)} %copy-done.1, f32[8]{0:T(128)} %get-tuple-element.88.refs_3_, ...), custom_call_target="tpu_custom_call" | custom-call | bytes 150000000 | tf_op jit(solution)/shard_map/reduce_group/pallas_call | solution.py:821
  398.7 0.6 fusion.16.refs_7_
  399.4 72.5 %finish_grads.1 = (bf16[2,64,1536]{2,1,0:T(8,128)(2,1)}, f32[24,128]{1,0:T(8,128)}, f32[128,1024]{1,0:T(8,128)}, f32[1,1024]{1,0:T(1,128)}) custom-call(bf16[128,1024]{1,0:T(8,128)(2,1)} %copy-done.2, bf16[128,3072]{1,0:T(8,128)(2,1)} %reduce_group.3.refs_1_.refs_4_, bf16[128,1024]{1,0:T(8,128)(2,1)} %refs_2_.3, f32[1,1024]{1,0:T(1,128)} %bitcast.27, ...), custom_call_target="tpu_custom_call" | custom-call | bytes 135000000 | tf_op jit(solution)/shard_map/finish_grads/pallas_call | solution.py:1594
  471.9 4.1 join_halves.1.early_ref
  476.1 3.0 write_results.1
  479.1 1.9 copy.29
  (62 shorter events, 3.1 us)
Async XLA Ops:
  7.2 104.0 %copy-start = (f32[8,32]{1,0:T(8,128)S(1)}, f32[8,32]{1,0:T(8,128)}, u32[]{:S(2)}) copy-start(f32[8,32]{1,0:T(8,128)} %param.20) | copy-start | bytes 3076
  7.2 105.1 %all-gather.2.cloned.1.call-start = ((), (), s32[]{:S(2)}) async-start(), calls=%async_computation.2 | async-start | bytes 4456448 | tf_op jit(solution)/shard_map/all_gather | solution.py:1678
  9.4 4.8 copy-start.2
  9.4 4.9 copy-start.9
  9.4 4.9 copy-start.10
  9.5 4.9 copy-start.11
  13.4 66.6 %copy-start.1 = (bf16[128,3072]{1,0:T(8,128)(2,1)}, bf16[128,3072]{1,0:T(8,128)(2,1)S(1)}, u32[]{:S(2)}) copy-start(bf16[128,3072]{1,0:T(8,128)(2,1)S(1)} %convolution_convert_fusion.refs_2_) | copy-start | bytes 2359300
  22.1 1.1 copy-start.7
  22.6 0.6 copy-start.15
  26.1 14.4 %all-to-all-start = ((s32[16,24,128]{2,1,0:T(8,128)}), s32[16,24,128]{2,1,0:T(8,128)S(1)}, u32[]{:S(2)}, u32[]{:S(2)}) async-start(s32[16,24,128]{2,1,0:T(8,128)} %make_lists.1), calls=%async_computation | async-start | bytes 393216 | tf_op jit(solution)/shard_map/all_to_all | solution.py:1670
  32.8 439.1 %reduce-scatter.2.cloned.1.call-start = ((), (), s32[]{:S(2)}) async-start(), calls=%async_computation.3 | async-start | bytes 10027008 | tf_op jit(solution)/shard_map/reduce_scatter | solution.py:909
  40.5 0.7 copy-start.8
  43.2 67.4 %copy-start.16 = (f32[8]{0:T(128)S(1)}, f32[8]{0:T(128)}, u32[]{:S(2)}) copy-start(f32[8]{0:T(128)} %param.21) | copy-start | bytes 100
  80.0 56.4 %collective-permute-start.3 = (bf16[128,2048]{1,0:T(8,128)(2,1)S(1)}, bf16[128,2048]{1,0:T(8,128)(2,1)S(1)}, u32[]{:S(2)}, u32[]{:S(2)}) collective-permute-start(bf16[128,2048]{1,0:T(8,128)(2,1)S(1)} %slice.17), channel_id=1, source_target_pairs={{0,1},{1,2},{2,3},{3,4},{4,5},{5,6},{6,7},{7,8},{8,9},{9,10},{10,1... | collective-permute-start | bytes 1572872 | tf_op jit(solution)/shard_map/ppermute | solution.py:25
  99.0 37.4 %collective-permute-start.2 = (bf16[128,2048]{1,0:T(8,128)(2,1)S(1)}, bf16[128,2048]{1,0:T(8,128)(2,1)S(1)}, u32[]{:S(2)}, u32[]{:S(2)}) collective-permute-start(bf16[128,2048]{1,0:T(8,128)(2,1)S(1)} %slice.17), channel_id=1, source_target_pairs={{0,2},{1,3},{2,4},{3,5},{4,6},{5,7},{6,8},{7,9},{8,10},{9,11},{10,... | collective-permute-start | bytes 1572872 | tf_op jit(solution)/shard_map/ppermute | solution.py:25
  101.0 35.5 %collective-permute-start.1 = (bf16[128,2048]{1,0:T(8,128)(2,1)S(1)}, bf16[128,2048]{1,0:T(8,128)(2,1)S(1)}, u32[]{:S(2)}, u32[]{:S(2)}) collective-permute-start(bf16[128,2048]{1,0:T(8,128)(2,1)S(1)} %slice.17), channel_id=1, source_target_pairs={{0,3},{1,4},{2,5},{3,6},{4,7},{5,8},{6,9},{7,10},{8,11},{9,12},{10... | collective-permute-start | bytes 1572872 | tf_op jit(solution)/shard_map/ppermute | solution.py:25
  108.5 28.0 %collective-permute-start = (bf16[128,2048]{1,0:T(8,128)(2,1)S(1)}, bf16[128,2048]{1,0:T(8,128)(2,1)S(1)}, u32[]{:S(2)}, u32[]{:S(2)}) collective-permute-start(bf16[128,2048]{1,0:T(8,128)(2,1)S(1)} %slice.17), channel_id=1, source_target_pairs={{0,4},{1,5},{2,6},{3,7},{4,8},{5,9},{6,10},{7,11},{8,12},{9,13},{1... | collective-permute-start | bytes 1572872 | tf_op jit(solution)/shard_map/ppermute | solution.py:25
  136.5 0.8 copy-start.3
  136.5 0.9 copy-start.4
  136.5 1.1 copy-start.5
  137.6 0.8 copy-start.6
  239.0 62.9 %copy-start.12 = (f32[8,128]{1,0:T(8,128)S(1)}, f32[8,128]{1,0:T(8,128)}, u32[]{:S(2)}) copy-start(f32[8,128]{1,0:T(8,128)} %get-tuple-element.74) | copy-start | bytes 12292
  327.6 71.1 %copy-start.14 = (f32[8]{0:T(128)S(1)}, f32[8]{0:T(128)}, u32[]{:S(2)}) copy-start(f32[8]{0:T(128)} %get-tuple-element.89.share_ref.refs_6_) | copy-start | bytes 100
  327.6 71.1 %copy-start.13 = (f32[1,1024]{1,0:T(1,128)S(1)}, f32[1,1024]{1,0:T(1,128)}, u32[]{:S(2)}) copy-start(f32[1,1024]{1,0:T(1,128)} %get-tuple-element.72) | copy-start | bytes 12292
Sparse Core Ops, SparseCore 0:
  14.3 77.6 all-gather.1
  239.2 218.6 reduce-scatter.1

commit v5 on v3

--- a/solution.py
+++ b/solution.py
@@ -1669,12 +1669,15 @@
     requests = place_requests(slot_shard, slot_index, slot_live, groups, capacity, slots)
     incoming = lax.all_to_all(requests, "mem", split_axis=0, concat_axis=0, tiled=True)
     keys_values, _ = lax.optimization_barrier((projected[:, width:], requests))
-    halos = [passed_along(keys_values, "mem", distance) for distance in range(repeats, 0, -1)]
+    distances = list(range(repeats, 0, -1))
+    halos = [passed_along(keys_values, "mem", distance) for distance in distances[: repeats // 2]]
     index, row_ids, bounds = read_lists(incoming, heads, rows, slots)
     bounds = bounds.reshape(-1)
     key_rows, value_rows = gather_rows(
         index.reshape(-1), bounds, memory_keys, memory_values, heads, groups, capacity
     )
+    keys_values, key_rows = lax.optimization_barrier((keys_values, key_rows))
+    halos += [passed_along(keys_values, "mem", distance) for distance in distances[repeats // 2 :]]
     all_queries = lax.all_gather(projected[:, :width], "mem", axis=0, tiled=True)
     local = local_forward(before_bias, book_lengths, projected, halos, heads, score_scale)
     partial = memory_forward(

time: 486 us -> 470 us (0.967)
  Pallas kernels: 416 us -> 389 us
  starting transfers between devices: 20.2 us -> 33.5 us
    pallas_call x1, Pallas kernels: 54.1 us -> 40.6 us  [gather_rows(): pl.pallas_call(kernel, grid_spec=pltpu.PrefetchScalarGridSpec(num_scalar_...]
    ppermute x4, starting transfers between devices: 13.4 us -> 26.8 us  [passed_along(): return lax.ppermute(value, axis, pairs)]
    pallas_call x2, Pallas kernels: 141 us -> 131 us  [reduce_group(): pl.pallas_call(kernel, in_specs=[vmem, *specs], out_specs=[vmem] * (len(o...]
  transfers between devices with their start and end apart: 7 -> 7, of which waited for: 1 -> 1; matrix products, arithmetic and copies ran while one was open for 3% -> 3% of each run, Pallas kernels for 65% -> 64%
where the time goes in v5:
time: 470 us; the launch traced here: 463 us
  Pallas kernels  389 us (83%)
  starting transfers between devices  33.5 us (7%)
  between operations  14.8 us (3%)
  other arithmetic  12.1 us (3%)
  matrix products  7.14 us (2%)
  local copies, waits for them, and re-layouts  5.79 us (1%)
    pallas_call x2, Pallas kernels, reduce_group(): pl.pallas_call(kernel, in_specs=[vmem, *specs], out_specs=[vmem] * (len(o...  131 us
    pallas_call x1, Pallas kernels, finish_grads(): pl.pallas_call(kernel, in_specs=[vmem] * (2 * count) + specs + [vmem], ou...  71.1 us
    pallas_call x1, Pallas kernels, gather_group(): pl.pallas_call(kernel, in_specs=[pl.BlockSpec(memory_space=pl.ANY), *spec...  56.8 us
    pallas_call x1, Pallas kernels, gather_rows(): pl.pallas_call(kernel, grid_spec=pltpu.PrefetchScalarGridSpec(num_scalar_...  40.6 us
    ppermute x4, starting transfers between devices, passed_along(): return lax.ppermute(value, axis, pairs)  26.8 us
    pallas_call x1, Pallas kernels, memory_backward(): pl.pallas_call(kernel, grid_spec=pltpu.PrefetchScalarGridSpec(num_scalar_...  25.5 us
    pallas_call x1, Pallas kernels, memory_forward(): pl.pallas_call(kernel, grid_spec=pltpu.PrefetchScalarGridSpec(num_scalar_...  24.1 us
    pallas_call x1, Pallas kernels, middle(): pl.pallas_call(kernel, grid=(steps,), in_specs=[full, full, full, whole(r...  16.1 us
  transfers between devices with their start and end apart: 7, of which 1 were waited for; matrix products, arithmetic and copies ran while one was open for 3% of the time, Pallas kernels for 64%

profile of v5, /device:TPU:9, one launch (start us, length us, event | category | flops | bytes accessed | tf_op | source)
XLA Modules:
  0.0 462.8 jit_solution(16663005316574309568)
XLA Ops:
  7.2 1.1 fusion.2
  8.3 1.1 fusion.4.refs_0_
  9.5 3.9 convolution_convert_fusion.refs_2_
  13.4 0.8 slice.16
  14.8 7.3 %sort.7 = s32[32768]{0:T(1024)S(1)} sort(s32[32768]{0:T(1024)S(1)} %reshape.297), dimensions={0}, to_apply=%region_0.1 | sort | flops 491520 | bytes 262144 | tf_op jit(solution)/shard_map/sort | solution.py:50
  22.6 0.6 pad_add_fusion.starts_ref
  23.2 2.9 make_lists.1
  26.1 6.7 %all-to-all-start = ((s32[16,24,128]{2,1,0:T(8,128)}), s32[16,24,128]{2,1,0:T(8,128)S(1)}, u32[]{:S(2)}, u32[]{:S(2)}) async-start(s32[16,24,128]{2,1,0:T(8,128)} %make_lists.1), calls=%async_computation | async-start | bytes 393216 | tf_op jit(solution)/shard_map/all_to_all | solution.py:1670
  32.9 4.0 collective-permute-start.1
  36.9 3.1 collective-permute-start
  40.5 0.7 copy-done.8
  41.2 2.0 read_lists.1
  43.2 40.6 %gather_rows.1 = (bf16[49152,128]{1,0:T(8,128)(2,1)}, bf16[49152,128]{1,0:T(8,128)(2,1)}) custom-call(s32[49152]{0:T(1024)} %bitcast.22, s32[2048]{0:T(1024)} %bitcast.24, bf16[4096,1024]{1,0:T(8,128)(2,1)} %keys.1, bf16[4096,1024]{1,0:T(8,128)(2,1)} %values.1), custom_call_target="tpu_custom_call" | custom-call | bytes 126000000 | tf_op jit(solution)/shard_map/gather_rows/pallas_call | solution.py:171
  83.8 8.2 %collective-permute-start.3 = (bf16[128,2048]{1,0:T(8,128)(2,1)S(1)}, bf16[128,2048]{1,0:T(8,128)(2,1)S(1)}, u32[]{:S(2)}, u32[]{:S(2)}) collective-permute-start(bf16[128,2048]{1,0:T(8,128)(2,1)S(1)} %slice.17), channel_id=1, source_target_pairs={{0,1},{1,2},{2,3},{3,4},{4,5},{5,6},{6,7},{7,8},{8,9},{9,10},{10,1... | collective-permute-start | bytes 1572872 | tf_op jit(solution)/shard_map/ppermute | solution.py:25
  92.0 11.4 %collective-permute-start.2 = (bf16[128,2048]{1,0:T(8,128)(2,1)S(1)}, bf16[128,2048]{1,0:T(8,128)(2,1)S(1)}, u32[]{:S(2)}, u32[]{:S(2)}) collective-permute-start(bf16[128,2048]{1,0:T(8,128)(2,1)S(1)} %slice.17), channel_id=1, source_target_pairs={{0,2},{1,3},{2,4},{3,5},{4,6},{5,7},{6,8},{7,9},{8,10},{9,11},{10,... | collective-permute-start | bytes 1572872 | tf_op jit(solution)/shard_map/ppermute | solution.py:25
  104.1 1.1 fusion.1.refs_0_
  105.2 24.1 %memory_forward.1.parts_ref = bf16[2048,1152]{1,0:T(8,128)(2,1)} custom-call(s32[2048]{0:T(1024)} %bitcast.25, bf16[2048,1024]{1,0:T(8,128)(2,1)} %all-gather.2.cloned.1.call-done.q_ref.refs_4_, bf16[49152,128]{1,0:T(8,128)(2,1)} %get-tuple-element.54.k_ref, bf16[49152,128]{1,0:T(8,128)(2,1)} %get-tuple-element.55.v_ref, s32[16,25,128]{2,1,0:T(8,128)} %get-tuple-element.56.id_ref), custom_call_target="tpu_custom_call" | custom-call | bytes 75000000 | tf_op jit(solution)/shard_map/memory_forward/pallas_call | solution.py:307
  129.4 0.7 copy-done.3
  130.4 0.8 copy-done.6
  131.2 58.7 %reduce_group.2 = (f32[128,1024]{1,0:T(8,128)}, f32[128,128]{1,0:T(8,128)}, f32[128,1024]{1,0:T(8,128)}, f32[128,128]{1,0:T(8,128)}) custom-call(bf16[2048,1152]{1,0:T(8,128)(2,1)} %memory_forward.1.parts_ref, f32[8,768]{1,0:T(8,128)} %fusion.1.refs_0_, s32[1,3]{1,0:T(1,128)} %refs_1_.5, bf16[128,3072]{1,0:T(8,128)(2,1)} %copy-done.1, ...), custom_call_target="tpu_custom_call" | custom-call | bytes 150000000 | tf_op jit(solution)/shard_map/reduce_group/pallas_call | solution.py:821
  189.9 16.1 %middle.1 = (bf16[128,1024]{1,0:T(8,128)(2,1)}, bf16[128,1024]{1,0:T(8,128)(2,1)}, bf16[128,4096]{1,0:T(8,128)(2,1)}, bf16[128,4096]{1,0:T(8,128)(2,1)}, bf16[12...) custom-call(bf16[128,1024]{1,0:T(8,128)(2,1)} %refs_2_.3, ...), custom_call_target="tpu_custom_call" | custom-call | bytes 54000000 | tf_op jit(solution)/shard_map/middle/pallas_call | solution.py:1260
  206.0 11.2 %pair_grads.1 = bf16[1024,4608]{1,0:T(8,128)(2,1)} custom-call(bf16[128,1024]{1,0:T(8,128)(2,1)} %get-tuple-element.64.refs_0_, bf16[128,1024]{1,0:T(8,128)(2,1)} %get-tuple-element.65.refs_1_, bf16[128,1024]{1,0:T(8,128)(2,1)} %refs_2_.2, bf16[128,1024]{1,0:T(8,128)(2,1)} %get-tuple-element.66.refs_3_, bf16[128,4096]{1,0:T(8,128)(2,1)} %get-tuple-element.67.refs_4_, ...), custom_call_target="tpu_custom_call" | custom-call | bytes 30000000 | tf_op jit(solution)/shard_map/pair_grads/pallas_call | solution.py:1379
  217.3 1.1 fusion.refs_0_
  218.4 56.8 %gather_group.1 = (bf16[2048,1152]{1,0:T(8,128)(2,1)}, f32[128,1024]{1,0:T(8,128)}, f32[8,768]{1,0:T(8,128)}) custom-call(bf16[128,1152]{1,0:T(8,128)(2,1)} %get-tuple-element.69.x_ref, f32[8,768]{1,0:T(8,128)} %fusion.1.refs_0_, s32[1,3]{1,0:T(1,128)} %refs_1_.5, bf16[128,3072]{1,0:T(8,128)(2,1)} %copy-done.1, f32[128,1024]{1,0:T(8,128)} %get-tuple-element.70.refs_3_, ...), custom_call_target="tpu_custom_call" | custom-call | bytes 150000000 | tf_op jit(solution)/shard_map/gather_group/pallas_call | solution.py:661
  275.2 1.0 fusion.9
  276.5 25.5 %memory_backward.1.parts_ref = bf16[2048,1024]{1,0:T(8,128)(2,1)} custom-call(s32[2048]{0:T(1024)} %bitcast.26, bf16[2048,1024]{1,0:T(8,128)(2,1)} %all-gather.2.cloned.1.call-done.q_ref.refs_4_, bf16[2048,1152]{1,0:T(8,128)(2,1)} %get-tuple-element.71.g_ref.refs_5_, bf16[49152,128]{1,0:T(8,128)(2,1)} %get-tuple-element.54.k_ref, ...), custom_call_target="tpu_custom_call" | custom-call | bytes 75000000 | tf_op jit(solution)/shard_map/memory_backward/pallas_call | solution.py:456
  302.0 72.7 %reduce_group.3.refs_1_.refs_4_ = bf16[128,3072]{1,0:T(8,128)(2,1)} custom-call(bf16[2048,1024]{1,0:T(8,128)(2,1)} %memory_backward.1.parts_ref, f32[8,768]{1,0:T(8,128)} %fusion.refs_0_, s32[1,3]{1,0:T(1,128)} %refs_1_.5, bf16[128,3072]{1,0:T(8,128)(2,1)} %copy-done.1, f32[8]{0:T(128)} %get-tuple-element.90.refs_3_, ...), custom_call_target="tpu_custom_call" | custom-call | bytes 150000000 | tf_op jit(solution)/shard_map/reduce_group/pallas_call | solution.py:821
  374.7 0.6 fusion.16.refs_7_
  375.3 71.1 %finish_grads.1 = (bf16[2,64,1536]{2,1,0:T(8,128)(2,1)}, f32[24,128]{1,0:T(8,128)}, f32[128,1024]{1,0:T(8,128)}, f32[1,1024]{1,0:T(1,128)}) custom-call(bf16[128,1024]{1,0:T(8,128)(2,1)} %copy-done.2, bf16[128,3072]{1,0:T(8,128)(2,1)} %reduce_group.3.refs_1_.refs_4_, bf16[128,1024]{1,0:T(8,128)(2,1)} %refs_2_.3, f32[1,1024]{1,0:T(1,128)} %bitcast.27, ...), custom_call_target="tpu_custom_call" | custom-call | bytes 135000000 | tf_op jit(solution)/shard_map/finish_grads/pallas_call | solution.py:1594
  446.4 4.1 join_halves.1.early_ref
  450.6 3.0 write_results.1
  453.6 1.9 copy.29
  (62 shorter events, 3.0 us)
Async XLA Ops:
  7.2 96.9 %copy-start = (f32[8,32]{1,0:T(8,128)S(1)}, f32[8,32]{1,0:T(8,128)}, u32[]{:S(2)}) copy-start(f32[8,32]{1,0:T(8,128)} %param.20) | copy-start | bytes 3076
  7.2 98.0 %all-gather.2.cloned.1.call-start = ((), (), s32[]{:S(2)}) async-start(), calls=%async_computation.2 | async-start | bytes 4456448 | tf_op jit(solution)/shard_map/all_gather | solution.py:1681
  9.4 4.8 %copy-start.2 = (bf16[128,1024]{1,0:T(8,128)(2,1)}, bf16[128,1024]{1,0:T(8,128)(2,1)S(1)}, u32[]{:S(2)}) copy-start(bf16[128,1024]{1,0:T(8,128)(2,1)S(1)} %fusion.4.refs_0_) | copy-start | bytes 786436
  9.4 4.9 %copy-start.9 = (s32[128,8,32]{0,2,1:T(8,128)S(1)}, s32[128,8,32]{0,2,1:T(8,128)}, u32[]{:S(2)}) copy-start(s32[128,8,32]{0,2,1:T(8,128)} %param.29) | copy-start | bytes 393220
  9.4 4.9 %copy-start.10 = (s32[128,8,32,1]{0,3,2,1:T(1,128)S(1)}, s32[128,8,32,1]{0,3,2,1:T(1,128)}, u32[]{:S(2)}) copy-start(s32[128,8,32,1]{0,3,2,1:T(1,128)} %param.28) | copy-start | bytes 393220
  9.5 4.9 %copy-start.11 = (s32[128,8,32]{0,2,1:T(8,128)S(1)}, s32[128,8,32]{0,2,1:T(8,128)}, u32[]{:S(2)}) copy-start(s32[128,8,32]{0,2,1:T(8,128)} %param.30) | copy-start | bytes 393220
  13.4 70.4 %copy-start.1 = (bf16[128,3072]{1,0:T(8,128)(2,1)}, bf16[128,3072]{1,0:T(8,128)(2,1)S(1)}, u32[]{:S(2)}) copy-start(bf16[128,3072]{1,0:T(8,128)(2,1)S(1)} %convolution_convert_fusion.refs_2_) | copy-start | bytes 2359300
  22.1 1.1 copy-start.7
  22.6 0.6 copy-start.15
  26.1 14.4 %all-to-all-start = ((s32[16,24,128]{2,1,0:T(8,128)}), s32[16,24,128]{2,1,0:T(8,128)S(1)}, u32[]{:S(2)}, u32[]{:S(2)}) async-start(s32[16,24,128]{2,1,0:T(8,128)} %make_lists.1), calls=%async_computation | async-start | bytes 393216 | tf_op jit(solution)/shard_map/all_to_all | solution.py:1670
  32.8 413.6 %reduce-scatter.2.cloned.1.call-start = ((), (), s32[]{:S(2)}) async-start(), calls=%async_computation.3 | async-start | bytes 10027008 | tf_op jit(solution)/shard_map/reduce_scatter | solution.py:909
  32.9 96.4 %collective-permute-start.1 = (bf16[128,2048]{1,0:T(8,128)(2,1)S(1)}, bf16[128,2048]{1,0:T(8,128)(2,1)S(1)}, u32[]{:S(2)}, u32[]{:S(2)}) collective-permute-start(bf16[128,2048]{1,0:T(8,128)(2,1)S(1)} %slice.17), channel_id=1, source_target_pairs={{0,3},{1,4},{2,5},{3,6},{4,7},{5,8},{6,9},{7,10},{8,11},{9,12},{10... | collective-permute-start | bytes 1572872 | tf_op jit(solution)/shard_map/ppermute | solution.py:25
  36.9 92.4 %collective-permute-start = (bf16[128,2048]{1,0:T(8,128)(2,1)S(1)}, bf16[128,2048]{1,0:T(8,128)(2,1)S(1)}, u32[]{:S(2)}, u32[]{:S(2)}) collective-permute-start(bf16[128,2048]{1,0:T(8,128)(2,1)S(1)} %slice.17), channel_id=1, source_target_pairs={{0,4},{1,5},{2,6},{3,7},{4,8},{5,9},{6,10},{7,11},{8,12},{9,13},{1... | collective-permute-start | bytes 1572872 | tf_op jit(solution)/shard_map/ppermute | solution.py:25
  40.5 0.7 copy-start.8
  43.2 60.3 %copy-start.16 = (f32[8]{0:T(128)S(1)}, f32[8]{0:T(128)}, u32[]{:S(2)}) copy-start(f32[8]{0:T(128)} %param.21) | copy-start | bytes 100
  83.8 45.5 %collective-permute-start.3 = (bf16[128,2048]{1,0:T(8,128)(2,1)S(1)}, bf16[128,2048]{1,0:T(8,128)(2,1)S(1)}, u32[]{:S(2)}, u32[]{:S(2)}) collective-permute-start(bf16[128,2048]{1,0:T(8,128)(2,1)S(1)} %slice.17), channel_id=1, source_target_pairs={{0,1},{1,2},{2,3},{3,4},{4,5},{5,6},{6,7},{7,8},{8,9},{9,10},{10,1... | collective-permute-start | bytes 1572872 | tf_op jit(solution)/shard_map/ppermute | solution.py:25
  92.0 37.3 %collective-permute-start.2 = (bf16[128,2048]{1,0:T(8,128)(2,1)S(1)}, bf16[128,2048]{1,0:T(8,128)(2,1)S(1)}, u32[]{:S(2)}, u32[]{:S(2)}) collective-permute-start(bf16[128,2048]{1,0:T(8,128)(2,1)S(1)} %slice.17), channel_id=1, source_target_pairs={{0,2},{1,3},{2,4},{3,5},{4,6},{5,7},{6,8},{7,9},{8,10},{9,11},{10,... | collective-permute-start | bytes 1572872 | tf_op jit(solution)/shard_map/ppermute | solution.py:25
  129.3 0.8 copy-start.3
  129.3 1.0 copy-start.4
  129.3 1.1 copy-start.5
  130.4 0.8 copy-start.6
  217.2 59.1 %copy-start.12 = (f32[8,128]{1,0:T(8,128)S(1)}, f32[8,128]{1,0:T(8,128)}, u32[]{:S(2)}) copy-start(f32[8,128]{1,0:T(8,128)} %get-tuple-element.76) | copy-start | bytes 12292
  302.0 72.7 %copy-start.14 = (f32[8]{0:T(128)S(1)}, f32[8]{0:T(128)}, u32[]{:S(2)}) copy-start(f32[8]{0:T(128)} %get-tuple-element.91.share_ref.refs_6_) | copy-start | bytes 100
  302.0 72.7 %copy-start.13 = (f32[1,1024]{1,0:T(1,128)S(1)}, f32[1,1024]{1,0:T(1,128)}, u32[]{:S(2)}) copy-start(f32[1,1024]{1,0:T(1,128)} %get-tuple-element.74) | copy-start | bytes 12292
Sparse Core Ops, SparseCore 0:
  14.3 85.6 all-gather.1
  217.4 215.7 reduce-scatter.1

commit v6 on v5

--- a/solution.py
+++ b/solution.py
@@ -1469,15 +1469,16 @@
     )(sums)
 
 
-def write_results(late, late_widths, early, early_widths, small, heads, buckets):
+def write_results(late, late_widths, early, early_widths, small, input_grad, heads, buckets):
     rows, width = late.shape[1], late.shape[2] * 2 // 3
     lines = width // 128
     count = len(late_widths) + len(early_widths)
 
-    def kernel(late_ref, early_ref, small_ref, *outs):
+    def kernel(late_ref, early_ref, small_ref, input_ref, *outs):
         spread_halves(late_ref, outs[: len(late_widths)])
         spread_halves(early_ref, outs[len(late_widths) : count])
-        attn_ref, ffn_ref, bias_ref, gate_ref = outs[count:]
+        attn_ref, ffn_ref, bias_ref, gate_ref, grad_ref = outs[count:]
+        grad_ref[...] = input_ref[...]
         attn_ref[...] = small_ref[:lines, :]
         ffn_ref[...] = small_ref[lines : 2 * lines, :]
         for head in range(heads):
@@ -1488,14 +1489,14 @@
         gate_ref[...] = small_ref[line : line + 1, :heads]
 
     shapes = [(rows, size) for size in [*late_widths, *early_widths]]
-    shapes += [(lines, 128), (lines, 128), (heads, buckets), (1, heads)]
+    shapes += [(lines, 128), (lines, 128), (heads, buckets), (1, heads), input_grad.shape]
     return pl.pallas_call(
         kernel,
         out_shape=[jax.ShapeDtypeStruct(shape, jnp.float32) for shape in shapes],
         compiler_params=pltpu.CompilerParams(vmem_limit_bytes=VMEM_LIMIT),
         cost_estimate=lasting(3),
         name="write_results",
-    )(late, early, small)
+    )(late, early, small, input_grad)
 
 
 def finish_grads(lefts, rights, small, sources, collective_id, beside):
@@ -1673,6 +1674,7 @@
     halos = [passed_along(keys_values, "mem", distance) for distance in distances[: repeats // 2]]
     index, row_ids, bounds = read_lists(incoming, heads, rows, slots)
     bounds = bounds.reshape(-1)
+    index, before_bias, after_bias = lax.optimization_barrier((index, before_bias, after_bias))
     key_rows, value_rows = gather_rows(
         index.reshape(-1), bounds, memory_keys, memory_values, heads, groups, capacity
     )
@@ -1808,8 +1810,10 @@
         late_both = lax.all_gather(scattered(late_halves), "dp", axis=0)
         early_both = lax.all_gather(early_sums, "dp", axis=0)
         small = lax.psum(small.at[: width // 128].set(attn_gain_part.reshape(-1, 128)), ("dp", "mem"))
-    qkv_grad, out_grad, up_grad, down_grad, attn_sum, ffn_sum, bias_sum, gate_sum = write_results(
-        late_both, [3 * width], early_both, early_widths, small, heads, buckets
+    qkv_grad, out_grad, up_grad, down_grad, attn_sum, ffn_sum, bias_sum, gate_sum, tokens_grad = (
+        write_results(
+            late_both, [3 * width], early_both, early_widths, small, tokens_grad, heads, buckets
+        )
     )
     return (
         block_out,

time: 470 us -> 466 us (level)
  starting transfers between devices: 33.5 us -> 17.8 us
  Pallas kernels: 389 us -> 398 us
    ppermute x4, starting transfers between devices: 26.8 us -> 11.1 us  [passed_along(): return lax.ppermute(value, axis, pairs)]
    pallas_call x2, Pallas kernels: 131 us -> 144 us  [reduce_group(): pl.pallas_call(kernel, in_specs=[vmem, *specs], out_specs=[vmem] * (len(o...]
    pallas_call x1, Pallas kernels: 71.1 us -> 60.3 us  [finish_grads(): pl.pallas_call(kernel, in_specs=[vmem] * (2 * count) + specs + [vmem], ou...]
    pallas_call x1, Pallas kernels: 40.6 us -> 46.6 us  [gather_rows(): pl.pallas_call(kernel, grid_spec=pltpu.PrefetchScalarGridSpec(num_scalar_...]
  transfers between devices with their start and end apart: 7 -> 7, of which waited for: 1 -> 1; matrix products, arithmetic and copies ran while one was open for 3% -> 3% of each run, Pallas kernels for 64% -> 66%
where the time goes in v6:
time: 466 us; the launch traced here: 457 us
  Pallas kernels  398 us (85%)
  starting transfers between devices  17.8 us (4%)
  between operations  14.9 us (3%)
  other arithmetic  12.1 us (3%)
  matrix products  7.13 us (2%)
    pallas_call x2, Pallas kernels, reduce_group(): pl.pallas_call(kernel, in_specs=[vmem, *specs], out_specs=[vmem] * (len(o...  144 us
    pallas_call x1, Pallas kernels, finish_grads(): pl.pallas_call(kernel, in_specs=[vmem] * (2 * count) + specs + [vmem], ou...  60.3 us
    pallas_call x1, Pallas kernels, gather_group(): pl.pallas_call(kernel, in_specs=[pl.BlockSpec(memory_space=pl.ANY), *spec...  57.1 us
    pallas_call x1, Pallas kernels, gather_rows(): pl.pallas_call(kernel, grid_spec=pltpu.PrefetchScalarGridSpec(num_scalar_...  46.6 us
    pallas_call x1, Pallas kernels, memory_backward(): pl.pallas_call(kernel, grid_spec=pltpu.PrefetchScalarGridSpec(num_scalar_...  25.7 us
    pallas_call x1, Pallas kernels, memory_forward(): pl.pallas_call(kernel, grid_spec=pltpu.PrefetchScalarGridSpec(num_scalar_...  24.1 us
    pallas_call x1, Pallas kernels, middle(): pl.pallas_call(kernel, grid=(steps,), in_specs=[full, full, full, whole(r...  16 us
    pallas_call x1, Pallas kernels, pair_grads(): pl.pallas_call(kernel, in_specs=[vmem] * (2 * count), out_specs=pl.BlockS...  11.3 us
  transfers between devices with their start and end apart: 7, of which 1 were waited for; matrix products, arithmetic and copies ran while one was open for 3% of the time, Pallas kernels for 66%

profile of v6, /device:TPU:9, one launch (start us, length us, event | category | flops | bytes accessed | tf_op | source)
XLA Modules:
  0.0 457.1 jit_solution(4503338348758942829)
XLA Ops:
  7.2 1.1 fusion.2
  8.3 1.1 fusion.4.refs_0_
  9.5 3.9 convolution_convert_fusion.refs_2_
  13.4 0.8 slice.16
  14.8 7.3 %sort.7 = s32[32768]{0:T(1024)S(1)} sort(s32[32768]{0:T(1024)S(1)} %reshape.297), dimensions={0}, to_apply=%region_0.1 | sort | flops 491520 | bytes 262144 | tf_op jit(solution)/shard_map/sort | solution.py:50
  22.7 0.6 pad_add_fusion.starts_ref
  23.2 2.9 make_lists.1
  26.1 6.7 %all-to-all-start = ((s32[16,24,128]{2,1,0:T(8,128)}), s32[16,24,128]{2,1,0:T(8,128)S(1)}, u32[]{:S(2)}, u32[]{:S(2)}) async-start(s32[16,24,128]{2,1,0:T(8,128)} %make_lists.1), calls=%async_computation | async-start | bytes 393216 | tf_op jit(solution)/shard_map/all_to_all | solution.py:1671
  32.9 4.0 collective-permute-start.1
  36.9 3.1 collective-permute-start
  40.0 1.1 fusion.refs_0_
  41.2 1.1 fusion.1.refs_0_
  42.3 0.7 copy-done.9
  42.9 2.0 read_lists.1
  45.0 46.6 %gather_rows.1 = (bf16[49152,128]{1,0:T(8,128)(2,1)}, bf16[49152,128]{1,0:T(8,128)(2,1)}) custom-call(s32[49152]{0:T(1024)} %bitcast.22, s32[2048]{0:T(1024)} %bitcast.24, bf16[4096,1024]{1,0:T(8,128)(2,1)} %keys.1, bf16[4096,1024]{1,0:T(8,128)(2,1)} %values.1), custom_call_target="tpu_custom_call" | custom-call | bytes 126000000 | tf_op jit(solution)/shard_map/gather_rows/pallas_call | solution.py:171
  91.6 1.9 collective-permute-start.3
  93.5 2.1 collective-permute-start.2
  96.2 3.7 all-gather.2.cloned.1.call-done.q_ref.refs_4_
  99.9 24.1 %memory_forward.1.parts_ref = bf16[2048,1152]{1,0:T(8,128)(2,1)} custom-call(s32[2048]{0:T(1024)} %bitcast.25, bf16[2048,1024]{1,0:T(8,128)(2,1)} %all-gather.2.cloned.1.call-done.q_ref.refs_4_, bf16[49152,128]{1,0:T(8,128)(2,1)} %get-tuple-element.59.k_ref, bf16[49152,128]{1,0:T(8,128)(2,1)} %get-tuple-element.60.v_ref, s32[16,25,128]{2,1,0:T(8,128)} %get-tuple-element.61.id_ref), custom_call_target="tpu_custom_call" | custom-call | bytes 75000000 | tf_op jit(solution)/shard_map/memory_forward/pallas_call | solution.py:307
  124.1 0.7 copy-done.4
  125.2 0.8 copy-done.7
  125.9 63.2 %reduce_group.2 = (f32[128,1024]{1,0:T(8,128)}, f32[128,128]{1,0:T(8,128)}, f32[128,1024]{1,0:T(8,128)}, f32[128,128]{1,0:T(8,128)}) custom-call(bf16[2048,1152]{1,0:T(8,128)(2,1)} %memory_forward.1.parts_ref, f32[8,768]{1,0:T(8,128)} %fusion.1.refs_0_, s32[1,3]{1,0:T(1,128)} %refs_1_.5, bf16[128,3072]{1,0:T(8,128)(2,1)} %copy-done.2, ...), custom_call_target="tpu_custom_call" | custom-call | bytes 150000000 | tf_op jit(solution)/shard_map/reduce_group/pallas_call | solution.py:821
  189.1 16.0 %middle.1 = (bf16[128,1024]{1,0:T(8,128)(2,1)}, bf16[128,1024]{1,0:T(8,128)(2,1)}, bf16[128,4096]{1,0:T(8,128)(2,1)}, bf16[128,4096]{1,0:T(8,128)(2,1)}, bf16[12...) custom-call(bf16[128,1024]{1,0:T(8,128)(2,1)} %refs_2_.3, ...), custom_call_target="tpu_custom_call" | custom-call | bytes 54000000 | tf_op jit(solution)/shard_map/middle/pallas_call | solution.py:1260
  205.2 11.3 %pair_grads.1 = bf16[1024,4608]{1,0:T(8,128)(2,1)} custom-call(bf16[128,1024]{1,0:T(8,128)(2,1)} %get-tuple-element.70.refs_0_, bf16[128,1024]{1,0:T(8,128)(2,1)} %get-tuple-element.71.refs_1_, bf16[128,1024]{1,0:T(8,128)(2,1)} %refs_2_.2, bf16[128,1024]{1,0:T(8,128)(2,1)} %get-tuple-element.72.refs_3_, bf16[128,4096]{1,0:T(8,128)(2,1)} %get-tuple-element.73.refs_4_, ...), custom_call_target="tpu_custom_call" | custom-call | bytes 30000000 | tf_op jit(solution)/shard_map/pair_grads/pallas_call | solution.py:1379
  216.6 57.1 %gather_group.1 = (bf16[2048,1152]{1,0:T(8,128)(2,1)}, f32[128,1024]{1,0:T(8,128)}, f32[8,768]{1,0:T(8,128)}) custom-call(bf16[128,1152]{1,0:T(8,128)(2,1)} %get-tuple-element.75.x_ref, f32[8,768]{1,0:T(8,128)} %fusion.1.refs_0_, s32[1,3]{1,0:T(1,128)} %refs_1_.5, bf16[128,3072]{1,0:T(8,128)(2,1)} %copy-done.2, f32[128,1024]{1,0:T(8,128)} %get-tuple-element.76.refs_3_, ...), custom_call_target="tpu_custom_call" | custom-call | bytes 150000000 | tf_op jit(solution)/shard_map/gather_group/pallas_call | solution.py:661
  273.7 1.0 fusion.9
  274.9 25.7 %memory_backward.1.parts_ref = bf16[2048,1024]{1,0:T(8,128)(2,1)} custom-call(s32[2048]{0:T(1024)} %bitcast.26, bf16[2048,1024]{1,0:T(8,128)(2,1)} %all-gather.2.cloned.1.call-done.q_ref.refs_4_, bf16[2048,1152]{1,0:T(8,128)(2,1)} %get-tuple-element.77.g_ref.refs_5_, bf16[49152,128]{1,0:T(8,128)(2,1)} %get-tuple-element.59.k_ref, ...), custom_call_target="tpu_custom_call" | custom-call | bytes 75000000 | tf_op jit(solution)/shard_map/memory_backward/pallas_call | solution.py:456
  300.6 80.6 %reduce_group.3.refs_1_.refs_4_ = bf16[128,3072]{1,0:T(8,128)(2,1)} custom-call(bf16[2048,1024]{1,0:T(8,128)(2,1)} %memory_backward.1.parts_ref, f32[8,768]{1,0:T(8,128)} %fusion.refs_0_, s32[1,3]{1,0:T(1,128)} %refs_1_.5, bf16[128,3072]{1,0:T(8,128)(2,1)} %copy-done.2, f32[8]{0:T(128)} %get-tuple-element.98.refs_3_, ...), custom_call_target="tpu_custom_call" | custom-call | bytes 150000000 | tf_op jit(solution)/shard_map/reduce_group/pallas_call | solution.py:821
  381.3 0.6 fusion.16.refs_7_
  381.9 60.3 %finish_grads.1 = (bf16[2,64,1536]{2,1,0:T(8,128)(2,1)}, f32[24,128]{1,0:T(8,128)}, f32[128,1024]{1,0:T(8,128)}, f32[1,1024]{1,0:T(1,128)}) custom-call(bf16[128,1024]{1,0:T(8,128)(2,1)} %copy-done.3, bf16[128,3072]{1,0:T(8,128)(2,1)} %reduce_group.3.refs_1_.refs_4_, bf16[128,1024]{1,0:T(8,128)(2,1)} %refs_2_.3, f32[1,1024]{1,0:T(1,128)} %bitcast.27, ...), custom_call_target="tpu_custom_call" | custom-call | bytes 135000000 | tf_op jit(solution)/shard_map/finish_grads/pallas_call | solution.py:1595
  442.2 4.1 join_halves.1.early_ref
  446.4 3.4 write_results.1
  (63 shorter events, 2.5 us)
Async XLA Ops:
  7.2 32.9 %copy-start = (f32[8,32]{1,0:T(8,128)S(1)}, f32[8,32]{1,0:T(8,128)}, u32[]{:S(2)}) copy-start(f32[8,32]{1,0:T(8,128)} %param.20) | copy-start | bytes 3076
  7.2 92.7 %all-gather.2.cloned.1.call-start = ((), (), s32[]{:S(2)}) async-start(), calls=%async_computation.2 | async-start | bytes 4456448 | tf_op jit(solution)/shard_map/all_gather | solution.py:1683
  9.4 4.8 %copy-start.3 = (bf16[128,1024]{1,0:T(8,128)(2,1)}, bf16[128,1024]{1,0:T(8,128)(2,1)S(1)}, u32[]{:S(2)}) copy-start(bf16[128,1024]{1,0:T(8,128)(2,1)S(1)} %fusion.4.refs_0_) | copy-start | bytes 786436
  9.4 4.9 %copy-start.10 = (s32[128,8,32]{0,2,1:T(8,128)S(1)}, s32[128,8,32]{0,2,1:T(8,128)}, u32[]{:S(2)}) copy-start(s32[128,8,32]{0,2,1:T(8,128)} %param.29) | copy-start | bytes 393220
  9.4 4.9 %copy-start.11 = (s32[128,8,32,1]{0,3,2,1:T(1,128)S(1)}, s32[128,8,32,1]{0,3,2,1:T(1,128)}, u32[]{:S(2)}) copy-start(s32[128,8,32,1]{0,3,2,1:T(1,128)} %param.28) | copy-start | bytes 393220
  9.5 4.9 %copy-start.12 = (s32[128,8,32]{0,2,1:T(8,128)S(1)}, s32[128,8,32]{0,2,1:T(8,128)}, u32[]{:S(2)}) copy-start(s32[128,8,32]{0,2,1:T(8,128)} %param.30) | copy-start | bytes 393220
  13.4 78.2 %copy-start.2 = (bf16[128,3072]{1,0:T(8,128)(2,1)}, bf16[128,3072]{1,0:T(8,128)(2,1)S(1)}, u32[]{:S(2)}) copy-start(bf16[128,3072]{1,0:T(8,128)(2,1)S(1)} %convolution_convert_fusion.refs_2_) | copy-start | bytes 2359300
  22.1 1.1 copy-start.8
  22.6 0.6 copy-start.16
  26.1 16.1 %all-to-all-start = ((s32[16,24,128]{2,1,0:T(8,128)}), s32[16,24,128]{2,1,0:T(8,128)S(1)}, u32[]{:S(2)}, u32[]{:S(2)}) async-start(s32[16,24,128]{2,1,0:T(8,128)} %make_lists.1), calls=%async_computation | async-start | bytes 393216 | tf_op jit(solution)/shard_map/all_to_all | solution.py:1671
  32.8 409.4 %reduce-scatter.2.cloned.1.call-start = ((), (), s32[]{:S(2)}) async-start(), calls=%async_computation.3 | async-start | bytes 10027008 | tf_op jit(solution)/shard_map/reduce_scatter | solution.py:909
  32.9 91.2 %collective-permute-start.1 = (bf16[128,2048]{1,0:T(8,128)(2,1)S(1)}, bf16[128,2048]{1,0:T(8,128)(2,1)S(1)}, u32[]{:S(2)}, u32[]{:S(2)}) collective-permute-start(bf16[128,2048]{1,0:T(8,128)(2,1)S(1)} %slice.17), channel_id=1, source_target_pairs={{0,3},{1,4},{2,5},{3,6},{4,7},{5,8},{6,9},{7,10},{8,11},{9,12},{10... | collective-permute-start | bytes 1572872 | tf_op jit(solution)/shard_map/ppermute | solution.py:25
  36.9 87.2 %collective-permute-start = (bf16[128,2048]{1,0:T(8,128)(2,1)S(1)}, bf16[128,2048]{1,0:T(8,128)(2,1)S(1)}, u32[]{:S(2)}, u32[]{:S(2)}) collective-permute-start(bf16[128,2048]{1,0:T(8,128)(2,1)S(1)} %slice.17), channel_id=1, source_target_pairs={{0,4},{1,5},{2,6},{3,7},{4,8},{5,9},{6,10},{7,11},{8,12},{9,13},{1... | collective-permute-start | bytes 1572872 | tf_op jit(solution)/shard_map/ppermute | solution.py:25
  42.2 0.7 copy-start.9
  45.0 50.7 %copy-start.17 = (f32[8]{0:T(128)S(1)}, f32[8]{0:T(128)}, u32[]{:S(2)}) copy-start(f32[8]{0:T(128)} %param.21) | copy-start | bytes 100
  91.6 32.5 %collective-permute-start.3 = (bf16[128,2048]{1,0:T(8,128)(2,1)S(1)}, bf16[128,2048]{1,0:T(8,128)(2,1)S(1)}, u32[]{:S(2)}, u32[]{:S(2)}) collective-permute-start(bf16[128,2048]{1,0:T(8,128)(2,1)S(1)} %slice.17), channel_id=1, source_target_pairs={{0,1},{1,2},{2,3},{3,4},{4,5},{5,6},{6,7},{7,8},{8,9},{9,10},{10,1... | collective-permute-start | bytes 1572872 | tf_op jit(solution)/shard_map/ppermute | solution.py:25
  93.5 30.6 %collective-permute-start.2 = (bf16[128,2048]{1,0:T(8,128)(2,1)S(1)}, bf16[128,2048]{1,0:T(8,128)(2,1)S(1)}, u32[]{:S(2)}, u32[]{:S(2)}) collective-permute-start(bf16[128,2048]{1,0:T(8,128)(2,1)S(1)} %slice.17), channel_id=1, source_target_pairs={{0,2},{1,3},{2,4},{3,5},{4,6},{5,7},{6,8},{7,9},{8,10},{9,11},{10,... | collective-permute-start | bytes 1572872 | tf_op jit(solution)/shard_map/ppermute | solution.py:25
  124.0 0.8 copy-start.4
  124.0 1.0 copy-start.5
  124.1 1.1 copy-start.6
  125.2 0.8 copy-start.7
  216.5 58.3 %copy-start.13 = (f32[8,128]{1,0:T(8,128)S(1)}, f32[8,128]{1,0:T(8,128)}, u32[]{:S(2)}) copy-start(f32[8,128]{1,0:T(8,128)} %get-tuple-element.83) | copy-start | bytes 12292
  300.6 80.6 %copy-start.15 = (f32[8]{0:T(128)S(1)}, f32[8]{0:T(128)}, u32[]{:S(2)}) copy-start(f32[8]{0:T(128)} %get-tuple-element.99.share_ref.refs_6_) | copy-start | bytes 100
  300.6 80.6 %copy-start.14 = (f32[1,1024]{1,0:T(1,128)S(1)}, f32[1,1024]{1,0:T(1,128)}, u32[]{:S(2)}) copy-start(f32[1,1024]{1,0:T(1,128)} %get-tuple-element.81) | copy-start | bytes 12292
  381.9 67.9 %copy-start.1 = (f32[8,32]{1,0:T(8,128)S(1)}, f32[8,32]{1,0:T(8,128)}, u32[]{:S(2)}) copy-start(f32[8,32]{1,0:T(8,128)} %param.20) | copy-start | bytes 3076
Sparse Core Ops, SparseCore 0:
  14.4 85.4 all-gather.1
  216.7 219.3 reduce-scatter.1

commit v7 on v6

--- a/solution.py
+++ b/solution.py
@@ -595,6 +595,13 @@
             else:
                 pl.when(condition)(go)
 
+        def pass_all(distance):
+            if distance == 0:
+                pass_on(None, 0, 0)
+            else:
+                pass_on(layer + distance < depth, 4 * distance, up_slot(distance))
+                pass_on(layer - distance >= 0, -4 * distance, down_slot(distance))
+
         for distance in range(1, depth):
             from_above, from_below = layer + distance < depth, layer - distance >= 0
 
@@ -633,13 +640,10 @@
                     sent.append((condition, remote(here, here, send.at[2, slot, part], own_sem, to_x)))
                     sent.append((condition, remote(here, here, send.at[3, slot, part], own_sem, to_y)))
             meanwhile(distance - 1, depth - 1)
-            if distance == 1:
-                pass_on(None, 0, 0)
-            else:
-                pass_on(layer + distance - 1 < depth, 4 * (distance - 1), up_slot(distance - 1))
-                pass_on(layer - distance + 1 >= 0, -4 * (distance - 1), down_slot(distance - 1))
-        pass_on(layer + depth - 1 < depth, 4 * (depth - 1), up_slot(depth - 1))
-        pass_on(layer - depth + 1 >= 0, -4 * (depth - 1), down_slot(depth - 1))
+            if distance > 1:
+                pass_all(distance - 2)
+        for distance in (depth - 2, depth - 1):
+            pass_all(distance)
 
         def close(step, slot):
             arrived(to_x + step, 2, slot, 1)

time: 466 us -> 466 us (level)
    pallas_call x1, Pallas kernels: 60.3 us -> 78.5 us  [finish_grads(): pl.pallas_call(kernel, in_specs=[vmem] * (2 * count) + specs + [vmem], ou...]
    pallas_call x2, Pallas kernels: 144 us -> 128 us  [reduce_group(): pl.pallas_call(kernel, in_specs=[vmem, *specs], out_specs=[vmem] * (len(o...]
  transfers between devices with their start and end apart: 7 -> 7, of which waited for: 1 -> 2; matrix products, arithmetic and copies ran while one was open for 3% -> 3% of each run, Pallas kernels for 66% -> 66%
where the time goes in v7:
time: 466 us; the launch traced here: 458 us
  Pallas kernels  398 us (85%)
  starting transfers between devices  19.1 us (4%)
  between operations  14.9 us (3%)
  other arithmetic  12.1 us (3%)
  matrix products  7.13 us (2%)
    pallas_call x2, Pallas kernels, reduce_group(): pl.pallas_call(kernel, in_specs=[vmem, *specs], out_specs=[vmem] * (len(o...  128 us
    pallas_call x1, Pallas kernels, finish_grads(): pl.pallas_call(kernel, in_specs=[vmem] * (2 * count) + specs + [vmem], ou...  78.5 us
    pallas_call x1, Pallas kernels, gather_group(): pl.pallas_call(kernel, in_specs=[pl.BlockSpec(memory_space=pl.ANY), *spec...  54.5 us
    pallas_call x1, Pallas kernels, gather_rows(): pl.pallas_call(kernel, grid_spec=pltpu.PrefetchScalarGridSpec(num_scalar_...  47.7 us
    pallas_call x1, Pallas kernels, memory_backward(): pl.pallas_call(kernel, grid_spec=pltpu.PrefetchScalarGridSpec(num_scalar_...  25.7 us
    pallas_call x1, Pallas kernels, memory_forward(): pl.pallas_call(kernel, grid_spec=pltpu.PrefetchScalarGridSpec(num_scalar_...  24.1 us
    pallas_call x1, Pallas kernels, middle(): pl.pallas_call(kernel, grid=(steps,), in_specs=[full, full, full, whole(r...  16 us
    ppermute x4, starting transfers between devices, passed_along(): return lax.ppermute(value, axis, pairs)  12.4 us
  transfers between devices with their start and end apart: 7, of which 2 were waited for; matrix products, arithmetic and copies ran while one was open for 3% of the time, Pallas kernels for 66%

profile of v7, /device:TPU:9, one launch (start us, length us, event | category | flops | bytes accessed | tf_op | source)
XLA Modules:
  0.0 457.6 jit_solution(4416249956166482139)
XLA Ops:
  7.2 1.1 fusion.2
  8.3 1.1 fusion.4.refs_0_
  9.5 3.9 convolution_convert_fusion.refs_2_
  13.4 0.8 slice.16
  14.8 7.3 %sort.7 = s32[32768]{0:T(1024)S(1)} sort(s32[32768]{0:T(1024)S(1)} %reshape.297), dimensions={0}, to_apply=%region_0.1 | sort | flops 491520 | bytes 262144 | tf_op jit(solution)/shard_map/sort | solution.py:50
  22.7 0.6 pad_add_fusion.starts_ref
  23.2 2.9 make_lists.1
  26.1 6.7 %all-to-all-start = ((s32[16,24,128]{2,1,0:T(8,128)}), s32[16,24,128]{2,1,0:T(8,128)S(1)}, u32[]{:S(2)}, u32[]{:S(2)}) async-start(s32[16,24,128]{2,1,0:T(8,128)} %make_lists.1), calls=%async_computation | async-start | bytes 393216 | tf_op jit(solution)/shard_map/all_to_all | solution.py:1675
  32.9 4.0 collective-permute-start.1
  36.9 3.1 collective-permute-start
  40.0 1.1 fusion.refs_0_
  41.2 1.1 fusion.1.refs_0_
  42.3 0.7 copy-done.9
  42.9 2.0 read_lists.1
  45.0 47.7 %gather_rows.1 = (bf16[49152,128]{1,0:T(8,128)(2,1)}, bf16[49152,128]{1,0:T(8,128)(2,1)}) custom-call(s32[49152]{0:T(1024)} %bitcast.22, s32[2048]{0:T(1024)} %bitcast.24, bf16[4096,1024]{1,0:T(8,128)(2,1)} %keys.1, bf16[4096,1024]{1,0:T(8,128)(2,1)} %values.1), custom_call_target="tpu_custom_call" | custom-call | bytes 126000000 | tf_op jit(solution)/shard_map/gather_rows/pallas_call | solution.py:171
  92.7 1.9 collective-permute-start.3
  94.6 3.4 collective-permute-start.2
  98.6 1.3 all-gather.2.cloned.1.call-done.q_ref.refs_4_
  99.9 24.1 %memory_forward.1.parts_ref = bf16[2048,1152]{1,0:T(8,128)(2,1)} custom-call(s32[2048]{0:T(1024)} %bitcast.25, bf16[2048,1024]{1,0:T(8,128)(2,1)} %all-gather.2.cloned.1.call-done.q_ref.refs_4_, bf16[49152,128]{1,0:T(8,128)(2,1)} %get-tuple-element.59.k_ref, bf16[49152,128]{1,0:T(8,128)(2,1)} %get-tuple-element.60.v_ref, s32[16,25,128]{2,1,0:T(8,128)} %get-tuple-element.61.id_ref), custom_call_target="tpu_custom_call" | custom-call | bytes 75000000 | tf_op jit(solution)/shard_map/memory_forward/pallas_call | solution.py:307
  124.1 2.3 collective-permute-done.2.refs_5_.refs_9_
  126.4 0.8 copy-done.7
  127.2 62.4 %reduce_group.2 = (f32[128,1024]{1,0:T(8,128)}, f32[128,128]{1,0:T(8,128)}, f32[128,1024]{1,0:T(8,128)}, f32[128,128]{1,0:T(8,128)}) custom-call(bf16[2048,1152]{1,0:T(8,128)(2,1)} %memory_forward.1.parts_ref, f32[8,768]{1,0:T(8,128)} %fusion.1.refs_0_, s32[1,3]{1,0:T(1,128)} %refs_1_.5, bf16[128,3072]{1,0:T(8,128)(2,1)} %copy-done.2, ...), custom_call_target="tpu_custom_call" | custom-call | bytes 150000000 | tf_op jit(solution)/shard_map/reduce_group/pallas_call | solution.py:825
  189.6 16.0 %middle.1 = (bf16[128,1024]{1,0:T(8,128)(2,1)}, bf16[128,1024]{1,0:T(8,128)(2,1)}, bf16[128,4096]{1,0:T(8,128)(2,1)}, bf16[128,4096]{1,0:T(8,128)(2,1)}, bf16[12...) custom-call(bf16[128,1024]{1,0:T(8,128)(2,1)} %refs_2_.3, ...), custom_call_target="tpu_custom_call" | custom-call | bytes 54000000 | tf_op jit(solution)/shard_map/middle/pallas_call | solution.py:1264
  205.7 11.2 %pair_grads.1 = bf16[1024,4608]{1,0:T(8,128)(2,1)} custom-call(bf16[128,1024]{1,0:T(8,128)(2,1)} %get-tuple-element.70.refs_0_, bf16[128,1024]{1,0:T(8,128)(2,1)} %get-tuple-element.71.refs_1_, bf16[128,1024]{1,0:T(8,128)(2,1)} %refs_2_.2, bf16[128,1024]{1,0:T(8,128)(2,1)} %get-tuple-element.72.refs_3_, bf16[128,4096]{1,0:T(8,128)(2,1)} %get-tuple-element.73.refs_4_, ...), custom_call_target="tpu_custom_call" | custom-call | bytes 30000000 | tf_op jit(solution)/shard_map/pair_grads/pallas_call | solution.py:1383
  217.0 54.5 %gather_group.1 = (bf16[2048,1152]{1,0:T(8,128)(2,1)}, f32[128,1024]{1,0:T(8,128)}, f32[8,768]{1,0:T(8,128)}) custom-call(bf16[128,1152]{1,0:T(8,128)(2,1)} %get-tuple-element.75.x_ref, f32[8,768]{1,0:T(8,128)} %fusion.1.refs_0_, s32[1,3]{1,0:T(1,128)} %refs_1_.5, bf16[128,3072]{1,0:T(8,128)(2,1)} %copy-done.2, f32[128,1024]{1,0:T(8,128)} %get-tuple-element.76.refs_3_, ...), custom_call_target="tpu_custom_call" | custom-call | bytes 150000000 | tf_op jit(solution)/shard_map/gather_group/pallas_call | solution.py:665
  271.5 1.0 fusion.9
  272.7 25.7 %memory_backward.1.parts_ref = bf16[2048,1024]{1,0:T(8,128)(2,1)} custom-call(s32[2048]{0:T(1024)} %bitcast.26, bf16[2048,1024]{1,0:T(8,128)(2,1)} %all-gather.2.cloned.1.call-done.q_ref.refs_4_, bf16[2048,1152]{1,0:T(8,128)(2,1)} %get-tuple-element.77.g_ref.refs_5_, bf16[49152,128]{1,0:T(8,128)(2,1)} %get-tuple-element.59.k_ref, ...), custom_call_target="tpu_custom_call" | custom-call | bytes 75000000 | tf_op jit(solution)/shard_map/memory_backward/pallas_call | solution.py:456
  298.4 65.2 %reduce_group.3.refs_1_.refs_4_ = bf16[128,3072]{1,0:T(8,128)(2,1)} custom-call(bf16[2048,1024]{1,0:T(8,128)(2,1)} %memory_backward.1.parts_ref, f32[8,768]{1,0:T(8,128)} %fusion.refs_0_, s32[1,3]{1,0:T(1,128)} %refs_1_.5, bf16[128,3072]{1,0:T(8,128)(2,1)} %copy-done.2, f32[8]{0:T(128)} %get-tuple-element.98.refs_3_, ...), custom_call_target="tpu_custom_call" | custom-call | bytes 150000000 | tf_op jit(solution)/shard_map/reduce_group/pallas_call | solution.py:825
  363.6 0.6 fusion.16.refs_7_
  364.2 78.5 %finish_grads.1 = (bf16[2,64,1536]{2,1,0:T(8,128)(2,1)}, f32[24,128]{1,0:T(8,128)}, f32[128,1024]{1,0:T(8,128)}, f32[1,1024]{1,0:T(1,128)}) custom-call(bf16[128,1024]{1,0:T(8,128)(2,1)} %copy-done.3, bf16[128,3072]{1,0:T(8,128)(2,1)} %reduce_group.3.refs_1_.refs_4_, bf16[128,1024]{1,0:T(8,128)(2,1)} %refs_2_.3, f32[1,1024]{1,0:T(1,128)} %bitcast.27, ...), custom_call_target="tpu_custom_call" | custom-call | bytes 135000000 | tf_op jit(solution)/shard_map/finish_grads/pallas_call | solution.py:1599
  442.8 4.1 join_halves.1.early_ref
  446.9 3.4 write_results.1
  (63 shorter events, 2.1 us)
Async XLA Ops:
  7.2 32.9 %copy-start = (f32[8,32]{1,0:T(8,128)S(1)}, f32[8,32]{1,0:T(8,128)}, u32[]{:S(2)}) copy-start(f32[8,32]{1,0:T(8,128)} %param.20) | copy-start | bytes 3076
  7.2 92.7 %all-gather.2.cloned.1.call-start = ((), (), s32[]{:S(2)}) async-start(), calls=%async_computation.2 | async-start | bytes 4456448 | tf_op jit(solution)/shard_map/all_gather | solution.py:1687
  9.4 4.8 %copy-start.3 = (bf16[128,1024]{1,0:T(8,128)(2,1)}, bf16[128,1024]{1,0:T(8,128)(2,1)S(1)}, u32[]{:S(2)}) copy-start(bf16[128,1024]{1,0:T(8,128)(2,1)S(1)} %fusion.4.refs_0_) | copy-start | bytes 786436
  9.4 4.9 %copy-start.10 = (s32[128,8,32]{0,2,1:T(8,128)S(1)}, s32[128,8,32]{0,2,1:T(8,128)}, u32[]{:S(2)}) copy-start(s32[128,8,32]{0,2,1:T(8,128)} %param.29) | copy-start | bytes 393220
  9.4 4.9 %copy-start.11 = (s32[128,8,32,1]{0,3,2,1:T(1,128)S(1)}, s32[128,8,32,1]{0,3,2,1:T(1,128)}, u32[]{:S(2)}) copy-start(s32[128,8,32,1]{0,3,2,1:T(1,128)} %param.28) | copy-start | bytes 393220
  9.5 4.9 %copy-start.12 = (s32[128,8,32]{0,2,1:T(8,128)S(1)}, s32[128,8,32]{0,2,1:T(8,128)}, u32[]{:S(2)}) copy-start(s32[128,8,32]{0,2,1:T(8,128)} %param.30) | copy-start | bytes 393220
  13.4 79.3 %copy-start.2 = (bf16[128,3072]{1,0:T(8,128)(2,1)}, bf16[128,3072]{1,0:T(8,128)(2,1)S(1)}, u32[]{:S(2)}) copy-start(bf16[128,3072]{1,0:T(8,128)(2,1)S(1)} %convolution_convert_fusion.refs_2_) | copy-start | bytes 2359300
  22.1 1.1 copy-start.8
  22.6 0.6 copy-start.16
  26.1 16.1 %all-to-all-start = ((s32[16,24,128]{2,1,0:T(8,128)}), s32[16,24,128]{2,1,0:T(8,128)S(1)}, u32[]{:S(2)}, u32[]{:S(2)}) async-start(s32[16,24,128]{2,1,0:T(8,128)} %make_lists.1), calls=%async_computation | async-start | bytes 393216 | tf_op jit(solution)/shard_map/all_to_all | solution.py:1675
  32.8 410.0 %reduce-scatter.2.cloned.1.call-start = ((), (), s32[]{:S(2)}) async-start(), calls=%async_computation.3 | async-start | bytes 10027008 | tf_op jit(solution)/shard_map/reduce_scatter | solution.py:913
  32.9 91.1 %collective-permute-start.1 = (bf16[128,2048]{1,0:T(8,128)(2,1)S(1)}, bf16[128,2048]{1,0:T(8,128)(2,1)S(1)}, u32[]{:S(2)}, u32[]{:S(2)}) collective-permute-start(bf16[128,2048]{1,0:T(8,128)(2,1)S(1)} %slice.17), channel_id=1, source_target_pairs={{0,3},{1,4},{2,5},{3,6},{4,7},{5,8},{6,9},{7,10},{8,11},{9,12},{10... | collective-permute-start | bytes 1572872 | tf_op jit(solution)/shard_map/ppermute | solution.py:25
  36.9 87.1 %collective-permute-start = (bf16[128,2048]{1,0:T(8,128)(2,1)S(1)}, bf16[128,2048]{1,0:T(8,128)(2,1)S(1)}, u32[]{:S(2)}, u32[]{:S(2)}) collective-permute-start(bf16[128,2048]{1,0:T(8,128)(2,1)S(1)} %slice.17), channel_id=1, source_target_pairs={{0,4},{1,5},{2,6},{3,7},{4,8},{5,9},{6,10},{7,11},{8,12},{9,13},{1... | collective-permute-start | bytes 1572872 | tf_op jit(solution)/shard_map/ppermute | solution.py:25
  42.2 0.7 copy-start.9
  45.0 53.1 %copy-start.17 = (f32[8]{0:T(128)S(1)}, f32[8]{0:T(128)}, u32[]{:S(2)}) copy-start(f32[8]{0:T(128)} %param.21) | copy-start | bytes 100
  92.7 31.3 %collective-permute-start.3 = (bf16[128,2048]{1,0:T(8,128)(2,1)S(1)}, bf16[128,2048]{1,0:T(8,128)(2,1)S(1)}, u32[]{:S(2)}, u32[]{:S(2)}) collective-permute-start(bf16[128,2048]{1,0:T(8,128)(2,1)S(1)} %slice.17), channel_id=1, source_target_pairs={{0,1},{1,2},{2,3},{3,4},{4,5},{5,6},{6,7},{7,8},{8,9},{9,10},{10,1... | collective-permute-start | bytes 1572872 | tf_op jit(solution)/shard_map/ppermute | solution.py:25
  94.6 31.8 %collective-permute-start.2 = (bf16[128,2048]{1,0:T(8,128)(2,1)S(1)}, bf16[128,2048]{1,0:T(8,128)(2,1)S(1)}, u32[]{:S(2)}, u32[]{:S(2)}) collective-permute-start(bf16[128,2048]{1,0:T(8,128)(2,1)S(1)} %slice.17), channel_id=1, source_target_pairs={{0,2},{1,3},{2,4},{3,5},{4,6},{5,7},{6,8},{7,9},{8,10},{9,11},{10,... | collective-permute-start | bytes 1572872 | tf_op jit(solution)/shard_map/ppermute | solution.py:25
  124.0 2.4 copy-start.4
  124.0 2.4 copy-start.5
  124.0 2.4 copy-start.6
  126.4 0.8 copy-start.7
  216.9 55.6 %copy-start.13 = (f32[8,128]{1,0:T(8,128)S(1)}, f32[8,128]{1,0:T(8,128)}, u32[]{:S(2)}) copy-start(f32[8,128]{1,0:T(8,128)} %get-tuple-element.83) | copy-start | bytes 12292
  298.3 65.2 %copy-start.15 = (f32[8]{0:T(128)S(1)}, f32[8]{0:T(128)}, u32[]{:S(2)}) copy-start(f32[8]{0:T(128)} %get-tuple-element.99.share_ref.refs_6_) | copy-start | bytes 100
  298.4 65.2 %copy-start.14 = (f32[1,1024]{1,0:T(1,128)S(1)}, f32[1,1024]{1,0:T(1,128)}, u32[]{:S(2)}) copy-start(f32[1,1024]{1,0:T(1,128)} %get-tuple-element.81) | copy-start | bytes 12292
  364.2 86.1 %copy-start.1 = (f32[8,32]{1,0:T(8,128)S(1)}, f32[8,32]{1,0:T(8,128)}, u32[]{:S(2)}) copy-start(f32[8,32]{1,0:T(8,128)} %param.20) | copy-start | bytes 3076
Sparse Core Ops, SparseCore 0:
  14.4 85.4 all-gather.1
  217.1 210.9 reduce-scatter.1
